TPU v7x, 32 devices: a whole 2x2x4 slice. The times are simulated.
32 devices in a mesh: group: 2 (over y), ctx: 4 (over z), req: 4 (over x, core).
Axes of the slice: x: 2, y: 2, z: 4, core: 2. Of those that a mesh axis runs over, the one named last changes fastest.
Arguments:
- hidden_states: bfloat16 [8, 512, 3584], P(('group', 'req'), 'ctx'), parts along dimension 0, may hold values from -6 to 6
- queries_base: bfloat16 [8, 512, 2688], P(('group', 'req'), 'ctx'), parts along dimension 0, may hold values from -6 to 6
- kv_base: bfloat16 [8, 512, 768], P(('group', 'req'), 'ctx'), parts along dimension 0, may hold values from -6 to 6
- adapter_down: bfloat16 [128, 3584, 128], P(('group', 'req'), 'ctx'), parts along dimension 0, may hold values from -0.09375 to 0.09375
- adapter_up: bfloat16 [128, 128, 2688], P(('group', 'req'), 'ctx'), parts along dimension 0, may hold values from -0.75 to 0.75
- adapter_ids: int32 [8], P('group'), parts along dimension 0, may hold values from 0 to 63
- adapter_slots: int32 [128], P('group'), parts along dimension 0, may hold values from 0 to 63, each once
- rank_buckets: int32 [128], P('group'), parts along dimension 0, may hold values from 16 to 128, as said below
- lengths: int32 [8], P(('group', 'req')), parts along dimension 0, may hold values from 128 to 512, as said below
Outputs:
- attended: bfloat16 [8, 512, 2688], P(('group', 'req'), 'ctx'), parts along dimension 0
There are 2 independent parts, one for each index of `group`. A program takes and returns all parts, laid end to end along the dimension named above; each array names one. Nothing has to cross between parts.
Inputs may be any that keep to these rules, and one draw needn't show every extreme that they name: `adapter_slots`: each slot once; slot k lies on store shard k // 16. `rank_buckets`: each is 16, 64 or 128. `lengths`: multiples of 128.
All inputs are finite; a program needn't handle non-finite values.
Results may differ from a plain program's by a relative error of at most 0.0076.
Values may be sent and summed in bfloat16 or wider, within the bound.
No kernel may reach another device: no remote copies, remote signals or barrier semaphores. Data moves between devices by JAX's collectives and lax.ppermute only.
A program may use at most 128 MiB of HBM per device.

v0:
```python
import math

import jax
import jax.numpy as jnp
from jax import lax
from jax.sharding import PartitionSpec as P

HD = 128
KVH = 3
GROUP = 7


def body(
    hidden_states,
    queries_base,
    kv_base,
    adapter_down,
    adapter_up,
    adapter_ids,
    adapter_slots,
    rank_buckets,
    lengths,
):
    req_index = lax.axis_index("req")
    ctx_index = lax.axis_index("ctx")
    per_shard = adapter_down.shape[0]
    requests = adapter_ids.shape[0]
    store = adapter_slots.shape[0]
    rank_width = adapter_down.shape[2]
    tokens = hidden_states.shape[1]
    query_width = queries_base.shape[2]
    store_range = jnp.arange(store, dtype=jnp.int32)
    chosen = adapter_ids[:, None] == store_range[None, :]
    slot_of = jnp.sum(jnp.where(chosen, adapter_slots[None, :], 0), axis=1)
    rank_of = jnp.sum(jnp.where(chosen, rank_buckets[None, :], 0), axis=1)
    mine = jnp.arange(requests, dtype=jnp.int32) == req_index
    my_slot = jnp.sum(jnp.where(mine, slot_of, 0))
    my_rank = jnp.sum(jnp.where(mine, rank_of, 0))
    held = (
        slot_of[:, None] == req_index * per_shard + jnp.arange(per_shard, dtype=jnp.int32)[None, :]
    )
    select = held.astype(jnp.bfloat16)
    send_down = jnp.einsum(
        "qa,ard->qrd", select, adapter_down, preferred_element_type=jnp.float32
    ).astype(jnp.bfloat16)
    send_up = jnp.einsum(
        "qa,ard->qrd", select, adapter_up, preferred_element_type=jnp.float32
    ).astype(jnp.bfloat16)
    got_down, got_up = (
        lax.all_to_all(send_down, "req", split_axis=0, concat_axis=0, tiled=True),
        lax.all_to_all(send_up, "req", split_axis=0, concat_axis=0, tiled=True),
    )
    owner = my_slot // per_shard
    down_mine = lax.dynamic_index_in_dim(got_down, owner, 0, keepdims=False)
    up_mine = lax.dynamic_index_in_dim(got_up, owner, 0, keepdims=False)
    features = hidden_states[0]
    columns = features
    low_rank = jnp.dot(
        columns,
        lax.all_gather(down_mine, "ctx", axis=0, tiled=True),
        preferred_element_type=jnp.float32,
    )
    low_rank = jnp.where(
        jnp.arange(rank_width, dtype=jnp.int32)[None, :] < my_rank, low_rank, 0.0
    ).astype(jnp.bfloat16)
    columns = low_rank
    delta = jnp.dot(
        columns,
        lax.all_gather(up_mine, "ctx", axis=0, tiled=True),
        preferred_element_type=jnp.float32,
    )
    queries = (
        (queries_base[0].astype(jnp.float32) + delta)
        .astype(jnp.bfloat16)
        .reshape(tokens, KVH, GROUP, HD)
    )
    length = lengths[0]
    first_query = ctx_index * tokens
    query_pos = first_query + jnp.arange(tokens, dtype=jnp.int32)
    last_needed = jnp.minimum(first_query + tokens - 1, length - 1)
    scale = 1.0 / math.sqrt(HD)
    key_width = KVH * HD
    initial = (
        jnp.full((KVH, GROUP, tokens), -1e30, jnp.float32),
        jnp.zeros((KVH, GROUP, tokens), jnp.float32),
        jnp.zeros((KVH, GROUP, tokens, HD), jnp.float32),
    )
    piece = lax.all_gather(kv_base[0], "ctx", axis=0, tiled=True)
    count = piece.shape[0]
    width = math.gcd(count, 512)

    def key_block(index, state):
        largest, total, accum = state
        offset = index * width
        rows = lax.dynamic_slice_in_dim(piece, offset, width, 0)
        keys = rows[:, :key_width].reshape(width, KVH, HD)
        values = rows[:, key_width:].reshape(width, KVH, HD)
        key_pos = offset + jnp.arange(width, dtype=jnp.int32)
        score = (
            jnp.einsum("tkgd,skd->kgts", queries, keys, preferred_element_type=jnp.float32) * scale
        )
        allowed = (key_pos[None, :] <= query_pos[:, None]) & (key_pos[None, :] < length)
        masked = jnp.where(allowed, score, -1e30)
        newest = jnp.maximum(largest, jnp.max(masked, axis=-1))
        weight = jnp.where(allowed, jnp.exp(score - newest[..., None]), 0.0)
        factor = jnp.exp(largest - newest)
        total = total * factor + jnp.sum(weight, axis=-1)
        product = jnp.einsum(
            "kgts,skd->kgtd",
            weight.astype(jnp.bfloat16),
            values,
            preferred_element_type=jnp.float32,
        )
        accum = accum * factor[..., None] + product
        return (newest, total, accum)

    def compute(state):
        return lax.fori_loop(0, count // width, key_block, state)

    needed = (jnp.int32(0) <= last_needed) & (first_query < length)
    largest, total, accum = lax.cond(needed, compute, lambda state: state, initial)
    safe_total = jnp.where(total > 0.0, total, 1.0)
    output = accum / safe_total[..., None]
    output = jnp.transpose(output, (2, 0, 1, 3)).reshape(tokens, query_width)
    output = jnp.where(query_pos[:, None] < length, output, 0.0).astype(jnp.bfloat16)
    return output[None]


def solution(mesh):
    return jax.shard_map(
        body,
        mesh=mesh,
        in_specs=(
            P(("group", "req"), "ctx", None),
            P(("group", "req"), "ctx", None),
            P(("group", "req"), "ctx", None),
            P(("group", "req"), "ctx", None),
            P(("group", "req"), "ctx", None),
            P("group"),
            P("group"),
            P("group"),
            P(("group", "req")),
        ),
        out_specs=P(("group", "req"), "ctx", None),
        check_vma=False,
    )
```

profile of v0, /device:TPU:0, one launch (start us, length us, event | category | flops | bytes accessed | tf_op | source)
XLA Modules:
  0.0 103.9 jit_solution(7067902174623844848)
XLA Ops:
  0.0 0.0 copy-start
  0.0 0.0 copy-start.1
  0.0 1.0 %select_reduce_fusion.1 = (s32[4]{0:T(128)S(1)}, s32[4]{0:T(128)S(1)}) fusion(s32[64]{0:T(128)} %param.18, s32[4]{0:T(128)} %param.16, s32[64]{0:T(128)} %param.17), kind=kLoop, calls=%fused_computation.40 | loop fusion | flops 1272 | bytes 560 | tf_op jit(solution)/shard_map/reduce_sum | solution.py:35
  1.1 0.8 copy-done
  1.8 1.1 %convolution_convert_fusion = bf16[4,32,2688]{2,0,1:T(4,128)(2,1)S(1)} fusion(bf16[16,32,2688]{2,1,0:T(8,128)(2,1)S(1)} %copy-done, s32[16]{0:T(128)S(1)} %iota_add_fusion, s32[4]{0:T(128)S(1)} %get-tuple-element.71), kind=kOutput, calls=%fused_computation.25 | convolution fusion | flops 11354176 | bytes 3440720 | tf_op jit(solution)/shard_map/qa,ard->qrd/dot_general | solution.py:46
  3.0 0.9 copy.45
  3.9 4.2 %all-to-all-start.1 = ((bf16[4,32,2688]{2,1,0:T(8,128)(2,1)}), bf16[4,32,2688]{2,1,0:T(8,128)(2,1)}, u32[]{:S(2)}, u32[]{:S(2)}) async-start(bf16[4,32,2688]{2,1,0:T(8,128)(2,1)} %copy.45), calls=%async_computation.1 | async-start | bytes 1376256 | tf_op jit(solution)/shard_map/all_to_all | solution.py:51
  8.1 0.7 fusion.42
  12.2 0.0 copy-done.1
  12.2 0.8 copy.41
  13.1 4.3 %fusion.22 = bf16[4,896,128]{2,0,1:T(4,128)(2,1)S(1)} fusion(bf16[16,896,128]{2,1,0:T(8,128)(2,1)} %param.14, s32[16]{0:T(128)S(1)} %iota_add_fusion, s32[4]{0:T(128)S(1)} %get-tuple-element.71), kind=kOutput, calls=%fused_computation.28 | convolution fusion | flops 15138880 | bytes 4587600 | tf_op jit(solution)/shard_map/qa,ard->qrd/dot_general | solution.py:43
  17.4 1.0 %copy.43 = bf16[4,896,128]{2,1,0:T(8,128)(2,1)} copy(bf16[4,896,128]{2,0,1:T(4,128)(2,1)S(1)} %fusion.22) | data formatting | bytes 1835008 | tf_op jit(solution)/shard_map/convert_element_type | solution.py:45
  18.4 0.7 fusion.41
  19.1 20.4 %all-gather = bf16[1,512,768]{1,2,0:T(8,128)(2,1)S(1)} all-gather(bf16[1,128,768]{1,2,0:T(8,128)(2,1)} %copy.41), channel_id=2, replica_groups=mesh['group'=2,'ctx'=4,'req'=4] {'ctx'}, dimensions={1}, use_global_device_ids=true | all-gather | bytes 983040 | tf_op jit(solution)/shard_map/all_gather | solution.py:88
  39.5 0.0 all-to-all-done.1
  39.5 4.2 %all-to-all-start = ((bf16[4,896,128]{2,1,0:T(8,128)(2,1)}), bf16[4,896,128]{2,1,0:T(8,128)(2,1)}, u32[]{:S(2)}, u32[]{:S(2)}) async-start(bf16[4,896,128]{2,1,0:T(8,128)(2,1)} %copy.43), calls=%async_computation | async-start | bytes 1835008 | tf_op jit(solution)/shard_map/all_to_all | solution.py:50
  43.7 0.6 iota_compare_fusion.3
  44.4 0.9 constant_dynamic-slice_fusion.1
  45.3 17.8 %all-gather.2 = bf16[1,128,2688]{2,1,0:T(8,128)(2,1)} all-gather(bf16[1,32,2688]{2,1,0:T(8,128)(2,1)S(1)} %constant_dynamic-slice_fusion.1), channel_id=4, replica_groups=mesh['group'=2,'ctx'=4,'req'=4] {'ctx'}, dimensions={1}, use_global_device_ids=true | all-gather | bytes 860160 | tf_op jit(solution)/shard_map/all_gather | solution.py:69
  63.1 0.0 all-to-all-done
  63.1 1.0 constant_dynamic-slice_fusion
  64.1 19.8 %all-gather.1 = bf16[1,3584,128]{2,1,0:T(8,128)(2,1)} all-gather(bf16[1,896,128]{2,1,0:T(8,128)(2,1)S(1)} %constant_dynamic-slice_fusion), channel_id=3, replica_groups=mesh['group'=2,'ctx'=4,'req'=4] {'ctx'}, dimensions={1}, use_global_device_ids=true | all-gather | bytes 1146880 | tf_op jit(solution)/shard_map/all_gather | solution.py:60
  83.9 3.8 %fusion.20 = bf16[128,2688]{1,0:T(8,128)(2,1)} fusion(bf16[1,128,3584]{2,1,0:T(8,128)(2,1)} %param.11, bf16[1,3584,128]{2,1,0:T(8,128)(2,1)} %all-gather.1, bf16[1,128,2688]{2,1,0:T(8,128)(2,1)} %param.12, bf16[1,128,2688]{2,1,0:T(8,128)(2,1)} %all-gather.2, pred[128]{0:T(512)(128)(4,1)S(1)} %iota_compare_fusion.3), kind=kOutput, calls=%fused_computation.26 | convolution fusion | flops 206585856 | bytes 3899520 | tf_op jit(solution)/shard_map/dot_general | solution.py:67
  87.7 0.6 iota.33
  88.3 12.8 %conditional.1 = (f32[3,7,128]{2,1,0:T(8,128)S(1)}, f32[3,7,128,128]{2,3,1,0:T(8,128)}) conditional(s32[]{:T(128)} %convert_element_type.37, () %tuple.15, (s32[]{:T(128)}, s32[128]{0:T(128)}, s32[]{:T(128)}, bf16[512,768]{0,1:T(8,128)(2,1)S(1)}, bf16[128,2688]{1,0:T(8,128)(2,1)}) %tuple.28), branch_computations={%region_4.5_spmd, %region_5.8_spmd} | conditional | flops 720265728 | bytes 25450520 | solution.py:121
  88.3 2.2 %copy.46 = bf16[128,2688]{0,1:T(8,128)(2,1)} copy(bf16[128,2688]{1,0:T(8,128)(2,1)} %get-tuple-element.68) | data formatting | bytes 1376256 | tf_op jit(solution)/shard_map
  90.6 0.7 broadcast_add_fusion
  91.2 0.6 iota_compare_fusion.1
  91.9 0.1 fusion.14
  92.0 0.1 fusion.44
  92.1 2.1 %fusion = (f32[3,7,128]{2,1,0:T(8,128)S(1)}, f32[3,512,128,7]{2,1,3,0:T(8,128)S(1)}) fusion(pred[128,512]{0,1:T(8,128)(4,1)S(1)} %fusion.14, bf16[512,3,128,1]{0,2,3,1:T(8,128)(2,1)S(1)} %bitcast.60, bf16[128,3,7,128]{0,3,2,1:T(8,128)(2,1)} %bitcast.59), kind=kOutput, calls=%fused_computation.2 | convolution fusion | flops 356447616 | bytes 6662656 | tf_op jit(solution)/shard_map/cond/branch_1_fun/while/body/eval_jaxpr/tkgd,skd->kgts/dot_general | solution.py:100
  94.2 1.1 %fusion.4 = f32[3,7,128]{2,1,0:T(8,128)S(1)} fusion(f32[3,512,128,7]{2,1,3,0:T(8,128)S(1)} %get-tuple-element.77, f32[3,7,128]{2,1,0:T(8,128)S(1)} %broadcast_maximum_fusion, pred[128,512]{0,1:T(8,128)(4,1)S(1)} %fusion.14), kind=kLoop, calls=%fused_computation.6 | loop fusion | flops 5502336 | bytes 5592064 | tf_op jit(solution)/shard_map/cond/branch_1_fun/while/body/eval_jaxpr/reduce_sum | solution.py:107
  95.4 2.8 %fusion.11 = f32[3,7,128,128]{3,2,1,0:T(8,128)} fusion(bf16[512,3,128,1]{0,2,3,1:T(8,128)(2,1)S(1)} %bitcast.61, f32[3,512,128,7]{2,1,3,0:T(8,128)S(1)} %get-tuple-element.77, f32[3,7,128]{2,1,0:T(8,128)S(1)} %broadcast_maximum_fusion, pred[128,512]{0,1:T(8,128)(4,1)S(1)} %fusion.14, f32[3,7,128]{2,1,0:T(8,128)S(1)} %get-tuple-element.74), kind=kOutput, calls=%fused_computation.12 | convolution fusion | flops 358170624 | bytes 7361536 | tf_op jit(solution)/shard_map/cond/branch_1_fun/while/body/eval_jaxpr/kgts,skd->kgtd/dot_general | solution.py:108
  98.2 2.9 %copy.58 = f32[3,7,128,128]{2,3,1,0:T(8,128)} copy(f32[3,7,128,128]{3,2,1,0:T(8,128)} %fusion.11) | data formatting | bytes 2752512 | tf_op jit(solution)/shard_map/cond | solution.py:121
  101.1 1.5 %broadcast_divide_fusion = bf16[3,7,128,128]{2,3,1,0:T(8,128)(2,1)S(1)} fusion(f32[3,7,128,128]{2,3,1,0:T(8,128)} %get-tuple-element.69, f32[3,7,128]{2,1,0:T(8,128)S(1)} %compare_select_fusion), kind=kLoop, calls=%fused_computation.35 | loop fusion | flops 688128 | bytes 2075136 | tf_op jit(solution)/shard_map/div | solution.py:123
  102.6 0.1 select_convert_fusion
  102.8 1.1 %copy.48 = bf16[1,128,2688]{2,1,0:T(8,128)(2,1)} copy(bf16[1,128,2688]{1,2,0:T(8,128)(2,1)S(1)} %select_convert_fusion) | data formatting | bytes 1376256 | tf_op jit(solution)/shard_map/convert_element_type | solution.py:125
  (5 shorter events, 0.0 us)
Async XLA Ops:
  0.0 1.8 %copy-start = (bf16[16,32,2688]{2,1,0:T(8,128)(2,1)S(1)}, bf16[16,32,2688]{2,1,0:T(8,128)(2,1)}, u32[]{:S(2)}) copy-start(bf16[16,32,2688]{2,1,0:T(8,128)(2,1)} %param.15) | copy-start | bytes 8257540
  0.0 12.2 %copy-start.1 = (bf16[1,128,768]{2,1,0:T(8,128)(2,1)S(1)}, bf16[1,128,768]{2,1,0:T(8,128)(2,1)}, u32[]{:S(2)}) copy-start(bf16[1,128,768]{2,1,0:T(8,128)(2,1)} %param.13) | copy-start | bytes 589828
  3.9 35.6 %all-to-all-start.1 = ((bf16[4,32,2688]{2,1,0:T(8,128)(2,1)}), bf16[4,32,2688]{2,1,0:T(8,128)(2,1)}, u32[]{:S(2)}, u32[]{:S(2)}) async-start(bf16[4,32,2688]{2,1,0:T(8,128)(2,1)} %copy.45), calls=%async_computation.1 | async-start | bytes 1376256 | tf_op jit(solution)/shard_map/all_to_all | solution.py:51
  39.5 23.7 %all-to-all-start = ((bf16[4,896,128]{2,1,0:T(8,128)(2,1)}), bf16[4,896,128]{2,1,0:T(8,128)(2,1)}, u32[]{:S(2)}, u32[]{:S(2)}) async-start(bf16[4,896,128]{2,1,0:T(8,128)(2,1)} %copy.43), calls=%async_computation | async-start | bytes 1835008 | tf_op jit(solution)/shard_map/all_to_all | solution.py:50
where the time goes:
time: 105 us; the launch traced here: 104 us
  blocking collectives  58.1 us (55%)
  matrix products  14.2 us (14%)
  local copies, waits for them, and re-layouts  12.3 us (12%)
  starting transfers between devices  8.43 us (8%)
  other arithmetic  7.3 us (7%)
  between operations  3.51 us (3%)
    all_gather x1, blocking collectives, body(): piece = lax.all_gather(kv_base[0], 'ctx', axis=0, tiled=True)  20.4 us
    all_gather x1, blocking collectives, body(): lax.all_gather(down_mine, 'ctx', axis=0, tiled=True)  19.8 us
    all_gather x1, blocking collectives, body(): lax.all_gather(up_mine, 'ctx', axis=0, tiled=True)  17.8 us
    dot_general x1, matrix products, body(): jnp.einsum('qa,ard->qrd', select, adapter_down, preferred_element_type=jn...  4.29 us
    all_to_all x1, starting transfers between devices, body(): lax.all_to_all(send_down, 'req', split_axis=0, concat_axis=0, tiled=True)  4.22 us
    all_to_all x1, starting transfers between devices, body(): lax.all_to_all(send_up, 'req', split_axis=0, concat_axis=0, tiled=True)  4.21 us
    dot_general x1, matrix products, body(): jnp.dot(columns, lax.all_gather(up_mine, 'ctx', axis=0, tiled=True), pref...  3.82 us
    cond x1, local copies, waits for them, and re-layouts, body(): lax.cond(needed, compute, lambda state: state, initial)  2.88 us
  transfers between devices with their start and end apart: 2, of which 0 were waited for; matrix products, arithmetic and copies ran while one was open for 9% of the time, Pallas kernels for 0%

commit v1 on v0

--- a/solution.py
+++ b/solution.py
@@ -1,16 +1,211 @@
+import functools
 import math
 
 import jax
 import jax.numpy as jnp
 from jax import lax
+from jax.experimental import pallas as pl
+from jax.experimental.pallas import tpu as pltpu
 from jax.sharding import PartitionSpec as P
 
 HD = 128
 KVH = 3
 GROUP = 7
+HEADS = KVH * GROUP
+SMEM = pltpu.SMEM
+VMEM = pltpu.VMEM
+ANY = pl.ANY
+LOG2E = 1.0 / math.log(2.0)
+PARAMS = pltpu.CompilerParams(vmem_limit_bytes=48 * 1024 * 1024)
+
+
+def spec(space):
+    return pl.BlockSpec(memory_space=space)
+
+
+def select_kernel(ids, slots, store, keep, give, sems):
+    per_shard = store.shape[0]
+    me = lax.axis_index("req")
+    first = me * per_shard
+    targets = [(keep, 0, 0), (keep, 1, 2), (give, 0, 1), (give, 1, 3)]
+    for i, (out, k, flip) in enumerate(targets):
+        local = slots[ids[me ^ flip]] - first
+        held = (local >= 0) & (local < per_shard)
+
+        @pl.when(held)
+        def _():
+            pltpu.make_async_copy(store.at[local], out.at[k], sems.at[i]).start()
+
+        @pl.when(jnp.logical_not(held))
+        def _():
+            out[k] = jnp.zeros(out.shape[1:], out.dtype)
+
+    for i, (out, k, flip) in enumerate(targets):
+        local = slots[ids[me ^ flip]] - first
+        held = (local >= 0) & (local < per_shard)
+
+        @pl.when(held)
+        def _():
+            pltpu.make_async_copy(store.at[local], out.at[k], sems.at[i]).wait()
+
+
+def select(ids, slots, store):
+    shape = jax.ShapeDtypeStruct((2, *store.shape[1:]), store.dtype)
+    return pl.pallas_call(
+        select_kernel,
+        out_shape=(shape, shape),
+        in_specs=[spec(SMEM), spec(SMEM), spec(ANY)],
+        out_specs=(spec(VMEM), spec(VMEM)),
+        scratch_shapes=[pltpu.SemaphoreType.DMA((4,))],
+        compiler_params=PARAMS,
+    )(ids, slots, store)
+
+
+def fetch(ids, slots, store):
+    keep, give = select(ids, slots, store)
+    near = lax.ppermute(give, "req", [(i, i ^ 1) for i in range(4)])
+    far = lax.ppermute(keep[1] + near[1], "req", [(i, i ^ 2) for i in range(4)])
+    return keep[0] + near[0] + far
+
+
+def chain(array, step, count):
+    pairs = [(i, i + step) for i in range(count) if 0 <= i + step < count]
+    found = []
+    for _ in range(count - 1):
+        array = lax.ppermute(array, "ctx", pairs)
+        found.append(array)
+    return found
+
+
+def order(count):
+    return [0] + [-s for s in range(1, count)] + [s for s in range(1, count)]
+
+
+def low_rank_kernel(ids, ranks, hidden, *rest, count):
+    pieces, out, accum = rest[:-2], rest[-2], rest[-1]
+    rows = pieces[0].shape[0]
+    z = lax.axis_index("ctx")
+    rank = ranks[ids[lax.axis_index("req")]]
+    accum[...] = jnp.zeros_like(accum)
+    for offset, piece in zip(order(count), pieces):
+        place = z + offset
+
+        @pl.when((place >= 0) & (place < count))
+        def _():
+            columns = pl.ds(pl.multiple_of(place * rows, HD), rows)
+            accum[...] += jnp.dot(
+                hidden[:, columns], piece[...], preferred_element_type=jnp.float32
+            )
+
+    column = lax.broadcasted_iota(jnp.int32, accum.shape, 1)
+    out[...] = jnp.where(column < rank, accum[...], 0.0).astype(jnp.bfloat16)
+
+
+def low_rank(ids, ranks, hidden, pieces, count):
+    shape = (hidden.shape[0], pieces[0].shape[1])
+    return pl.pallas_call(
+        functools.partial(low_rank_kernel, count=count),
+        out_shape=jax.ShapeDtypeStruct(shape, jnp.bfloat16),
+        in_specs=[spec(SMEM)] * 2 + [spec(VMEM)] * (1 + len(pieces)),
+        out_specs=spec(VMEM),
+        scratch_shapes=[VMEM(shape, jnp.float32)],
+        compiler_params=PARAMS,
+        cost_estimate=pl.CostEstimate(flops=1 << 27, bytes_accessed=1 << 22, transcendentals=0),
+    )(ids, ranks, hidden, *pieces)
+
+
+def attend_kernel(lengths, base, low, *rest, count):
+    kvs, ups = rest[:count], rest[count:-2]
+    out, upper = rest[-2:]
+    tokens = base.shape[0]
+    rows = ups[0].shape[0]
+    z = lax.axis_index("ctx")
+    for offset, piece in zip(order(count), ups):
+        place = z + offset
+
+        @pl.when((place >= 0) & (place < count))
+        def _():
+            upper[pl.ds(pl.multiple_of(place * rows, rows), rows), :] = piece[...]
+
+    live = z * tokens < lengths[0]
+    factor = LOG2E / math.sqrt(HD)
+    query_pos = lax.broadcasted_iota(jnp.int32, (tokens, tokens), 0)
+    key_pos = lax.broadcasted_iota(jnp.int32, (tokens, tokens), 1)
+    causal = key_pos <= query_pos
+
+    @pl.when(jnp.logical_not(live))
+    def _():
+        out[...] = jnp.zeros_like(out)
+
+    for behind in range(count):
+
+        @pl.when(live & (z == behind))
+        def _():
+            for h in range(KVH):
+                keys = [kv[:, h * HD : (h + 1) * HD] for kv in kvs[: behind + 1]]
+                values = [
+                    kv[:, (KVH + h) * HD : (KVH + h + 1) * HD] for kv in kvs[: behind + 1]
+                ]
+                keys = jnp.concatenate(keys, axis=0)
+                values = jnp.concatenate(values, axis=0)
+                for g in range(GROUP):
+                    columns = slice((h * GROUP + g) * HD, (h * GROUP + g + 1) * HD)
+                    delta = jnp.dot(low[...], upper[:, columns], preferred_element_type=jnp.float32)
+                    query = (base[:, columns].astype(jnp.float32) + delta).astype(jnp.bfloat16)
+                    score = lax.dot_general(
+                        query, keys, (((1,), (1,)), ((), ())), preferred_element_type=jnp.float32
+                    )
+                    own = jnp.where(causal, score[:, :tokens], -1e30)
+                    if behind:
+                        own = jnp.concatenate([own, score[:, tokens:]], axis=1)
+                    score = own
+                    largest = jnp.max(score, axis=1, keepdims=True)
+                    weight = jnp.exp2((score - largest) * factor)
+                    total = jnp.sum(weight, axis=1, keepdims=True)
+                    product = jnp.dot(
+                        weight.astype(jnp.bfloat16), values, preferred_element_type=jnp.float32
+                    )
+                    out[:, columns] = (product / total).astype(jnp.bfloat16)
+
+
+def attend(lengths, base, low, kvs, ups, count):
+    return pl.pallas_call(
+        functools.partial(attend_kernel, count=count),
+        out_shape=jax.ShapeDtypeStruct(base.shape, jnp.bfloat16),
+        in_specs=[spec(SMEM)] + [spec(VMEM)] * (2 + len(kvs) + len(ups)),
+        out_specs=spec(VMEM),
+        scratch_shapes=[VMEM((low.shape[1], base.shape[1]), jnp.bfloat16)],
+        compiler_params=PARAMS,
+        cost_estimate=pl.CostEstimate(
+            flops=1 << 30, bytes_accessed=1 << 22, transcendentals=1 << 21
+        ),
+    )(lengths, base, low, *kvs, *ups)
 
 
 def body(
+    hidden_states,
+    queries_base,
+    kv_base,
+    adapter_down,
+    adapter_up,
+    adapter_ids,
+    adapter_slots,
+    rank_buckets,
+    lengths,
+    *,
+    count,
+):
+    kv = kv_base[0]
+    kvs = [kv] + chain(kv, 1, count)
+    down = fetch(adapter_ids, adapter_slots, adapter_down)
+    downs = [down] + chain(down, 1, count) + chain(down, -1, count)
+    up = fetch(adapter_ids, adapter_slots, adapter_up)
+    ups = [up] + chain(up, 1, count) + chain(up, -1, count)
+    low = low_rank(adapter_ids, rank_buckets, hidden_states[0], downs, count)
+    return attend(lengths, queries_base[0], low, kvs, ups, count)[None]
+
+
+def plain_body(
     hidden_states,
     queries_base,
     kv_base,
@@ -127,8 +322,13 @@
 
 
 def solution(mesh):
+    count = mesh.shape["ctx"]
+    if count == 4 and mesh.shape["req"] == 4:
+        local = functools.partial(body, count=count)
+    else:
+        local = plain_body
     return jax.shard_map(
-        body,
+        local,
         mesh=mesh,
         in_specs=(
             P(("group", "req"), "ctx", None),

time: 105 us -> 74.5 us (0.71)
  blocking collectives: 58.1 us -> 0 us
  starting transfers between devices: 8.43 us -> 47.1 us
  matrix products: 14.2 us -> 0 us
  Pallas kernels: 0 us -> 11.8 us
  waiting for transfers between devices: 0.01 us -> 10.2 us
  local copies, waits for them, and re-layouts: 12.3 us -> 3.53 us
  other arithmetic: 7.3 us -> 0.12 us
  between operations: 3.51 us -> 0.98 us
    all_gather x3 -> x0, blocking collectives: 58.1 us -> none  [the longest x1 20.4 us: body(): piece = lax.all_gather(kv_base[0], 'ctx', axis=0, tiled=True)]
    ppermute x0 -> x19, starting transfers between devices: none -> 47.1 us  [the longest x15 43.9 us: chain(): array = lax.ppermute(array, 'ctx', pairs)]
    dot_general x5 -> x0, matrix products: 14.2 us -> none  [the longest x1 4.29 us: body(): jnp.einsum('qa,ard->qrd', select, adapter_down, preferred_element_type=jn...]
    pallas_call x0 -> x4, Pallas kernels: none -> 11.8 us  [the longest x1 8.37 us: attend(): pl.pallas_call(functools.partial(attend_kernel, count=count), out_shape=j...]
    ppermute x0 -> x19, waiting for transfers between devices: none -> 10.2 us  [the longest x2 6.32 us: fetch(): far = lax.ppermute(keep[1] + near[1], 'req', [(i, i ^ 2) for i in range(4)])]
    all_to_all x2 -> x0, starting transfers between devices: 8.43 us -> none  [the longest x1 4.22 us: body(): lax.all_to_all(send_down, 'req', split_axis=0, concat_axis=0, tiled=True)]
    reduce_sum x4 -> x0, other arithmetic: 3.52 us -> none  [the longest x1 1.11 us: key_block(): total = total * factor + jnp.sum(weight, axis=-1)]
    convert_element_type x3 -> x0, local copies, waits for them, and re-layouts: 3.1 us -> none  [the longest x1 1.13 us: body(): jnp.where(query_pos[:, None] < length, output, 0.0).astype(jnp.bfloat16)]
  transfers between devices with their start and end apart: 2 -> 19, of which waited for: 0 -> 3; matrix products, arithmetic and copies ran while one was open for 9% -> 0% of each run, Pallas kernels for 0% -> 3%
where the time goes in v1:
time: 74.5 us; the launch traced here: 73.8 us
  starting transfers between devices  47.1 us (63%)
  Pallas kernels  11.8 us (16%)
  waiting for transfers between devices  10.2 us (14%)
  local copies, waits for them, and re-layouts  3.53 us (5%)
  between operations  0.98 us (1%)
    ppermute x15, starting transfers between devices, chain(): array = lax.ppermute(array, 'ctx', pairs)  43.9 us
    pallas_call x1, Pallas kernels, attend(): pl.pallas_call(functools.partial(attend_kernel, count=count), out_shape=j...  8.37 us
    ppermute x2, waiting for transfers between devices, fetch(): far = lax.ppermute(keep[1] + near[1], 'req', [(i, i ^ 2) for i in range(4)])  6.32 us
    ppermute x15, waiting for transfers between devices, chain(): array = lax.ppermute(array, 'ctx', pairs)  3.87 us
    unnamed x16, local copies, waits for them, and re-layouts  3.53 us
    ppermute x2, starting transfers between devices, fetch(): far = lax.ppermute(keep[1] + near[1], 'req', [(i, i ^ 2) for i in range(4)])  2.16 us
    pallas_call x2, Pallas kernels, select(): pl.pallas_call(select_kernel, out_shape=(shape, shape), in_specs=[spec(SM...  1.99 us
  transfers between devices with their start and end apart: 19, of which 3 were waited for; matrix products, arithmetic and copies ran while one was open for 0% of the time, Pallas kernels for 3%

profile of v1, /device:TPU:0, one launch (start us, length us, event | category | flops | bytes accessed | tf_op | source)
XLA Modules:
  0.0 73.8 jit_solution(10675408927872722911)
XLA Ops:
  0.0 0.0 copy-start
  0.0 2.0 %copy-done = bf16[16,896,128]{2,1,0:T(8,128)(2,1)S(1)} copy-done((bf16[16,896,128]{2,1,0:T(8,128)(2,1)S(1)}, bf16[16,896,128]{2,1,0:T(8,128)(2,1)}, u32[]{:S(2)}) %copy-start) | copy-done | bytes 3670040
  2.0 0.0 copy-start.3
  2.0 0.7 copy-done.3
  2.7 0.0 copy-start.4
  2.7 0.7 copy-done.4
  3.4 0.0 copy-start.1
  3.4 0.0 copy-start.7
  3.4 1.1 %shard_map.91 = (bf16[2,896,128]{2,1,0:T(8,128)(2,1)S(1)}, bf16[2,896,128]{2,1,0:T(8,128)(2,1)S(1)}) custom-call(s32[4]{0:T(128)S(1)} %copy-done.3, s32[64]{0:T(128)S(1)} %copy-done.4, bf16[16,896,128]{2,1,0:T(8,128)(2,1)S(1)} %copy-done), custom_call_target="tpu_custom_call" | custom-call | tf_op jit(solution)/shard_map/pallas_call | solution.py:54
  4.4 0.0 copy-start.2
  4.4 0.0 copy-start.5
  4.4 0.0 copy-start.6
  4.5 0.5 collective-permute-start
  5.0 0.2 copy-done.1
  5.1 0.9 %shard_map.93 = (bf16[2,32,2688]{2,1,0:T(8,128)(2,1)S(1)}, bf16[2,32,2688]{2,1,0:T(8,128)(2,1)S(1)}) custom-call(s32[4]{0:T(128)S(1)} %copy-done.3, s32[64]{0:T(128)S(1)} %copy-done.4, bf16[16,32,2688]{2,1,0:T(8,128)(2,1)S(1)} %copy-done.1), custom_call_target="tpu_custom_call" | custom-call | tf_op jit(solution)/shard_map/pallas_call | solution.py:54
  6.1 0.5 collective-permute-start.11
  6.6 0.0 copy-done.7
  6.6 4.5 %collective-permute-start.8 = (bf16[128,768]{1,0:T(8,128)(2,1)S(1)}, bf16[128,768]{1,0:T(8,128)(2,1)S(1)}, u32[]{:S(2)}, u32[]{:S(2)}) collective-permute-start(bf16[128,768]{1,0:T(8,128)(2,1)S(1)} %bitcast.18), channel_id=1, source_target_pairs={{0,4},{4,8},{8,12},{1,5},{5,9},{9,13},{2,6},{6,10},{10,14},{3,7},{... | collective-permute-start | bytes 589832 | tf_op jit(solution)/shard_map/ppermute | solution.py:75
  11.1 0.0 collective-permute-done
  11.1 1.6 %collective-permute-start.1 = (bf16[896,128]{1,0:T(8,128)(2,1)S(1)}, bf16[896,128]{1,0:T(8,128)(2,1)S(1)}, u32[]{:S(2)}, u32[]{:S(2)}) collective-permute-start(bf16[896,128]{1,0:T(8,128)(2,1)S(1)} %fusion), channel_id=1, source_target_pairs={{0,2},{1,3},{2,0},{3,1},{4,6},{5,7},{6,4},{7,5},{8,10},{9,11},{10,... | collective-permute-start | bytes 688136 | tf_op jit(solution)/shard_map/ppermute | solution.py:67
  12.7 0.0 collective-permute-done.11
  12.7 0.6 collective-permute-start.12
  13.3 6.3 %collective-permute-done.1 = bf16[896,128]{1,0:T(8,128)(2,1)S(1)} collective-permute-done((bf16[896,128]{1,0:T(8,128)(2,1)S(1)}, bf16[896,128]{1,0:T(8,128)(2,1)S(1)}, u32[]{:S(2)}, u32[]{:S(2)}) %collective-permute-start.1) | collective-permute-done | bytes 229408 | tf_op jit(solution)/shard_map/ppermute | solution.py:67
  19.7 3.5 %collective-permute-start.2 = (bf16[896,128]{1,0:T(8,128)(2,1)S(1)}, bf16[896,128]{1,0:T(8,128)(2,1)S(1)}, u32[]{:S(2)}, u32[]{:S(2)}) collective-permute-start(bf16[896,128]{1,0:T(8,128)(2,1)S(1)} %fusion.2.rest_0_), channel_id=1, source_target_pairs={{0,4},{4,8},{8,12},{1,5},{5,9},{9,13},{2,6},{6,10},{10,14},{3,7},{... | collective-permute-start | bytes 688136 | tf_op jit(solution)/shard_map/ppermute | solution.py:75
  23.2 1.3 %collective-permute-start.5 = (bf16[896,128]{1,0:T(8,128)(2,1)S(1)}, bf16[896,128]{1,0:T(8,128)(2,1)S(1)}, u32[]{:S(2)}, u32[]{:S(2)}) collective-permute-start(bf16[896,128]{1,0:T(8,128)(2,1)S(1)} %fusion.2.rest_0_), channel_id=1, source_target_pairs={{4,0},{8,4},{12,8},{5,1},{9,5},{13,9},{6,2},{10,6},{14,10},{7,3},{... | collective-permute-start | bytes 688136 | tf_op jit(solution)/shard_map/ppermute | solution.py:75
  24.5 0.0 collective-permute-done.12
  24.5 4.6 %collective-permute-start.13 = (bf16[32,2688]{1,0:T(8,128)(2,1)S(1)}, bf16[32,2688]{1,0:T(8,128)(2,1)S(1)}, u32[]{:S(2)}, u32[]{:S(2)}) collective-permute-start(bf16[32,2688]{1,0:T(8,128)(2,1)S(1)} %fusion.5.rest_4_), channel_id=1, source_target_pairs={{0,4},{4,8},{8,12},{1,5},{5,9},{9,13},{2,6},{6,10},{10,14},{3,7},{... | collective-permute-start | bytes 516104 | tf_op jit(solution)/shard_map/ppermute | solution.py:75
  29.1 1.3 %collective-permute-start.16 = (bf16[32,2688]{1,0:T(8,128)(2,1)S(1)}, bf16[32,2688]{1,0:T(8,128)(2,1)S(1)}, u32[]{:S(2)}, u32[]{:S(2)}) collective-permute-start(bf16[32,2688]{1,0:T(8,128)(2,1)S(1)} %fusion.5.rest_4_), channel_id=1, source_target_pairs={{4,0},{8,4},{12,8},{5,1},{9,5},{13,9},{6,2},{10,6},{14,10},{7,3},{... | collective-permute-start | bytes 516104 | tf_op jit(solution)/shard_map/ppermute | solution.py:75
  30.4 0.0 collective-permute-done.2.rest_1_
  30.4 4.6 %collective-permute-start.3 = (bf16[896,128]{1,0:T(8,128)(2,1)S(1)}, bf16[896,128]{1,0:T(8,128)(2,1)S(1)}, u32[]{:S(2)}, u32[]{:S(2)}) collective-permute-start(bf16[896,128]{1,0:T(8,128)(2,1)S(1)} %collective-permute-done.2.rest_1_), channel_id=1, source_target_pairs={{0,4},{4,8},{8,12},{1,5},{5,9},{9,13},{2,6},{6,10},{10,14},{3,7},{... | collective-permute-start | bytes 688136 | tf_op jit(solution)/shard_map/ppermute | solution.py:75
  35.0 0.0 collective-permute-done.5.rest_4_
  35.0 1.3 %collective-permute-start.6 = (bf16[896,128]{1,0:T(8,128)(2,1)S(1)}, bf16[896,128]{1,0:T(8,128)(2,1)S(1)}, u32[]{:S(2)}, u32[]{:S(2)}) collective-permute-start(bf16[896,128]{1,0:T(8,128)(2,1)S(1)} %collective-permute-done.5.rest_4_), channel_id=1, source_target_pairs={{4,0},{8,4},{12,8},{5,1},{9,5},{13,9},{6,2},{10,6},{14,10},{7,3},{... | collective-permute-start | bytes 688136 | tf_op jit(solution)/shard_map/ppermute | solution.py:75
  36.3 0.0 collective-permute-done.8.rest_1_
  36.3 4.6 %collective-permute-start.9 = (bf16[128,768]{1,0:T(8,128)(2,1)S(1)}, bf16[128,768]{1,0:T(8,128)(2,1)S(1)}, u32[]{:S(2)}, u32[]{:S(2)}) collective-permute-start(bf16[128,768]{1,0:T(8,128)(2,1)S(1)} %collective-permute-done.8.rest_1_), channel_id=1, source_target_pairs={{0,4},{4,8},{8,12},{1,5},{5,9},{9,13},{2,6},{6,10},{10,14},{3,7},{... | collective-permute-start | bytes 589832 | tf_op jit(solution)/shard_map/ppermute | solution.py:75
  40.9 0.0 collective-permute-done.13.rest_5_
  40.9 3.5 %collective-permute-start.14 = (bf16[32,2688]{1,0:T(8,128)(2,1)S(1)}, bf16[32,2688]{1,0:T(8,128)(2,1)S(1)}, u32[]{:S(2)}, u32[]{:S(2)}) collective-permute-start(bf16[32,2688]{1,0:T(8,128)(2,1)S(1)} %collective-permute-done.13.rest_5_), channel_id=1, source_target_pairs={{0,4},{4,8},{8,12},{1,5},{5,9},{9,13},{2,6},{6,10},{10,14},{3,7},{... | collective-permute-start | bytes 516104 | tf_op jit(solution)/shard_map/ppermute | solution.py:75
  44.3 0.0 collective-permute-done.16.rest_8_
  44.4 1.3 %collective-permute-start.17 = (bf16[32,2688]{1,0:T(8,128)(2,1)S(1)}, bf16[32,2688]{1,0:T(8,128)(2,1)S(1)}, u32[]{:S(2)}, u32[]{:S(2)}) collective-permute-start(bf16[32,2688]{1,0:T(8,128)(2,1)S(1)} %collective-permute-done.16.rest_8_), channel_id=1, source_target_pairs={{4,0},{8,4},{12,8},{5,1},{9,5},{13,9},{6,2},{10,6},{14,10},{7,3},{... | collective-permute-start | bytes 516104 | tf_op jit(solution)/shard_map/ppermute | solution.py:75
  45.7 0.0 collective-permute-done.3.rest_2_
  45.7 4.6 %collective-permute-start.4 = (bf16[896,128]{1,0:T(8,128)(2,1)S(1)}, bf16[896,128]{1,0:T(8,128)(2,1)S(1)}, u32[]{:S(2)}, u32[]{:S(2)}) collective-permute-start(bf16[896,128]{1,0:T(8,128)(2,1)S(1)} %collective-permute-done.3.rest_2_), channel_id=1, source_target_pairs={{0,4},{4,8},{8,12},{1,5},{5,9},{9,13},{2,6},{6,10},{10,14},{3,7},{... | collective-permute-start | bytes 688136 | tf_op jit(solution)/shard_map/ppermute | solution.py:75
  50.2 0.0 collective-permute-done.6.rest_5_
  50.2 1.3 %collective-permute-start.7 = (bf16[896,128]{1,0:T(8,128)(2,1)S(1)}, bf16[896,128]{1,0:T(8,128)(2,1)S(1)}, u32[]{:S(2)}, u32[]{:S(2)}) collective-permute-start(bf16[896,128]{1,0:T(8,128)(2,1)S(1)} %collective-permute-done.6.rest_5_), channel_id=1, source_target_pairs={{4,0},{8,4},{12,8},{5,1},{9,5},{13,9},{6,2},{10,6},{14,10},{7,3},{... | collective-permute-start | bytes 688136 | tf_op jit(solution)/shard_map/ppermute | solution.py:75
  51.5 0.0 collective-permute-done.9.rest_2_
  51.6 4.6 %collective-permute-start.10 = (bf16[128,768]{1,0:T(8,128)(2,1)S(1)}, bf16[128,768]{1,0:T(8,128)(2,1)S(1)}, u32[]{:S(2)}, u32[]{:S(2)}) collective-permute-start(bf16[128,768]{1,0:T(8,128)(2,1)S(1)} %collective-permute-done.9.rest_2_), channel_id=1, source_target_pairs={{0,4},{4,8},{8,12},{1,5},{5,9},{9,13},{2,6},{6,10},{10,14},{3,7},{... | collective-permute-start | bytes 589832 | tf_op jit(solution)/shard_map/ppermute | solution.py:75
  56.1 0.0 collective-permute-done.14.rest_6_
  56.1 1.9 %collective-permute-start.15 = (bf16[32,2688]{1,0:T(8,128)(2,1)S(1)}, bf16[32,2688]{1,0:T(8,128)(2,1)S(1)}, u32[]{:S(2)}, u32[]{:S(2)}) collective-permute-start(bf16[32,2688]{1,0:T(8,128)(2,1)S(1)} %collective-permute-done.14.rest_6_), channel_id=1, source_target_pairs={{0,4},{4,8},{8,12},{1,5},{5,9},{9,13},{2,6},{6,10},{10,14},{3,7},{... | collective-permute-start | bytes 516104 | tf_op jit(solution)/shard_map/ppermute | solution.py:75
  58.1 0.0 collective-permute-done.17.rest_9_
  58.1 1.3 %collective-permute-start.18 = (bf16[32,2688]{1,0:T(8,128)(2,1)S(1)}, bf16[32,2688]{1,0:T(8,128)(2,1)S(1)}, u32[]{:S(2)}, u32[]{:S(2)}) collective-permute-start(bf16[32,2688]{1,0:T(8,128)(2,1)S(1)} %collective-permute-done.17.rest_9_), channel_id=1, source_target_pairs={{4,0},{8,4},{12,8},{5,1},{9,5},{13,9},{6,2},{10,6},{14,10},{7,3},{... | collective-permute-start | bytes 516104 | tf_op jit(solution)/shard_map/ppermute | solution.py:75
  60.0 0.0 collective-permute-done.4.rest_3_
  60.0 0.0 collective-permute-done.7.rest_6_
  60.0 0.0 copy-done.2
  60.1 0.0 copy-done.5
  60.1 1.5 %shard_map.92.low = bf16[128,128]{1,0:T(8,128)(2,1)S(1)} custom-call(s32[4]{0:T(128)S(1)} %copy-done.3, s32[64]{0:T(128)S(1)} %copy-done.5, bf16[128,3584]{1,0:T(8,128)(2,1)S(1)} %bitcast.16, bf16[896,128]{1,0:T(8,128)(2,1)S(1)} %fusion.2.rest_0_, bf16[896,128]{1,0:T(8,128)(2,1)S(1)} %collective-permute-done.2.rest_1_, ...), custom_call_target="tpu_custom_call" | custom-call | flops 134217728 | bytes 4194304 | tf_op jit(solution)/shard_map/pallas_call | solution.py:106
  61.5 0.0 collective-permute-done.10.rest_3_
  61.5 0.1 collective-permute-done.15.rest_7_
  61.6 3.7 %collective-permute-done.18.rest_10_ = bf16[32,2688]{1,0:T(8,128)(2,1)S(1)} collective-permute-done((bf16[32,2688]{1,0:T(8,128)(2,1)S(1)}, bf16[32,2688]{1,0:T(8,128)(2,1)S(1)}, u32[]{:S(2)}, u32[]{:S(2)}) %collective-permute-start.18) | collective-permute-done | bytes 172064 | tf_op jit(solution)/shard_map/ppermute | solution.py:75
  65.4 0.0 copy-done.6
  65.4 8.4 %shard_map.94 = bf16[128,2688]{1,0:T(8,128)(2,1)} custom-call(s32[1]{0:T(128)S(6)} %copy.10.lengths, bf16[128,2688]{1,0:T(8,128)(2,1)S(1)} %bitcast.17, bf16[128,128]{1,0:T(8,128)(2,1)S(1)} %shard_map.92.low, bf16[128,768]{1,0:T(8,128)(2,1)S(1)} %bitcast.19, bf16[128,768]{1,0:T(8,128)(2,1)S(1)} %collective-permute-done.8.rest_1_, ...), custom_call_target="tpu_custom_call" | custom-call | flops 1073741824 | bytes 4194304 | tf_op jit(solution)/shard_map/pallas_call | solution.py:172
  (4 shorter events, 0.1 us)
Async XLA Ops:
  0.0 2.0 %copy-start = (bf16[16,896,128]{2,1,0:T(8,128)(2,1)S(1)}, bf16[16,896,128]{2,1,0:T(8,128)(2,1)}, u32[]{:S(2)}) copy-start(bf16[16,896,128]{2,1,0:T(8,128)(2,1)} %store.2) | copy-start | bytes 11010052
  2.0 0.7 copy-start.3
  2.7 0.7 copy-start.4
  3.4 1.8 %copy-start.1 = (bf16[16,32,2688]{2,1,0:T(8,128)(2,1)S(1)}, bf16[16,32,2688]{2,1,0:T(8,128)(2,1)}, u32[]{:S(2)}) copy-start(bf16[16,32,2688]{2,1,0:T(8,128)(2,1)} %store.3) | copy-start | bytes 8257540
  3.4 3.2 %copy-start.7 = (bf16[1,128,768]{2,1,0:T(8,128)(2,1)S(1)}, bf16[1,128,768]{2,1,0:T(8,128)(2,1)}, u32[]{:S(2)}) copy-start(bf16[1,128,768]{2,1,0:T(8,128)(2,1)} %param.11) | copy-start | bytes 589828
  4.4 55.6 %copy-start.2 = (bf16[1,128,3584]{2,1,0:T(8,128)(2,1)S(1)}, bf16[1,128,3584]{2,1,0:T(8,128)(2,1)}, u32[]{:S(2)}) copy-start(bf16[1,128,3584]{2,1,0:T(8,128)(2,1)} %param.9) | copy-start | bytes 2752516
  4.4 55.6 %copy-start.5 = (s32[64]{0:T(128)S(1)}, s32[64]{0:T(128)}, u32[]{:S(2)}) copy-start(s32[64]{0:T(128)} %ranks.1) | copy-start | bytes 772
  4.4 60.9 %copy-start.6 = (bf16[1,128,2688]{2,1,0:T(8,128)(2,1)S(1)}, bf16[1,128,2688]{2,1,0:T(8,128)(2,1)}, u32[]{:S(2)}) copy-start(bf16[1,128,2688]{2,1,0:T(8,128)(2,1)} %param.10) | copy-start | bytes 2064388
  4.5 6.6 %collective-permute-start = (bf16[2,896,128]{2,1,0:T(8,128)(2,1)S(1)}, bf16[2,896,128]{2,1,0:T(8,128)(2,1)S(1)}, u32[]{:S(2)}, u32[]{:S(2)}) collective-permute-start(bf16[2,896,128]{2,1,0:T(8,128)(2,1)S(1)} %get-tuple-element.10), channel_id=1, source_target_pairs={{0,1},{1,0},{2,3},{3,2},{4,5},{5,4},{6,7},{7,6},{8,9},{9,8},{10,11... | collective-permute-start | bytes 1376264 | tf_op jit(solution)/shard_map/ppermute | solution.py:66
  6.1 6.6 %collective-permute-start.11 = (bf16[2,32,2688]{2,1,0:T(8,128)(2,1)S(1)}, bf16[2,32,2688]{2,1,0:T(8,128)(2,1)S(1)}, u32[]{:S(2)}, u32[]{:S(2)}) collective-permute-start(bf16[2,32,2688]{2,1,0:T(8,128)(2,1)S(1)} %get-tuple-element.12), channel_id=1, source_target_pairs={{0,1},{1,0},{2,3},{3,2},{4,5},{5,4},{6,7},{7,6},{8,9},{9,8},{10,11... | collective-permute-start | bytes 1032200 | tf_op jit(solution)/shard_map/ppermute | solution.py:66
  6.6 29.7 %collective-permute-start.8 = (bf16[128,768]{1,0:T(8,128)(2,1)S(1)}, bf16[128,768]{1,0:T(8,128)(2,1)S(1)}, u32[]{:S(2)}, u32[]{:S(2)}) collective-permute-start(bf16[128,768]{1,0:T(8,128)(2,1)S(1)} %bitcast.18), channel_id=1, source_target_pairs={{0,4},{4,8},{8,12},{1,5},{5,9},{9,13},{2,6},{6,10},{10,14},{3,7},{... | collective-permute-start | bytes 589832 | tf_op jit(solution)/shard_map/ppermute | solution.py:75
  11.1 8.5 %collective-permute-start.1 = (bf16[896,128]{1,0:T(8,128)(2,1)S(1)}, bf16[896,128]{1,0:T(8,128)(2,1)S(1)}, u32[]{:S(2)}, u32[]{:S(2)}) collective-permute-start(bf16[896,128]{1,0:T(8,128)(2,1)S(1)} %fusion), channel_id=1, source_target_pairs={{0,2},{1,3},{2,0},{3,1},{4,6},{5,7},{6,4},{7,5},{8,10},{9,11},{10,... | collective-permute-start | bytes 688136 | tf_op jit(solution)/shard_map/ppermute | solution.py:67
  12.7 11.8 %collective-permute-start.12 = (bf16[32,2688]{1,0:T(8,128)(2,1)S(1)}, bf16[32,2688]{1,0:T(8,128)(2,1)S(1)}, u32[]{:S(2)}, u32[]{:S(2)}) collective-permute-start(bf16[32,2688]{1,0:T(8,128)(2,1)S(1)} %fusion.3), channel_id=1, source_target_pairs={{0,2},{1,3},{2,0},{3,1},{4,6},{5,7},{6,4},{7,5},{8,10},{9,11},{10,... | collective-permute-start | bytes 516104 | tf_op jit(solution)/shard_map/ppermute | solution.py:67
  19.7 10.7 %collective-permute-start.2 = (bf16[896,128]{1,0:T(8,128)(2,1)S(1)}, bf16[896,128]{1,0:T(8,128)(2,1)S(1)}, u32[]{:S(2)}, u32[]{:S(2)}) collective-permute-start(bf16[896,128]{1,0:T(8,128)(2,1)S(1)} %fusion.2.rest_0_), channel_id=1, source_target_pairs={{0,4},{4,8},{8,12},{1,5},{5,9},{9,13},{2,6},{6,10},{10,14},{3,7},{... | collective-permute-start | bytes 688136 | tf_op jit(solution)/shard_map/ppermute | solution.py:75
  23.2 11.8 %collective-permute-start.5 = (bf16[896,128]{1,0:T(8,128)(2,1)S(1)}, bf16[896,128]{1,0:T(8,128)(2,1)S(1)}, u32[]{:S(2)}, u32[]{:S(2)}) collective-permute-start(bf16[896,128]{1,0:T(8,128)(2,1)S(1)} %fusion.2.rest_0_), channel_id=1, source_target_pairs={{4,0},{8,4},{12,8},{5,1},{9,5},{13,9},{6,2},{10,6},{14,10},{7,3},{... | collective-permute-start | bytes 688136 | tf_op jit(solution)/shard_map/ppermute | solution.py:75
  24.5 16.3 %collective-permute-start.13 = (bf16[32,2688]{1,0:T(8,128)(2,1)S(1)}, bf16[32,2688]{1,0:T(8,128)(2,1)S(1)}, u32[]{:S(2)}, u32[]{:S(2)}) collective-permute-start(bf16[32,2688]{1,0:T(8,128)(2,1)S(1)} %fusion.5.rest_4_), channel_id=1, source_target_pairs={{0,4},{4,8},{8,12},{1,5},{5,9},{9,13},{2,6},{6,10},{10,14},{3,7},{... | collective-permute-start | bytes 516104 | tf_op jit(solution)/shard_map/ppermute | solution.py:75
  29.1 15.2 %collective-permute-start.16 = (bf16[32,2688]{1,0:T(8,128)(2,1)S(1)}, bf16[32,2688]{1,0:T(8,128)(2,1)S(1)}, u32[]{:S(2)}, u32[]{:S(2)}) collective-permute-start(bf16[32,2688]{1,0:T(8,128)(2,1)S(1)} %fusion.5.rest_4_), channel_id=1, source_target_pairs={{4,0},{8,4},{12,8},{5,1},{9,5},{13,9},{6,2},{10,6},{14,10},{7,3},{... | collective-permute-start | bytes 516104 | tf_op jit(solution)/shard_map/ppermute | solution.py:75
  30.4 15.2 %collective-permute-start.3 = (bf16[896,128]{1,0:T(8,128)(2,1)S(1)}, bf16[896,128]{1,0:T(8,128)(2,1)S(1)}, u32[]{:S(2)}, u32[]{:S(2)}) collective-permute-start(bf16[896,128]{1,0:T(8,128)(2,1)S(1)} %collective-permute-done.2.rest_1_), channel_id=1, source_target_pairs={{0,4},{4,8},{8,12},{1,5},{5,9},{9,13},{2,6},{6,10},{10,14},{3,7},{... | collective-permute-start | bytes 688136 | tf_op jit(solution)/shard_map/ppermute | solution.py:75
  35.0 15.2 %collective-permute-start.6 = (bf16[896,128]{1,0:T(8,128)(2,1)S(1)}, bf16[896,128]{1,0:T(8,128)(2,1)S(1)}, u32[]{:S(2)}, u32[]{:S(2)}) collective-permute-start(bf16[896,128]{1,0:T(8,128)(2,1)S(1)} %collective-permute-done.5.rest_4_), channel_id=1, source_target_pairs={{4,0},{8,4},{12,8},{5,1},{9,5},{13,9},{6,2},{10,6},{14,10},{7,3},{... | collective-permute-start | bytes 688136 | tf_op jit(solution)/shard_map/ppermute | solution.py:75
  36.3 15.2 %collective-permute-start.9 = (bf16[128,768]{1,0:T(8,128)(2,1)S(1)}, bf16[128,768]{1,0:T(8,128)(2,1)S(1)}, u32[]{:S(2)}, u32[]{:S(2)}) collective-permute-start(bf16[128,768]{1,0:T(8,128)(2,1)S(1)} %collective-permute-done.8.rest_1_), channel_id=1, source_target_pairs={{0,4},{4,8},{8,12},{1,5},{5,9},{9,13},{2,6},{6,10},{10,14},{3,7},{... | collective-permute-start | bytes 589832 | tf_op jit(solution)/shard_map/ppermute | solution.py:75
  40.9 15.2 %collective-permute-start.14 = (bf16[32,2688]{1,0:T(8,128)(2,1)S(1)}, bf16[32,2688]{1,0:T(8,128)(2,1)S(1)}, u32[]{:S(2)}, u32[]{:S(2)}) collective-permute-start(bf16[32,2688]{1,0:T(8,128)(2,1)S(1)} %collective-permute-done.13.rest_5_), channel_id=1, source_target_pairs={{0,4},{4,8},{8,12},{1,5},{5,9},{9,13},{2,6},{6,10},{10,14},{3,7},{... | collective-permute-start | bytes 516104 | tf_op jit(solution)/shard_map/ppermute | solution.py:75
  44.4 13.7 %collective-permute-start.17 = (bf16[32,2688]{1,0:T(8,128)(2,1)S(1)}, bf16[32,2688]{1,0:T(8,128)(2,1)S(1)}, u32[]{:S(2)}, u32[]{:S(2)}) collective-permute-start(bf16[32,2688]{1,0:T(8,128)(2,1)S(1)} %collective-permute-done.16.rest_8_), channel_id=1, source_target_pairs={{4,0},{8,4},{12,8},{5,1},{9,5},{13,9},{6,2},{10,6},{14,10},{7,3},{... | collective-permute-start | bytes 516104 | tf_op jit(solution)/shard_map/ppermute | solution.py:75
  45.7 14.4 %collective-permute-start.4 = (bf16[896,128]{1,0:T(8,128)(2,1)S(1)}, bf16[896,128]{1,0:T(8,128)(2,1)S(1)}, u32[]{:S(2)}, u32[]{:S(2)}) collective-permute-start(bf16[896,128]{1,0:T(8,128)(2,1)S(1)} %collective-permute-done.3.rest_2_), channel_id=1, source_target_pairs={{0,4},{4,8},{8,12},{1,5},{5,9},{9,13},{2,6},{6,10},{10,14},{3,7},{... | collective-permute-start | bytes 688136 | tf_op jit(solution)/shard_map/ppermute | solution.py:75
  50.2 9.8 %collective-permute-start.7 = (bf16[896,128]{1,0:T(8,128)(2,1)S(1)}, bf16[896,128]{1,0:T(8,128)(2,1)S(1)}, u32[]{:S(2)}, u32[]{:S(2)}) collective-permute-start(bf16[896,128]{1,0:T(8,128)(2,1)S(1)} %collective-permute-done.6.rest_5_), channel_id=1, source_target_pairs={{4,0},{8,4},{12,8},{5,1},{9,5},{13,9},{6,2},{10,6},{14,10},{7,3},{... | collective-permute-start | bytes 688136 | tf_op jit(solution)/shard_map/ppermute | solution.py:75
  51.6 10.0 %collective-permute-start.10 = (bf16[128,768]{1,0:T(8,128)(2,1)S(1)}, bf16[128,768]{1,0:T(8,128)(2,1)S(1)}, u32[]{:S(2)}, u32[]{:S(2)}) collective-permute-start(bf16[128,768]{1,0:T(8,128)(2,1)S(1)} %collective-permute-done.9.rest_2_), channel_id=1, source_target_pairs={{0,4},{4,8},{8,12},{1,5},{5,9},{9,13},{2,6},{6,10},{10,14},{3,7},{... | collective-permute-start | bytes 589832 | tf_op jit(solution)/shard_map/ppermute | solution.py:75
  56.1 5.5 %collective-permute-start.15 = (bf16[32,2688]{1,0:T(8,128)(2,1)S(1)}, bf16[32,2688]{1,0:T(8,128)(2,1)S(1)}, u32[]{:S(2)}, u32[]{:S(2)}) collective-permute-start(bf16[32,2688]{1,0:T(8,128)(2,1)S(1)} %collective-permute-done.14.rest_6_), channel_id=1, source_target_pairs={{0,4},{4,8},{8,12},{1,5},{5,9},{9,13},{2,6},{6,10},{10,14},{3,7},{... | collective-permute-start | bytes 516104 | tf_op jit(solution)/shard_map/ppermute | solution.py:75
  58.1 7.3 %collective-permute-start.18 = (bf16[32,2688]{1,0:T(8,128)(2,1)S(1)}, bf16[32,2688]{1,0:T(8,128)(2,1)S(1)}, u32[]{:S(2)}, u32[]{:S(2)}) collective-permute-start(bf16[32,2688]{1,0:T(8,128)(2,1)S(1)} %collective-permute-done.17.rest_9_), channel_id=1, source_target_pairs={{4,0},{8,4},{12,8},{5,1},{9,5},{13,9},{6,2},{10,6},{14,10},{7,3},{... | collective-permute-start | bytes 516104 | tf_op jit(solution)/shard_map/ppermute | solution.py:75

commit v2 on v1

--- a/solution.py
+++ b/solution.py
@@ -1,4 +1,3 @@
-import functools
 import math
 
 import jax
@@ -14,9 +13,10 @@
 HEADS = KVH * GROUP
 SMEM = pltpu.SMEM
 VMEM = pltpu.VMEM
-ANY = pl.ANY
+HBM = pltpu.HBM
 LOG2E = 1.0 / math.log(2.0)
 PARAMS = pltpu.CompilerParams(vmem_limit_bytes=48 * 1024 * 1024)
+WHOLE = pltpu.CompilerParams(vmem_limit_bytes=62 * 1024 * 1024)
 
 
 def spec(space):
@@ -54,10 +54,10 @@
     return pl.pallas_call(
         select_kernel,
         out_shape=(shape, shape),
-        in_specs=[spec(SMEM), spec(SMEM), spec(ANY)],
+        in_specs=[spec(SMEM), spec(SMEM), spec(HBM)],
         out_specs=(spec(VMEM), spec(VMEM)),
         scratch_shapes=[pltpu.SemaphoreType.DMA((4,))],
-        compiler_params=PARAMS,
+        compiler_params=WHOLE,
     )(ids, slots, store)
 
 
@@ -68,29 +68,40 @@
     return keep[0] + near[0] + far
 
 
-def chain(array, step, count):
-    pairs = [(i, i + step) for i in range(count) if 0 <= i + step < count]
-    found = []
-    for _ in range(count - 1):
-        array = lax.ppermute(array, "ctx", pairs)
-        found.append(array)
-    return found
-
-
-def order(count):
-    return [0] + [-s for s in range(1, count)] + [s for s in range(1, count)]
-
-
-def low_rank_kernel(ids, ranks, hidden, *rest, count):
+def spread(shard):
+    near = lax.ppermute(shard, "ctx", [(0, 1), (1, 0), (2, 3), (3, 2)])
+    cross = lax.ppermute(shard, "ctx", [(0, 3), (3, 0), (1, 2), (2, 1)])
+    inner = lax.ppermute(near, "ctx", [(1, 2), (2, 1)])
+    outer = lax.ppermute(cross, "ctx", [(1, 0), (2, 3)])
+    return [shard, near, cross, inner, outer]
+
+
+def places(z):
+    inner = (z == 1) | (z == 2)
+    return [(z, None), (z ^ 1, None), (z ^ 3, None), (z ^ 2, inner), (z ^ 2, jnp.logical_not(inner))]
+
+
+def when(condition):
+    return (lambda f: f()) if condition is None else pl.when(condition)
+
+
+def spread_up(shard):
+    return [
+        shard,
+        lax.ppermute(shard, "ctx", [(0, 1), (2, 3)]),
+        lax.ppermute(shard, "ctx", [(0, 2), (1, 3)]),
+        lax.ppermute(shard, "ctx", [(0, 3), (1, 2)]),
+    ]
+
+
+def low_rank_kernel(ids, ranks, hidden, *rest):
     pieces, out, accum = rest[:-2], rest[-2], rest[-1]
     rows = pieces[0].shape[0]
-    z = lax.axis_index("ctx")
     rank = ranks[ids[lax.axis_index("req")]]
     accum[...] = jnp.zeros_like(accum)
-    for offset, piece in zip(order(count), pieces):
-        place = z + offset
-
-        @pl.when((place >= 0) & (place < count))
+    for (place, there), piece in zip(places(lax.axis_index("ctx")), pieces):
+
+        @when(there)
         def _():
             columns = pl.ds(pl.multiple_of(place * rows, HD), rows)
             accum[...] += jnp.dot(
@@ -101,10 +112,10 @@
     out[...] = jnp.where(column < rank, accum[...], 0.0).astype(jnp.bfloat16)
 
 
-def low_rank(ids, ranks, hidden, pieces, count):
+def low_rank(ids, ranks, hidden, pieces):
     shape = (hidden.shape[0], pieces[0].shape[1])
     return pl.pallas_call(
-        functools.partial(low_rank_kernel, count=count),
+        low_rank_kernel,
         out_shape=jax.ShapeDtypeStruct(shape, jnp.bfloat16),
         in_specs=[spec(SMEM)] * 2 + [spec(VMEM)] * (1 + len(pieces)),
         out_specs=spec(VMEM),
@@ -114,67 +125,84 @@
     )(ids, ranks, hidden, *pieces)
 
 
-def attend_kernel(lengths, base, low, *rest, count):
-    kvs, ups = rest[:count], rest[count:-2]
-    out, upper = rest[-2:]
+def attend_kernel(lengths, base, low, *rest):
+    kvs, ups = rest[:4], rest[4:9]
+    out, upper, queries = rest[9:]
     tokens = base.shape[0]
     rows = ups[0].shape[0]
     z = lax.axis_index("ctx")
-    for offset, piece in zip(order(count), ups):
-        place = z + offset
-
-        @pl.when((place >= 0) & (place < count))
-        def _():
-            upper[pl.ds(pl.multiple_of(place * rows, rows), rows), :] = piece[...]
-
     live = z * tokens < lengths[0]
     factor = LOG2E / math.sqrt(HD)
+    block = GROUP * tokens
+
+    @pl.when(live)
+    def _():
+        for (place, there), piece in zip(places(z), ups):
+
+            @when(there)
+            def _():
+                upper[pl.ds(pl.multiple_of(place * rows, rows), rows), :] = piece[...]
+
+        for j in range(HEADS):
+            columns = slice(j * HD, (j + 1) * HD)
+            delta = jnp.dot(low[...], upper[:, columns], preferred_element_type=jnp.float32)
+            queries[j * tokens : (j + 1) * tokens, :] = (
+                base[:, columns].astype(jnp.float32) + delta
+            ).astype(jnp.bfloat16)
+
+    @pl.when(jnp.logical_not(live))
+    def _():
+        out[...] = jnp.zeros_like(out)
+
     query_pos = lax.broadcasted_iota(jnp.int32, (tokens, tokens), 0)
     key_pos = lax.broadcasted_iota(jnp.int32, (tokens, tokens), 1)
     causal = key_pos <= query_pos
-
-    @pl.when(jnp.logical_not(live))
-    def _():
-        out[...] = jnp.zeros_like(out)
-
-    for behind in range(count):
-
-        @pl.when(live & (z == behind))
+    for mine, needed in enumerate(((0,), (0, 1), (0, 3, 2), (0, 1, 2, 3))):
+
+        @pl.when(live & (z == mine))
         def _():
             for h in range(KVH):
-                keys = [kv[:, h * HD : (h + 1) * HD] for kv in kvs[: behind + 1]]
-                values = [
-                    kv[:, (KVH + h) * HD : (KVH + h + 1) * HD] for kv in kvs[: behind + 1]
-                ]
+                keys = [kvs[i][:, h * HD : (h + 1) * HD] for i in needed]
+                values = [kvs[i][:, (KVH + h) * HD : (KVH + h + 1) * HD] for i in needed]
                 keys = jnp.concatenate(keys, axis=0)
                 values = jnp.concatenate(values, axis=0)
+                scores = lax.dot_general(
+                    queries[h * block : (h + 1) * block, :],
+                    keys,
+                    (((1,), (1,)), ((), ())),
+                    preferred_element_type=jnp.float32,
+                )
+                weights, totals = [], []
                 for g in range(GROUP):
-                    columns = slice((h * GROUP + g) * HD, (h * GROUP + g + 1) * HD)
-                    delta = jnp.dot(low[...], upper[:, columns], preferred_element_type=jnp.float32)
-                    query = (base[:, columns].astype(jnp.float32) + delta).astype(jnp.bfloat16)
-                    score = lax.dot_general(
-                        query, keys, (((1,), (1,)), ((), ())), preferred_element_type=jnp.float32
-                    )
+                    score = scores[g * tokens : (g + 1) * tokens, :]
                     own = jnp.where(causal, score[:, :tokens], -1e30)
-                    if behind:
+                    if mine:
                         own = jnp.concatenate([own, score[:, tokens:]], axis=1)
-                    score = own
-                    largest = jnp.max(score, axis=1, keepdims=True)
-                    weight = jnp.exp2((score - largest) * factor)
-                    total = jnp.sum(weight, axis=1, keepdims=True)
-                    product = jnp.dot(
-                        weight.astype(jnp.bfloat16), values, preferred_element_type=jnp.float32
-                    )
-                    out[:, columns] = (product / total).astype(jnp.bfloat16)
-
-
-def attend(lengths, base, low, kvs, ups, count):
+                    largest = jnp.max(own, axis=1, keepdims=True)
+                    weight = jnp.exp2((own - largest) * factor)
+                    totals.append(jnp.sum(weight, axis=1, keepdims=True))
+                    weights.append(weight.astype(jnp.bfloat16))
+                product = jnp.dot(
+                    jnp.concatenate(weights, axis=0), values, preferred_element_type=jnp.float32
+                )
+                for g in range(GROUP):
+                    j = h * GROUP + g
+                    out[:, j * HD : (j + 1) * HD] = (
+                        product[g * tokens : (g + 1) * tokens, :] / totals[g]
+                    ).astype(jnp.bfloat16)
+
+
+def attend(lengths, base, low, kvs, ups):
+    tokens, width = base.shape
     return pl.pallas_call(
-        functools.partial(attend_kernel, count=count),
+        attend_kernel,
         out_shape=jax.ShapeDtypeStruct(base.shape, jnp.bfloat16),
         in_specs=[spec(SMEM)] + [spec(VMEM)] * (2 + len(kvs) + len(ups)),
         out_specs=spec(VMEM),
-        scratch_shapes=[VMEM((low.shape[1], base.shape[1]), jnp.bfloat16)],
+        scratch_shapes=[
+            VMEM((low.shape[1], width), jnp.bfloat16),
+            VMEM((HEADS * tokens, HD), jnp.bfloat16),
+        ],
         compiler_params=PARAMS,
         cost_estimate=pl.CostEstimate(
             flops=1 << 30, bytes_accessed=1 << 22, transcendentals=1 << 21
@@ -192,17 +220,16 @@
     adapter_slots,
     rank_buckets,
     lengths,
-    *,
-    count,
 ):
-    kv = kv_base[0]
-    kvs = [kv] + chain(kv, 1, count)
+    kvs = spread_up(kv_base[0])
     down = fetch(adapter_ids, adapter_slots, adapter_down)
-    downs = [down] + chain(down, 1, count) + chain(down, -1, count)
+    down, kvs[1] = lax.optimization_barrier((down, kvs[1]))
+    downs = spread(down)
     up = fetch(adapter_ids, adapter_slots, adapter_up)
-    ups = [up] + chain(up, 1, count) + chain(up, -1, count)
-    low = low_rank(adapter_ids, rank_buckets, hidden_states[0], downs, count)
-    return attend(lengths, queries_base[0], low, kvs, ups, count)[None]
+    up, kvs[2], kvs[3] = lax.optimization_barrier((up, kvs[2], kvs[3]))
+    ups = spread(up)
+    low = low_rank(adapter_ids, rank_buckets, hidden_states[0], downs)
+    return attend(lengths, queries_base[0], low, kvs, ups)[None]
 
 
 def plain_body(
@@ -322,13 +349,9 @@
 
 
 def solution(mesh):
-    count = mesh.shape["ctx"]
-    if count == 4 and mesh.shape["req"] == 4:
-        local = functools.partial(body, count=count)
-    else:
-        local = plain_body
+    paired = mesh.shape["ctx"] == 4 and mesh.shape["req"] == 4
     return jax.shard_map(
-        local,
+        body if paired else plain_body,
         mesh=mesh,
         in_specs=(
             P(("group", "req"), "ctx", None),

time: 74.5 us -> 60.2 us (0.81)
  the two profiles are of different devices: /device:TPU:0 before, /device:TPU:18 now
where the time goes in v2:
time: 60.2 us; the launch traced here: 59.3 us
  starting transfers between devices  31 us (51%)
  waiting for transfers between devices  14 us (23%)
  Pallas kernels  9.29 us (15%)
  other arithmetic  4.08 us (7%)
  between operations  0.84 us (1%)
    ppermute x2, starting transfers between devices, spread(): near = lax.ppermute(shard, 'ctx', [(0, 1), (1, 0), (2, 3), (3, 2)])  9.69 us
    ppermute x2, starting transfers between devices, spread(): inner = lax.ppermute(near, 'ctx', [(1, 2), (2, 1)])  5.84 us
    ppermute x2, waiting for transfers between devices, fetch(): far = lax.ppermute(keep[1] + near[1], 'req', [(i, i ^ 2) for i in range(4)])  5.45 us
    pallas_call x2, Pallas kernels, select(): pl.pallas_call(select_kernel, out_shape=(shape, shape), in_specs=[spec(SM...  5.37 us
    ppermute x2, waiting for transfers between devices, spread(): inner = lax.ppermute(near, 'ctx', [(1, 2), (2, 1)])  4.92 us
    ppermute x2, starting transfers between devices, spread(): cross = lax.ppermute(shard, 'ctx', [(0, 3), (3, 0), (1, 2), (2, 1)])  4.14 us
    ppermute x2, waiting for transfers between devices, spread(): cross = lax.ppermute(shard, 'ctx', [(0, 3), (3, 0), (1, 2), (2, 1)])  3.65 us
    ppermute x1, starting transfers between devices, spread_up(): lax.ppermute(shard, 'ctx', [(0, 1), (2, 3)])  3.48 us
  transfers between devices with their start and end apart: 15, of which 5 were waited for; matrix products, arithmetic and copies ran while one was open for 7% of the time, Pallas kernels for 6%

profile of v2, /device:TPU:18, one launch (start us, length us, event | category | flops | bytes accessed | tf_op | source)
XLA Modules:
  0.0 59.3 jit_solution(703438780795085426)
XLA Ops:
  0.0 0.0 copy-start.4
  0.0 2.7 %shard_map.91 = (bf16[2,896,128]{2,1,0:T(8,128)(2,1)}, bf16[2,896,128]{2,1,0:T(8,128)(2,1)}) custom-call(s32[4]{0:T(128)} %ids.5, s32[64]{0:T(128)} %slots.3, bf16[16,896,128]{2,1,0:T(8,128)(2,1)} %store.2), custom_call_target="tpu_custom_call" | custom-call | tf_op jit(solution)/shard_map/pallas_call | solution.py:54
  2.7 0.0 copy-start
  2.7 0.0 copy-start.1
  2.7 0.0 copy-start.2
  2.8 0.0 copy-start.3
  2.8 0.1 collective-permute-start
  2.9 2.7 %shard_map.93 = (bf16[2,32,2688]{2,1,0:T(8,128)(2,1)}, bf16[2,32,2688]{2,1,0:T(8,128)(2,1)}) custom-call(s32[4]{0:T(128)} %ids.5, s32[64]{0:T(128)} %slots.3, bf16[16,32,2688]{2,1,0:T(8,128)(2,1)} %store.3), custom_call_target="tpu_custom_call" | custom-call | tf_op jit(solution)/shard_map/pallas_call | solution.py:54
  5.5 0.5 collective-permute-start.7
  6.0 0.0 copy-done.4
  6.0 3.5 %collective-permute-start.2 = (bf16[128,768]{1,0:T(8,128)(2,1)S(1)}, bf16[128,768]{1,0:T(8,128)(2,1)S(1)}, u32[]{:S(2)}, u32[]{:S(2)}) collective-permute-start(bf16[128,768]{1,0:T(8,128)(2,1)S(1)} %bitcast.18), channel_id=1, source_target_pairs={{0,4},{8,12},{1,5},{9,13},{2,6},{10,14},{3,7},{11,15},{16,20},{24,... | collective-permute-start | bytes 589832 | tf_op jit(solution)/shard_map/ppermute | solution.py:91
  9.5 1.3 %collective-permute-start.10 = (bf16[128,768]{1,0:T(8,128)(2,1)S(1)}, bf16[128,768]{1,0:T(8,128)(2,1)S(1)}, u32[]{:S(2)}, u32[]{:S(2)}) collective-permute-start(bf16[128,768]{1,0:T(8,128)(2,1)S(1)} %bitcast.19), channel_id=1, source_target_pairs={{0,12},{4,8},{1,13},{5,9},{2,14},{6,10},{3,15},{7,11},{16,28},{20,... | collective-permute-start | bytes 589832 | tf_op jit(solution)/shard_map/ppermute | solution.py:93
  10.8 1.3 %collective-permute-start.9 = (bf16[128,768]{1,0:T(8,128)(2,1)S(1)}, bf16[128,768]{1,0:T(8,128)(2,1)S(1)}, u32[]{:S(2)}, u32[]{:S(2)}) collective-permute-start(bf16[128,768]{1,0:T(8,128)(2,1)S(1)} %bitcast.20), channel_id=1, source_target_pairs={{0,8},{4,12},{1,9},{5,13},{2,10},{6,14},{3,11},{7,15},{16,24},{20,... | collective-permute-start | bytes 589832 | tf_op jit(solution)/shard_map/ppermute | solution.py:92
  12.1 0.0 collective-permute-done
  12.1 1.1 %fusion = bf16[896,128]{1,0:T(8,128)(2,1)S(1)} fusion(bf16[2,896,128]{2,1,0:T(8,128)(2,1)} %collective-permute-done, bf16[2,896,128]{2,1,0:T(8,128)(2,1)} %get-tuple-element.14), kind=kLoop, calls=%fused_computation.1 | loop fusion | flops 114688 | bytes 688128 | tf_op jit(solution)/shard_map/add | solution.py:67
  13.2 0.7 %collective-permute-start.1 = (bf16[896,128]{1,0:T(8,128)(2,1)S(1)}, bf16[896,128]{1,0:T(8,128)(2,1)S(1)}, u32[]{:S(2)}, u32[]{:S(2)}) collective-permute-start(bf16[896,128]{1,0:T(8,128)(2,1)S(1)} %fusion), channel_id=1, source_target_pairs={{0,2},{1,3},{2,0},{3,1},{4,6},{5,7},{6,4},{7,5},{8,10},{9,11},{10,... | collective-permute-start | bytes 688136 | tf_op jit(solution)/shard_map/ppermute | solution.py:67
  13.8 0.0 collective-permute-done.7
  13.8 1.0 %fusion.3 = bf16[32,2688]{1,0:T(8,128)(2,1)S(1)} fusion(bf16[2,32,2688]{2,1,0:T(8,128)(2,1)S(1)} %collective-permute-done.7, bf16[2,32,2688]{2,1,0:T(8,128)(2,1)} %get-tuple-element.18), kind=kLoop, calls=%fused_computation.6 | loop fusion | flops 86016 | bytes 516096 | tf_op jit(solution)/shard_map/add | solution.py:67
  14.8 1.5 %collective-permute-start.8 = (bf16[32,2688]{1,0:T(8,128)(2,1)S(1)}, bf16[32,2688]{1,0:T(8,128)(2,1)S(1)}, u32[]{:S(2)}, u32[]{:S(2)}) collective-permute-start(bf16[32,2688]{1,0:T(8,128)(2,1)S(1)} %fusion.3), channel_id=1, source_target_pairs={{0,2},{1,3},{2,0},{3,1},{4,6},{5,7},{6,4},{7,5},{8,10},{9,11},{10,... | collective-permute-start | bytes 516104 | tf_op jit(solution)/shard_map/ppermute | solution.py:67
  16.3 5.4 %collective-permute-done.1 = bf16[896,128]{1,0:T(8,128)(2,1)S(1)} collective-permute-done((bf16[896,128]{1,0:T(8,128)(2,1)S(1)}, bf16[896,128]{1,0:T(8,128)(2,1)S(1)}, u32[]{:S(2)}, u32[]{:S(2)}) %collective-permute-start.1) | collective-permute-done | bytes 229408 | tf_op jit(solution)/shard_map/ppermute | solution.py:67
  21.8 1.1 %fusion.2.rest_0_ = bf16[896,128]{1,0:T(8,128)(2,1)S(1)} fusion(bf16[896,128]{1,0:T(8,128)(2,1)S(1)} %collective-permute-done.1, bf16[2,896,128]{2,1,0:T(8,128)(2,1)} %collective-permute-done, bf16[2,896,128]{2,1,0:T(8,128)(2,1)} %get-tuple-element.14), kind=kLoop, calls=%fused_computation.4 | loop fusion | flops 229376 | bytes 917504 | tf_op jit(solution)/shard_map/add | solution.py:68
  22.8 0.0 collective-permute-done.2.rest_1_
  22.9 0.1 collective-permute-start.3
  22.9 4.1 %collective-permute-start.4 = (bf16[896,128]{1,0:T(8,128)(2,1)S(1)}, bf16[896,128]{1,0:T(8,128)(2,1)S(1)}, u32[]{:S(2)}, u32[]{:S(2)}) collective-permute-start(bf16[896,128]{1,0:T(8,128)(2,1)S(1)} %fusion.2.rest_0_), channel_id=1, source_target_pairs={{0,12},{12,0},{4,8},{8,4},{1,13},{13,1},{5,9},{9,5},{2,14},{14,2},... | collective-permute-start | bytes 688136 | tf_op jit(solution)/shard_map/ppermute | solution.py:73
  27.1 0.0 collective-permute-done.8
  27.1 1.0 %fusion.5.rest_4_ = bf16[32,2688]{1,0:T(8,128)(2,1)S(1)} fusion(bf16[32,2688]{1,0:T(8,128)(2,1)S(1)} %collective-permute-done.8, bf16[2,32,2688]{2,1,0:T(8,128)(2,1)S(1)} %collective-permute-done.7, bf16[2,32,2688]{2,1,0:T(8,128)(2,1)} %get-tuple-element.18), kind=kLoop, calls=%fused_computation.9 | loop fusion | flops 172032 | bytes 688128 | tf_op jit(solution)/shard_map/add | solution.py:68
  28.0 0.0 collective-permute-done.10.rest_3_
  28.0 0.0 collective-permute-done.9.rest_2_
  28.1 9.6 %collective-permute-start.11 = (bf16[32,2688]{1,0:T(8,128)(2,1)S(1)}, bf16[32,2688]{1,0:T(8,128)(2,1)S(1)}, u32[]{:S(2)}, u32[]{:S(2)}) collective-permute-start(bf16[32,2688]{1,0:T(8,128)(2,1)S(1)} %fusion.5.rest_4_), channel_id=1, source_target_pairs={{0,4},{4,0},{8,12},{12,8},{1,5},{5,1},{9,13},{13,9},{2,6},{6,2},{1... | collective-permute-start | bytes 516104 | tf_op jit(solution)/shard_map/ppermute | solution.py:72
  37.7 0.0 collective-permute-start.12
  37.7 0.0 collective-permute-done.3.rest_1_
  37.7 3.9 %collective-permute-start.5 = (bf16[896,128]{1,0:T(8,128)(2,1)S(1)}, bf16[896,128]{1,0:T(8,128)(2,1)S(1)}, u32[]{:S(2)}, u32[]{:S(2)}) collective-permute-start(bf16[896,128]{1,0:T(8,128)(2,1)S(1)} %collective-permute-done.3.rest_1_), channel_id=1, source_target_pairs={{4,8},{8,4},{5,9},{9,5},{6,10},{10,6},{7,11},{11,7},{20,24},{24,20... | collective-permute-start | bytes 688136 | tf_op jit(solution)/shard_map/ppermute | solution.py:74
  41.6 3.2 %collective-permute-done.4.rest_2_ = bf16[896,128]{1,0:T(8,128)(2,1)S(1)} collective-permute-done((bf16[896,128]{1,0:T(8,128)(2,1)S(1)}, bf16[896,128]{1,0:T(8,128)(2,1)S(1)}, u32[]{:S(2)}, u32[]{:S(2)}) %collective-permute-start.4) | collective-permute-done | bytes 229408 | tf_op jit(solution)/shard_map/ppermute | solution.py:73
  44.8 1.3 %collective-permute-start.6 = (bf16[896,128]{1,0:T(8,128)(2,1)S(1)}, bf16[896,128]{1,0:T(8,128)(2,1)S(1)}, u32[]{:S(2)}, u32[]{:S(2)}) collective-permute-start(bf16[896,128]{1,0:T(8,128)(2,1)S(1)} %collective-permute-done.4.rest_2_), channel_id=1, source_target_pairs={{4,0},{8,12},{5,1},{9,13},{6,2},{10,14},{7,3},{11,15},{20,16},{24,... | collective-permute-start | bytes 688136 | tf_op jit(solution)/shard_map/ppermute | solution.py:75
  46.1 0.0 collective-permute-done.11.rest_5_
  46.1 1.9 %collective-permute-start.13 = (bf16[32,2688]{1,0:T(8,128)(2,1)S(1)}, bf16[32,2688]{1,0:T(8,128)(2,1)S(1)}, u32[]{:S(2)}, u32[]{:S(2)}) collective-permute-start(bf16[32,2688]{1,0:T(8,128)(2,1)S(1)} %collective-permute-done.11.rest_5_), channel_id=1, source_target_pairs={{4,8},{8,4},{5,9},{9,5},{6,10},{10,6},{7,11},{11,7},{20,24},{24,20... | collective-permute-start | bytes 516104 | tf_op jit(solution)/shard_map/ppermute | solution.py:74
  48.1 0.4 collective-permute-done.12.rest_6_
  48.5 1.3 %collective-permute-start.14 = (bf16[32,2688]{1,0:T(8,128)(2,1)S(1)}, bf16[32,2688]{1,0:T(8,128)(2,1)S(1)}, u32[]{:S(2)}, u32[]{:S(2)}) collective-permute-start(bf16[32,2688]{1,0:T(8,128)(2,1)S(1)} %collective-permute-done.12.rest_6_), channel_id=1, source_target_pairs={{4,0},{8,12},{5,1},{9,13},{6,2},{10,14},{7,3},{11,15},{20,16},{24,... | collective-permute-start | bytes 516104 | tf_op jit(solution)/shard_map/ppermute | solution.py:75
  50.4 3.0 %collective-permute-done.5.rest_3_ = bf16[896,128]{1,0:T(8,128)(2,1)S(1)} collective-permute-done((bf16[896,128]{1,0:T(8,128)(2,1)S(1)}, bf16[896,128]{1,0:T(8,128)(2,1)S(1)}, u32[]{:S(2)}, u32[]{:S(2)}) %collective-permute-start.5) | collective-permute-done | bytes 229408 | tf_op jit(solution)/shard_map/ppermute | solution.py:74
  53.4 0.0 collective-permute-done.6.rest_4_
  53.4 0.0 copy-done
  53.4 0.0 copy-done.1
  53.4 0.0 copy-done.2
  53.4 1.1 %shard_map.92.low = bf16[128,128]{1,0:T(8,128)(2,1)S(1)} custom-call(s32[4]{0:T(128)S(1)} %copy-done.1, s32[64]{0:T(128)S(1)} %copy-done.2, bf16[128,3584]{1,0:T(8,128)(2,1)S(1)} %bitcast.16, bf16[896,128]{1,0:T(8,128)(2,1)S(1)} %fusion.2.rest_0_, bf16[896,128]{1,0:T(8,128)(2,1)S(1)} %collective-permute-done.3.rest_1_, ...), custom_call_target="tpu_custom_call" | custom-call | flops 134217728 | bytes 4194304 | tf_op jit(solution)/shard_map/pallas_call | solution.py:117
  54.5 1.9 %collective-permute-done.13.rest_7_ = bf16[32,2688]{1,0:T(8,128)(2,1)S(1)} collective-permute-done((bf16[32,2688]{1,0:T(8,128)(2,1)S(1)}, bf16[32,2688]{1,0:T(8,128)(2,1)S(1)}, u32[]{:S(2)}, u32[]{:S(2)}) %collective-permute-start.13) | collective-permute-done | bytes 172064 | tf_op jit(solution)/shard_map/ppermute | solution.py:74
  56.5 0.0 collective-permute-done.14.rest_8_
  56.5 0.0 copy-done.3
  56.5 2.8 %shard_map.94 = bf16[128,2688]{1,0:T(8,128)(2,1)} custom-call(s32[1]{0:T(128)S(6)} %copy.10.lengths, bf16[128,2688]{1,0:T(8,128)(2,1)S(1)} %bitcast.17, bf16[128,128]{1,0:T(8,128)(2,1)S(1)} %shard_map.92.low, bf16[128,768]{1,0:T(8,128)(2,1)S(1)} %bitcast.21, bf16[128,768]{1,0:T(8,128)(2,1)S(1)} %collective-permute-done.2.rest_1_, ...), custom_call_target="tpu_custom_call" | custom-call | flops 1073741824 | bytes 4194304 | tf_op jit(solution)/shard_map/pallas_call | solution.py:197
Async XLA Ops:
  0.0 6.0 %copy-start.4 = (bf16[1,128,768]{2,1,0:T(8,128)(2,1)S(1)}, bf16[1,128,768]{2,1,0:T(8,128)(2,1)}, u32[]{:S(2)}) copy-start(bf16[1,128,768]{2,1,0:T(8,128)(2,1)} %param.11) | copy-start | bytes 589828
  2.7 50.7 %copy-start = (bf16[1,128,3584]{2,1,0:T(8,128)(2,1)S(1)}, bf16[1,128,3584]{2,1,0:T(8,128)(2,1)}, u32[]{:S(2)}) copy-start(bf16[1,128,3584]{2,1,0:T(8,128)(2,1)} %param.9) | copy-start | bytes 2752516
  2.7 50.7 %copy-start.1 = (s32[4]{0:T(128)S(1)}, s32[4]{0:T(128)}, u32[]{:S(2)}) copy-start(s32[4]{0:T(128)} %ids.5) | copy-start | bytes 52
  2.7 50.7 %copy-start.2 = (s32[64]{0:T(128)S(1)}, s32[64]{0:T(128)}, u32[]{:S(2)}) copy-start(s32[64]{0:T(128)} %ranks.1) | copy-start | bytes 772
  2.8 53.7 %copy-start.3 = (bf16[1,128,2688]{2,1,0:T(8,128)(2,1)S(1)}, bf16[1,128,2688]{2,1,0:T(8,128)(2,1)}, u32[]{:S(2)}) copy-start(bf16[1,128,2688]{2,1,0:T(8,128)(2,1)} %param.10) | copy-start | bytes 2064388
  2.8 9.3 %collective-permute-start = (bf16[2,896,128]{2,1,0:T(8,128)(2,1)}, bf16[2,896,128]{2,1,0:T(8,128)(2,1)}, u32[]{:S(2)}, u32[]{:S(2)}) collective-permute-start(bf16[2,896,128]{2,1,0:T(8,128)(2,1)} %get-tuple-element.15), channel_id=1, source_target_pairs={{0,1},{1,0},{2,3},{3,2},{4,5},{5,4},{6,7},{7,6},{8,9},{9,8},{10,11... | collective-permute-start | bytes 1376264 | tf_op jit(solution)/shard_map/ppermute | solution.py:66
  5.5 8.3 %collective-permute-start.7 = (bf16[2,32,2688]{2,1,0:T(8,128)(2,1)}, bf16[2,32,2688]{2,1,0:T(8,128)(2,1)S(1)}, u32[]{:S(2)}, u32[]{:S(2)}) collective-permute-start(bf16[2,32,2688]{2,1,0:T(8,128)(2,1)} %get-tuple-element.19), channel_id=1, source_target_pairs={{0,1},{1,0},{2,3},{3,2},{4,5},{5,4},{6,7},{7,6},{8,9},{9,8},{10,11... | collective-permute-start | bytes 1032200 | tf_op jit(solution)/shard_map/ppermute | solution.py:66
  6.0 16.8 %collective-permute-start.2 = (bf16[128,768]{1,0:T(8,128)(2,1)S(1)}, bf16[128,768]{1,0:T(8,128)(2,1)S(1)}, u32[]{:S(2)}, u32[]{:S(2)}) collective-permute-start(bf16[128,768]{1,0:T(8,128)(2,1)S(1)} %bitcast.18), channel_id=1, source_target_pairs={{0,4},{8,12},{1,5},{9,13},{2,6},{10,14},{3,7},{11,15},{16,20},{24,... | collective-permute-start | bytes 589832 | tf_op jit(solution)/shard_map/ppermute | solution.py:91
  9.5 18.5 %collective-permute-start.10 = (bf16[128,768]{1,0:T(8,128)(2,1)S(1)}, bf16[128,768]{1,0:T(8,128)(2,1)S(1)}, u32[]{:S(2)}, u32[]{:S(2)}) collective-permute-start(bf16[128,768]{1,0:T(8,128)(2,1)S(1)} %bitcast.19), channel_id=1, source_target_pairs={{0,12},{4,8},{1,13},{5,9},{2,14},{6,10},{3,15},{7,11},{16,28},{20,... | collective-permute-start | bytes 589832 | tf_op jit(solution)/shard_map/ppermute | solution.py:93
  10.8 17.2 %collective-permute-start.9 = (bf16[128,768]{1,0:T(8,128)(2,1)S(1)}, bf16[128,768]{1,0:T(8,128)(2,1)S(1)}, u32[]{:S(2)}, u32[]{:S(2)}) collective-permute-start(bf16[128,768]{1,0:T(8,128)(2,1)S(1)} %bitcast.20), channel_id=1, source_target_pairs={{0,8},{4,12},{1,9},{5,13},{2,10},{6,14},{3,11},{7,15},{16,24},{20,... | collective-permute-start | bytes 589832 | tf_op jit(solution)/shard_map/ppermute | solution.py:92
  13.2 8.6 %collective-permute-start.1 = (bf16[896,128]{1,0:T(8,128)(2,1)S(1)}, bf16[896,128]{1,0:T(8,128)(2,1)S(1)}, u32[]{:S(2)}, u32[]{:S(2)}) collective-permute-start(bf16[896,128]{1,0:T(8,128)(2,1)S(1)} %fusion), channel_id=1, source_target_pairs={{0,2},{1,3},{2,0},{3,1},{4,6},{5,7},{6,4},{7,5},{8,10},{9,11},{10,... | collective-permute-start | bytes 688136 | tf_op jit(solution)/shard_map/ppermute | solution.py:67
  14.8 12.3 %collective-permute-start.8 = (bf16[32,2688]{1,0:T(8,128)(2,1)S(1)}, bf16[32,2688]{1,0:T(8,128)(2,1)S(1)}, u32[]{:S(2)}, u32[]{:S(2)}) collective-permute-start(bf16[32,2688]{1,0:T(8,128)(2,1)S(1)} %fusion.3), channel_id=1, source_target_pairs={{0,2},{1,3},{2,0},{3,1},{4,6},{5,7},{6,4},{7,5},{8,10},{9,11},{10,... | collective-permute-start | bytes 516104 | tf_op jit(solution)/shard_map/ppermute | solution.py:67
  22.9 14.8 %collective-permute-start.3 = (bf16[896,128]{1,0:T(8,128)(2,1)S(1)}, bf16[896,128]{1,0:T(8,128)(2,1)S(1)}, u32[]{:S(2)}, u32[]{:S(2)}) collective-permute-start(bf16[896,128]{1,0:T(8,128)(2,1)S(1)} %fusion.2.rest_0_), channel_id=1, source_target_pairs={{0,4},{4,0},{8,12},{12,8},{1,5},{5,1},{9,13},{13,9},{2,6},{6,2},{1... | collective-permute-start | bytes 688136 | tf_op jit(solution)/shard_map/ppermute | solution.py:72
  22.9 21.9 %collective-permute-start.4 = (bf16[896,128]{1,0:T(8,128)(2,1)S(1)}, bf16[896,128]{1,0:T(8,128)(2,1)S(1)}, u32[]{:S(2)}, u32[]{:S(2)}) collective-permute-start(bf16[896,128]{1,0:T(8,128)(2,1)S(1)} %fusion.2.rest_0_), channel_id=1, source_target_pairs={{0,12},{12,0},{4,8},{8,4},{1,13},{13,1},{5,9},{9,5},{2,14},{14,2},... | collective-permute-start | bytes 688136 | tf_op jit(solution)/shard_map/ppermute | solution.py:73
  28.1 18.1 %collective-permute-start.11 = (bf16[32,2688]{1,0:T(8,128)(2,1)S(1)}, bf16[32,2688]{1,0:T(8,128)(2,1)S(1)}, u32[]{:S(2)}, u32[]{:S(2)}) collective-permute-start(bf16[32,2688]{1,0:T(8,128)(2,1)S(1)} %fusion.5.rest_4_), channel_id=1, source_target_pairs={{0,4},{4,0},{8,12},{12,8},{1,5},{5,1},{9,13},{13,9},{2,6},{6,2},{1... | collective-permute-start | bytes 516104 | tf_op jit(solution)/shard_map/ppermute | solution.py:72
  37.7 10.8 %collective-permute-start.12 = (bf16[32,2688]{1,0:T(8,128)(2,1)S(1)}, bf16[32,2688]{1,0:T(8,128)(2,1)S(1)}, u32[]{:S(2)}, u32[]{:S(2)}) collective-permute-start(bf16[32,2688]{1,0:T(8,128)(2,1)S(1)} %fusion.5.rest_4_), channel_id=1, source_target_pairs={{0,12},{12,0},{4,8},{8,4},{1,13},{13,1},{5,9},{9,5},{2,14},{14,2},... | collective-permute-start | bytes 516104 | tf_op jit(solution)/shard_map/ppermute | solution.py:73
  37.7 15.7 %collective-permute-start.5 = (bf16[896,128]{1,0:T(8,128)(2,1)S(1)}, bf16[896,128]{1,0:T(8,128)(2,1)S(1)}, u32[]{:S(2)}, u32[]{:S(2)}) collective-permute-start(bf16[896,128]{1,0:T(8,128)(2,1)S(1)} %collective-permute-done.3.rest_1_), channel_id=1, source_target_pairs={{4,8},{8,4},{5,9},{9,5},{6,10},{10,6},{7,11},{11,7},{20,24},{24,20... | collective-permute-start | bytes 688136 | tf_op jit(solution)/shard_map/ppermute | solution.py:74
  44.8 8.6 %collective-permute-start.6 = (bf16[896,128]{1,0:T(8,128)(2,1)S(1)}, bf16[896,128]{1,0:T(8,128)(2,1)S(1)}, u32[]{:S(2)}, u32[]{:S(2)}) collective-permute-start(bf16[896,128]{1,0:T(8,128)(2,1)S(1)} %collective-permute-done.4.rest_2_), channel_id=1, source_target_pairs={{4,0},{8,12},{5,1},{9,13},{6,2},{10,14},{7,3},{11,15},{20,16},{24,... | collective-permute-start | bytes 688136 | tf_op jit(solution)/shard_map/ppermute | solution.py:75
  46.1 10.4 %collective-permute-start.13 = (bf16[32,2688]{1,0:T(8,128)(2,1)S(1)}, bf16[32,2688]{1,0:T(8,128)(2,1)S(1)}, u32[]{:S(2)}, u32[]{:S(2)}) collective-permute-start(bf16[32,2688]{1,0:T(8,128)(2,1)S(1)} %collective-permute-done.11.rest_5_), channel_id=1, source_target_pairs={{4,8},{8,4},{5,9},{9,5},{6,10},{10,6},{7,11},{11,7},{20,24},{24,20... | collective-permute-start | bytes 516104 | tf_op jit(solution)/shard_map/ppermute | solution.py:74
  48.5 8.0 %collective-permute-start.14 = (bf16[32,2688]{1,0:T(8,128)(2,1)S(1)}, bf16[32,2688]{1,0:T(8,128)(2,1)S(1)}, u32[]{:S(2)}, u32[]{:S(2)}) collective-permute-start(bf16[32,2688]{1,0:T(8,128)(2,1)S(1)} %collective-permute-done.12.rest_6_), channel_id=1, source_target_pairs={{4,0},{8,12},{5,1},{9,13},{6,2},{10,14},{7,3},{11,15},{20,16},{24,... | collective-permute-start | bytes 516104 | tf_op jit(solution)/shard_map/ppermute | solution.py:75

commit v3 on v2

--- a/solution.py
+++ b/solution.py
@@ -16,82 +16,61 @@
 HBM = pltpu.HBM
 LOG2E = 1.0 / math.log(2.0)
 PARAMS = pltpu.CompilerParams(vmem_limit_bytes=48 * 1024 * 1024)
-WHOLE = pltpu.CompilerParams(vmem_limit_bytes=62 * 1024 * 1024)
+WHOLE = pltpu.CompilerParams(vmem_limit_bytes=52 * 1024 * 1024)
 
 
 def spec(space):
     return pl.BlockSpec(memory_space=space)
 
 
-def select_kernel(ids, slots, store, keep, give, sems):
-    per_shard = store.shape[0]
+def select_kernel(ids, slots, *rest):
+    stores, outs, sems = rest[:2], rest[2:6], rest[6]
+    per_shard = stores[0].shape[0]
     me = lax.axis_index("req")
     first = me * per_shard
-    targets = [(keep, 0, 0), (keep, 1, 2), (give, 0, 1), (give, 1, 3)]
-    for i, (out, k, flip) in enumerate(targets):
+    copies = []
+    for i, flip in enumerate((0, 2, 1, 3)):
         local = slots[ids[me ^ flip]] - first
         held = (local >= 0) & (local < per_shard)
+        for f, store in enumerate(stores):
+            out = outs[2 * f + i // 2]
+            copies.append((held, local, store, out, i % 2, sems.at[4 * f + i]))
+    for held, local, store, out, k, sem in copies:
 
         @pl.when(held)
         def _():
-            pltpu.make_async_copy(store.at[local], out.at[k], sems.at[i]).start()
+            pltpu.make_async_copy(store.at[local], out.at[k], sem).start()
 
         @pl.when(jnp.logical_not(held))
         def _():
             out[k] = jnp.zeros(out.shape[1:], out.dtype)
 
-    for i, (out, k, flip) in enumerate(targets):
-        local = slots[ids[me ^ flip]] - first
-        held = (local >= 0) & (local < per_shard)
+    for held, local, store, out, k, sem in copies:
 
         @pl.when(held)
         def _():
-            pltpu.make_async_copy(store.at[local], out.at[k], sems.at[i]).wait()
-
-
-def select(ids, slots, store):
-    shape = jax.ShapeDtypeStruct((2, *store.shape[1:]), store.dtype)
+            pltpu.make_async_copy(store.at[local], out.at[k], sem).wait()
+
+
+def select(ids, slots, down, up):
+    shapes = [jax.ShapeDtypeStruct((2, *x.shape[1:]), x.dtype) for x in (down, down, up, up)]
     return pl.pallas_call(
         select_kernel,
-        out_shape=(shape, shape),
-        in_specs=[spec(SMEM), spec(SMEM), spec(HBM)],
-        out_specs=(spec(VMEM), spec(VMEM)),
-        scratch_shapes=[pltpu.SemaphoreType.DMA((4,))],
+        out_shape=shapes,
+        in_specs=[spec(SMEM), spec(SMEM), spec(HBM), spec(HBM)],
+        out_specs=[spec(VMEM)] * 4,
+        scratch_shapes=[pltpu.SemaphoreType.DMA((8,))],
         compiler_params=WHOLE,
-    )(ids, slots, store)
-
-
-def fetch(ids, slots, store):
-    keep, give = select(ids, slots, store)
-    near = lax.ppermute(give, "req", [(i, i ^ 1) for i in range(4)])
-    far = lax.ppermute(keep[1] + near[1], "req", [(i, i ^ 2) for i in range(4)])
-    return keep[0] + near[0] + far
-
-
+    )(ids, slots, down, up)
+
+
+SIBLING = [(0, 1), (1, 0), (2, 3), (3, 2)]
+ACROSS = [(0, 2), (1, 3), (2, 0), (3, 1)]
 def spread(shard):
-    near = lax.ppermute(shard, "ctx", [(0, 1), (1, 0), (2, 3), (3, 2)])
-    cross = lax.ppermute(shard, "ctx", [(0, 3), (3, 0), (1, 2), (2, 1)])
-    inner = lax.ppermute(near, "ctx", [(1, 2), (2, 1)])
-    outer = lax.ppermute(cross, "ctx", [(1, 0), (2, 3)])
-    return [shard, near, cross, inner, outer]
-
-
-def places(z):
-    inner = (z == 1) | (z == 2)
-    return [(z, None), (z ^ 1, None), (z ^ 3, None), (z ^ 2, inner), (z ^ 2, jnp.logical_not(inner))]
-
-
-def when(condition):
-    return (lambda f: f()) if condition is None else pl.when(condition)
-
-
-def spread_up(shard):
-    return [
-        shard,
-        lax.ppermute(shard, "ctx", [(0, 1), (2, 3)]),
-        lax.ppermute(shard, "ctx", [(0, 2), (1, 3)]),
-        lax.ppermute(shard, "ctx", [(0, 3), (1, 2)]),
-    ]
+    near = lax.ppermute(shard, "ctx", [(i, i ^ 1) for i in range(4)])
+    two = lax.ppermute(shard, "ctx", [(i, i ^ 2) for i in range(4)])
+    cross = lax.ppermute(two, "ctx", [(i, i ^ 1) for i in range(4)])
+    return [shard, near, two, cross]
 
 
 def low_rank_kernel(ids, ranks, hidden, *rest):
@@ -99,14 +78,10 @@
     rows = pieces[0].shape[0]
     rank = ranks[ids[lax.axis_index("req")]]
     accum[...] = jnp.zeros_like(accum)
-    for (place, there), piece in zip(places(lax.axis_index("ctx")), pieces):
-
-        @when(there)
-        def _():
-            columns = pl.ds(pl.multiple_of(place * rows, HD), rows)
-            accum[...] += jnp.dot(
-                hidden[:, columns], piece[...], preferred_element_type=jnp.float32
-            )
+    for flip, piece in enumerate(pieces):
+        place = lax.axis_index("ctx") ^ flip
+        columns = pl.ds(pl.multiple_of(place * rows, HD), rows)
+        accum[...] += jnp.dot(hidden[:, columns], piece[...], preferred_element_type=jnp.float32)
 
     column = lax.broadcasted_iota(jnp.int32, accum.shape, 1)
     out[...] = jnp.where(column < rank, accum[...], 0.0).astype(jnp.bfloat16)
@@ -126,8 +101,8 @@
 
 
 def attend_kernel(lengths, base, low, *rest):
-    kvs, ups = rest[:4], rest[4:9]
-    out, upper, queries = rest[9:]
+    kvs, ups = rest[:4], rest[4:8]
+    out, upper, queries = rest[8:]
     tokens = base.shape[0]
     rows = ups[0].shape[0]
     z = lax.axis_index("ctx")
@@ -137,11 +112,8 @@
 
     @pl.when(live)
     def _():
-        for (place, there), piece in zip(places(z), ups):
-
-            @when(there)
-            def _():
-                upper[pl.ds(pl.multiple_of(place * rows, rows), rows), :] = piece[...]
+        for flip, piece in enumerate(ups):
+            upper[pl.ds(pl.multiple_of((z ^ flip) * rows, rows), rows), :] = piece[...]
 
         for j in range(HEADS):
             columns = slice(j * HD, (j + 1) * HD)
@@ -157,7 +129,7 @@
     query_pos = lax.broadcasted_iota(jnp.int32, (tokens, tokens), 0)
     key_pos = lax.broadcasted_iota(jnp.int32, (tokens, tokens), 1)
     causal = key_pos <= query_pos
-    for mine, needed in enumerate(((0,), (0, 1), (0, 3, 2), (0, 1, 2, 3))):
+    for mine, needed in enumerate(((0,), (0, 1), (0, 2, 3), (0, 1, 2, 3))):
 
         @pl.when(live & (z == mine))
         def _():
@@ -221,12 +193,20 @@
     rank_buckets,
     lengths,
 ):
-    kvs = spread_up(kv_base[0])
-    down = fetch(adapter_ids, adapter_slots, adapter_down)
+    keep_down, give_down, keep_up, give_up = select(
+        adapter_ids, adapter_slots, adapter_down, adapter_up
+    )
+    near_down = lax.ppermute(give_down, "req", SIBLING)
+    near_up = lax.ppermute(give_up, "req", SIBLING)
+    far_down = lax.ppermute(keep_down[1] + near_down[1], "req", ACROSS)
+    pass_up, kv = lax.optimization_barrier((keep_up[1] + near_up[1], kv_base[0]))
+    far_up = lax.ppermute(pass_up, "req", ACROSS)
+    kvs = spread(kv)
+    down = keep_down[0] + near_down[0] + far_down
     down, kvs[1] = lax.optimization_barrier((down, kvs[1]))
     downs = spread(down)
-    up = fetch(adapter_ids, adapter_slots, adapter_up)
-    up, kvs[2], kvs[3] = lax.optimization_barrier((up, kvs[2], kvs[3]))
+    up = keep_up[0] + near_up[0] + far_up
+    up, kvs[2] = lax.optimization_barrier((up, kvs[2]))
     ups = spread(up)
     low = low_rank(adapter_ids, rank_buckets, hidden_states[0], downs)
     return attend(lengths, queries_base[0], low, kvs, ups)[None]

time: 60.2 us -> 58.6 us (0.973)
  the two profiles are of different devices: /device:TPU:18 before, /device:TPU:0 now
where the time goes in v3:
time: 58.6 us; the launch traced here: 58.3 us
  waiting for transfers between devices  35.6 us (61%)
  starting transfers between devices  15.4 us (26%)
  Pallas kernels  5.02 us (9%)
  local copies, waits for them, and re-layouts  1.41 us (2%)
  between operations  0.71 us (1%)
    ppermute x3, waiting for transfers between devices, spread(): two = lax.ppermute(shard, 'ctx', [(i, i ^ 2) for i in range(4)])  12.9 us
    ppermute x3, waiting for transfers between devices, spread(): near = lax.ppermute(shard, 'ctx', [(i, i ^ 1) for i in range(4)])  12.6 us
    ppermute x3, waiting for transfers between devices, spread(): cross = lax.ppermute(two, 'ctx', [(i, i ^ 1) for i in range(4)])  7.69 us
    ppermute x3, starting transfers between devices, spread(): near = lax.ppermute(shard, 'ctx', [(i, i ^ 1) for i in range(4)])  5.8 us
    ppermute x3, starting transfers between devices, spread(): two = lax.ppermute(shard, 'ctx', [(i, i ^ 2) for i in range(4)])  3.15 us
    ppermute x1, starting transfers between devices, body(): far_down = lax.ppermute(keep_down[1] + near_down[1], 'req', ACROSS)  2.84 us
    ppermute x3, starting transfers between devices, spread(): cross = lax.ppermute(two, 'ctx', [(i, i ^ 1) for i in range(4)])  2.44 us
    pallas_call x1, Pallas kernels, attend(): pl.pallas_call(attend_kernel, out_shape=jax.ShapeDtypeStruct(base.shape,...  2.33 us
  transfers between devices with their start and end apart: 13, of which 10 were waited for; matrix products, arithmetic and copies ran while one was open for 0% of the time, Pallas kernels for 2%

profile of v3, /device:TPU:0, one launch (start us, length us, event | category | flops | bytes accessed | tf_op | source)
XLA Modules:
  0.0 58.3 jit_solution(12927005819914919500)
XLA Ops:
  0.0 0.0 copy-start
  0.0 0.0 copy-start.1
  0.0 0.7 %copy-done.1 = s32[4]{0:T(128)S(1)} copy-done((s32[4]{0:T(128)S(1)}, s32[4]{0:T(128)}, u32[]{:S(2)}) %copy-start.1) | copy-done | bytes 40
  0.7 0.0 copy-start.3
  0.7 0.7 %copy-done.3 = s32[64]{0:T(128)S(1)} copy-done((s32[64]{0:T(128)S(1)}, s32[64]{0:T(128)}, u32[]{:S(2)}) %copy-start.3) | copy-done | bytes 280
  1.4 0.0 copy-start.5
  1.4 0.0 copy-start.2
  1.4 1.7 %shard_map.91 = (bf16[2,896,128]{2,1,0:T(8,128)(2,1)S(1)}, bf16[2,896,128]{2,1,0:T(8,128)(2,1)S(1)}, bf16[2,32,2688]{2,1,0:T(8,128)(2,1)S(1)}, bf16[2,32,2688]{2,1,0:T(8,128)(2,1)S(1)}) custom-call(s32[4]{0:T(128)S(1)} %copy-done.1, s32[64]{0:T(128)S(1)} %copy-done.3, bf16[16,896,128]{2,1,0:T(8,128)(2,1)} %rest_0_.1, bf16[16,32,2688]{2,1,0:T(8,128)(2,1)} %rest_1_.1), custom_call_target="tpu_custom_call" | custom-call | tf_op jit(solution)/shard_map/pallas_call | solution.py:57
  3.2 0.0 copy-start.4
  3.2 0.5 collective-permute-start
  3.7 0.1 collective-permute-start.2
  3.8 1.4 %collective-permute-done = bf16[2,896,128]{2,1,0:T(8,128)(2,1)S(1)} collective-permute-done((bf16[2,896,128]{2,1,0:T(8,128)(2,1)S(1)}, bf16[2,896,128]{2,1,0:T(8,128)(2,1)S(1)}, u32[]{:S(2)}, u32[]{:S(2)}) %collective-permute-start) | collective-permute-done | bytes 458784 | tf_op jit(solution)/shard_map/ppermute | solution.py:199
  5.2 2.8 %collective-permute-start.1 = (bf16[896,128]{1,0:T(8,128)(2,1)S(1)}, bf16[896,128]{1,0:T(8,128)(2,1)S(1)}, u32[]{:S(2)}, u32[]{:S(2)}) collective-permute-start(bf16[896,128]{1,0:T(8,128)(2,1)S(1)} %fusion), channel_id=1, source_target_pairs={{0,2},{1,3},{2,0},{3,1},{4,6},{5,7},{6,4},{7,5},{8,10},{9,11},{10,... | collective-permute-start | bytes 688136 | tf_op jit(solution)/shard_map/ppermute | solution.py:201
  8.0 0.0 collective-permute-done.2
  8.0 0.0 copy-done.5
  8.0 1.6 %collective-permute-start.3 = (bf16[128,768]{1,0:T(8,128)(2,1)S(1)}, bf16[128,768]{1,0:T(8,128)(2,1)S(1)}, u32[]{:S(2)}, u32[]{:S(2)}) collective-permute-start(bf16[128,768]{1,0:T(8,128)(2,1)S(1)} %bitcast.18), channel_id=1, source_target_pairs={{0,4},{4,0},{8,12},{12,8},{1,5},{5,1},{9,13},{13,9},{2,6},{6,2},{1... | collective-permute-start | bytes 589832 | tf_op jit(solution)/shard_map/ppermute | solution.py:70
  9.7 2.6 %collective-permute-start.8 = (bf16[128,768]{1,0:T(8,128)(2,1)S(1)}, bf16[128,768]{1,0:T(8,128)(2,1)S(1)}, u32[]{:S(2)}, u32[]{:S(2)}) collective-permute-start(bf16[128,768]{1,0:T(8,128)(2,1)S(1)} %bitcast.19), channel_id=1, source_target_pairs={{0,8},{4,12},{8,0},{12,4},{1,9},{5,13},{9,1},{13,5},{2,10},{6,14},... | collective-permute-start | bytes 589832 | tf_op jit(solution)/shard_map/ppermute | solution.py:71
  12.3 0.6 %collective-permute-start.7 = (bf16[32,2688]{1,0:T(8,128)(2,1)S(1)}, bf16[32,2688]{1,0:T(8,128)(2,1)S(1)}, u32[]{:S(2)}, u32[]{:S(2)}) collective-permute-start(bf16[32,2688]{1,0:T(8,128)(2,1)S(1)} %fusion.5), channel_id=1, source_target_pairs={{0,2},{1,3},{2,0},{3,1},{4,6},{5,7},{6,4},{7,5},{8,10},{9,11},{10,... | collective-permute-start | bytes 516104 | tf_op jit(solution)/shard_map/ppermute | solution.py:203
  12.9 1.1 %collective-permute-done.1 = bf16[896,128]{1,0:T(8,128)(2,1)S(1)} collective-permute-done((bf16[896,128]{1,0:T(8,128)(2,1)S(1)}, bf16[896,128]{1,0:T(8,128)(2,1)S(1)}, u32[]{:S(2)}, u32[]{:S(2)}) %collective-permute-start.1) | collective-permute-done | bytes 229408 | tf_op jit(solution)/shard_map/ppermute | solution.py:201
  14.0 4.9 %collective-permute-done.3.rest_1_ = bf16[128,768]{1,0:T(8,128)(2,1)S(1)} collective-permute-done((bf16[128,768]{1,0:T(8,128)(2,1)S(1)}, bf16[128,768]{1,0:T(8,128)(2,1)S(1)}, u32[]{:S(2)}, u32[]{:S(2)}) %collective-permute-start.3) | collective-permute-done | bytes 196640 | tf_op jit(solution)/shard_map/ppermute | solution.py:70
  18.9 0.6 collective-permute-start.5
  19.4 0.0 collective-permute-done.7
  19.5 8.6 %collective-permute-done.8.rest_2_ = bf16[128,768]{1,0:T(8,128)(2,1)S(1)} collective-permute-done((bf16[128,768]{1,0:T(8,128)(2,1)S(1)}, bf16[128,768]{1,0:T(8,128)(2,1)S(1)}, u32[]{:S(2)}, u32[]{:S(2)}) %collective-permute-start.8) | collective-permute-done | bytes 196640 | tf_op jit(solution)/shard_map/ppermute | solution.py:71
  28.0 0.0 collective-permute-start.11
  28.0 3.8 %collective-permute-start.4 = (bf16[896,128]{1,0:T(8,128)(2,1)S(1)}, bf16[896,128]{1,0:T(8,128)(2,1)S(1)}, u32[]{:S(2)}, u32[]{:S(2)}) collective-permute-start(bf16[896,128]{1,0:T(8,128)(2,1)S(1)} %fusion.2.rest_0_), channel_id=1, source_target_pairs={{0,4},{4,0},{8,12},{12,8},{1,5},{5,1},{9,13},{13,9},{2,6},{6,2},{1... | collective-permute-start | bytes 688136 | tf_op jit(solution)/shard_map/ppermute | solution.py:70
  31.8 3.1 %collective-permute-done.5.rest_2_ = bf16[896,128]{1,0:T(8,128)(2,1)S(1)} collective-permute-done((bf16[896,128]{1,0:T(8,128)(2,1)S(1)}, bf16[896,128]{1,0:T(8,128)(2,1)S(1)}, u32[]{:S(2)}, u32[]{:S(2)}) %collective-permute-start.5) | collective-permute-done | bytes 229408 | tf_op jit(solution)/shard_map/ppermute | solution.py:71
  34.9 0.4 collective-permute-start.6
  35.3 1.7 %collective-permute-start.9 = (bf16[128,768]{1,0:T(8,128)(2,1)S(1)}, bf16[128,768]{1,0:T(8,128)(2,1)S(1)}, u32[]{:S(2)}, u32[]{:S(2)}) collective-permute-start(bf16[128,768]{1,0:T(8,128)(2,1)S(1)} %collective-permute-done.8.rest_2_), channel_id=1, source_target_pairs={{0,4},{4,0},{8,12},{12,8},{1,5},{5,1},{9,13},{13,9},{2,6},{6,2},{1... | collective-permute-start | bytes 589832 | tf_op jit(solution)/shard_map/ppermute | solution.py:72
  36.9 0.4 collective-permute-start.10
  37.3 1.3 %collective-permute-done.11.rest_6_ = bf16[32,2688]{1,0:T(8,128)(2,1)S(1)} collective-permute-done((bf16[32,2688]{1,0:T(8,128)(2,1)S(1)}, bf16[32,2688]{1,0:T(8,128)(2,1)S(1)}, u32[]{:S(2)}, u32[]{:S(2)}) %collective-permute-start.11) | collective-permute-done | bytes 172064 | tf_op jit(solution)/shard_map/ppermute | solution.py:71
  38.5 0.4 collective-permute-start.12
  39.6 0.8 %collective-permute-done.4.rest_1_ = bf16[896,128]{1,0:T(8,128)(2,1)S(1)} collective-permute-done((bf16[896,128]{1,0:T(8,128)(2,1)S(1)}, bf16[896,128]{1,0:T(8,128)(2,1)S(1)}, u32[]{:S(2)}, u32[]{:S(2)}) %collective-permute-start.4) | collective-permute-done | bytes 229408 | tf_op jit(solution)/shard_map/ppermute | solution.py:70
  40.4 4.9 %collective-permute-done.6.rest_3_ = bf16[896,128]{1,0:T(8,128)(2,1)S(1)} collective-permute-done((bf16[896,128]{1,0:T(8,128)(2,1)S(1)}, bf16[896,128]{1,0:T(8,128)(2,1)S(1)}, u32[]{:S(2)}, u32[]{:S(2)}) %collective-permute-start.6) | collective-permute-done | bytes 229408 | tf_op jit(solution)/shard_map/ppermute | solution.py:72
  45.3 0.0 copy-done
  45.3 0.0 copy-done.2
  45.3 0.9 %shard_map.92.low = bf16[128,128]{1,0:T(8,128)(2,1)S(1)} custom-call(s32[4]{0:T(128)S(1)} %copy-done.1, s32[64]{0:T(128)S(1)} %copy-done.2, bf16[128,3584]{1,0:T(8,128)(2,1)S(1)} %bitcast.16, bf16[896,128]{1,0:T(8,128)(2,1)S(1)} %fusion.2.rest_0_, bf16[896,128]{1,0:T(8,128)(2,1)S(1)} %collective-permute-done.4.rest_1_, ...), custom_call_target="tpu_custom_call" | custom-call | flops 134217728 | bytes 4194304 | tf_op jit(solution)/shard_map/pallas_call | solution.py:92
  46.3 6.9 %collective-permute-done.10.rest_5_ = bf16[32,2688]{1,0:T(8,128)(2,1)S(1)} collective-permute-done((bf16[32,2688]{1,0:T(8,128)(2,1)S(1)}, bf16[32,2688]{1,0:T(8,128)(2,1)S(1)}, u32[]{:S(2)}, u32[]{:S(2)}) %collective-permute-start.10) | collective-permute-done | bytes 172064 | tf_op jit(solution)/shard_map/ppermute | solution.py:70
  53.2 0.0 collective-permute-done.9.rest_3_
  53.2 2.8 %collective-permute-done.12.rest_7_ = bf16[32,2688]{1,0:T(8,128)(2,1)S(1)} collective-permute-done((bf16[32,2688]{1,0:T(8,128)(2,1)S(1)}, bf16[32,2688]{1,0:T(8,128)(2,1)S(1)}, u32[]{:S(2)}, u32[]{:S(2)}) %collective-permute-start.12) | collective-permute-done | bytes 172064 | tf_op jit(solution)/shard_map/ppermute | solution.py:72
  56.0 0.0 copy-done.4
  56.0 2.3 %shard_map.93 = bf16[128,2688]{1,0:T(8,128)(2,1)} custom-call(s32[1]{0:T(128)S(6)} %copy.10.lengths, bf16[128,2688]{1,0:T(8,128)(2,1)S(1)} %bitcast.17, bf16[128,128]{1,0:T(8,128)(2,1)S(1)} %shard_map.92.low, bf16[128,768]{1,0:T(8,128)(2,1)S(1)} %bitcast.20, bf16[128,768]{1,0:T(8,128)(2,1)S(1)} %collective-permute-done.3.rest_1_, ...), custom_call_target="tpu_custom_call" | custom-call | flops 1073741824 | bytes 4194304 | tf_op jit(solution)/shard_map/pallas_call | solution.py:169
  (4 shorter events, 0.1 us)
Async XLA Ops:
  0.0 45.3 %copy-start = (bf16[1,128,3584]{2,1,0:T(8,128)(2,1)S(1)}, bf16[1,128,3584]{2,1,0:T(8,128)(2,1)}, u32[]{:S(2)}) copy-start(bf16[1,128,3584]{2,1,0:T(8,128)(2,1)} %param.9) | copy-start | bytes 2752516
  0.0 0.7 %copy-start.1 = (s32[4]{0:T(128)S(1)}, s32[4]{0:T(128)}, u32[]{:S(2)}) copy-start(s32[4]{0:T(128)} %ids.3) | copy-start | bytes 52
  0.7 0.7 %copy-start.3 = (s32[64]{0:T(128)S(1)}, s32[64]{0:T(128)}, u32[]{:S(2)}) copy-start(s32[64]{0:T(128)} %slots.1) | copy-start | bytes 772
  1.4 6.6 %copy-start.5 = (bf16[1,128,768]{2,1,0:T(8,128)(2,1)S(1)}, bf16[1,128,768]{2,1,0:T(8,128)(2,1)}, u32[]{:S(2)}) copy-start(bf16[1,128,768]{2,1,0:T(8,128)(2,1)} %param.11) | copy-start | bytes 589828
  1.4 43.9 %copy-start.2 = (s32[64]{0:T(128)S(1)}, s32[64]{0:T(128)}, u32[]{:S(2)}) copy-start(s32[64]{0:T(128)} %ranks.1) | copy-start | bytes 772
  3.2 52.9 %copy-start.4 = (bf16[1,128,2688]{2,1,0:T(8,128)(2,1)S(1)}, bf16[1,128,2688]{2,1,0:T(8,128)(2,1)}, u32[]{:S(2)}) copy-start(bf16[1,128,2688]{2,1,0:T(8,128)(2,1)} %param.10) | copy-start | bytes 2064388
  3.2 2.0 %collective-permute-start = (bf16[2,896,128]{2,1,0:T(8,128)(2,1)S(1)}, bf16[2,896,128]{2,1,0:T(8,128)(2,1)S(1)}, u32[]{:S(2)}, u32[]{:S(2)}) collective-permute-start(bf16[2,896,128]{2,1,0:T(8,128)(2,1)S(1)} %get-tuple-element.16), channel_id=1, source_target_pairs={{0,1},{1,0},{2,3},{3,2},{4,5},{5,4},{6,7},{7,6},{8,9},{9,8},{10,11... | collective-permute-start | bytes 1376264 | tf_op jit(solution)/shard_map/ppermute | solution.py:199
  3.7 4.3 %collective-permute-start.2 = (bf16[2,32,2688]{2,1,0:T(8,128)(2,1)S(1)}, bf16[2,32,2688]{2,1,0:T(8,128)(2,1)S(1)}, u32[]{:S(2)}, u32[]{:S(2)}) collective-permute-start(bf16[2,32,2688]{2,1,0:T(8,128)(2,1)S(1)} %get-tuple-element.18), channel_id=1, source_target_pairs={{0,1},{1,0},{2,3},{3,2},{4,5},{5,4},{6,7},{7,6},{8,9},{9,8},{10,11... | collective-permute-start | bytes 1032200 | tf_op jit(solution)/shard_map/ppermute | solution.py:200
  5.2 8.8 %collective-permute-start.1 = (bf16[896,128]{1,0:T(8,128)(2,1)S(1)}, bf16[896,128]{1,0:T(8,128)(2,1)S(1)}, u32[]{:S(2)}, u32[]{:S(2)}) collective-permute-start(bf16[896,128]{1,0:T(8,128)(2,1)S(1)} %fusion), channel_id=1, source_target_pairs={{0,2},{1,3},{2,0},{3,1},{4,6},{5,7},{6,4},{7,5},{8,10},{9,11},{10,... | collective-permute-start | bytes 688136 | tf_op jit(solution)/shard_map/ppermute | solution.py:201
  8.0 10.8 %collective-permute-start.3 = (bf16[128,768]{1,0:T(8,128)(2,1)S(1)}, bf16[128,768]{1,0:T(8,128)(2,1)S(1)}, u32[]{:S(2)}, u32[]{:S(2)}) collective-permute-start(bf16[128,768]{1,0:T(8,128)(2,1)S(1)} %bitcast.18), channel_id=1, source_target_pairs={{0,4},{4,0},{8,12},{12,8},{1,5},{5,1},{9,13},{13,9},{2,6},{6,2},{1... | collective-permute-start | bytes 589832 | tf_op jit(solution)/shard_map/ppermute | solution.py:70
  9.7 18.4 %collective-permute-start.8 = (bf16[128,768]{1,0:T(8,128)(2,1)S(1)}, bf16[128,768]{1,0:T(8,128)(2,1)S(1)}, u32[]{:S(2)}, u32[]{:S(2)}) collective-permute-start(bf16[128,768]{1,0:T(8,128)(2,1)S(1)} %bitcast.19), channel_id=1, source_target_pairs={{0,8},{4,12},{8,0},{12,4},{1,9},{5,13},{9,1},{13,5},{2,10},{6,14},... | collective-permute-start | bytes 589832 | tf_op jit(solution)/shard_map/ppermute | solution.py:71
  12.3 7.2 %collective-permute-start.7 = (bf16[32,2688]{1,0:T(8,128)(2,1)S(1)}, bf16[32,2688]{1,0:T(8,128)(2,1)S(1)}, u32[]{:S(2)}, u32[]{:S(2)}) collective-permute-start(bf16[32,2688]{1,0:T(8,128)(2,1)S(1)} %fusion.5), channel_id=1, source_target_pairs={{0,2},{1,3},{2,0},{3,1},{4,6},{5,7},{6,4},{7,5},{8,10},{9,11},{10,... | collective-permute-start | bytes 516104 | tf_op jit(solution)/shard_map/ppermute | solution.py:203
  18.9 16.0 %collective-permute-start.5 = (bf16[896,128]{1,0:T(8,128)(2,1)S(1)}, bf16[896,128]{1,0:T(8,128)(2,1)S(1)}, u32[]{:S(2)}, u32[]{:S(2)}) collective-permute-start(bf16[896,128]{1,0:T(8,128)(2,1)S(1)} %fusion.2.rest_0_), channel_id=1, source_target_pairs={{0,8},{4,12},{8,0},{12,4},{1,9},{5,13},{9,1},{13,5},{2,10},{6,14},... | collective-permute-start | bytes 688136 | tf_op jit(solution)/shard_map/ppermute | solution.py:71
  28.0 10.5 %collective-permute-start.11 = (bf16[32,2688]{1,0:T(8,128)(2,1)S(1)}, bf16[32,2688]{1,0:T(8,128)(2,1)S(1)}, u32[]{:S(2)}, u32[]{:S(2)}) collective-permute-start(bf16[32,2688]{1,0:T(8,128)(2,1)S(1)} %fusion.4.rest_4_), channel_id=1, source_target_pairs={{0,8},{4,12},{8,0},{12,4},{1,9},{5,13},{9,1},{13,5},{2,10},{6,14},... | collective-permute-start | bytes 516104 | tf_op jit(solution)/shard_map/ppermute | solution.py:71
  28.0 12.4 %collective-permute-start.4 = (bf16[896,128]{1,0:T(8,128)(2,1)S(1)}, bf16[896,128]{1,0:T(8,128)(2,1)S(1)}, u32[]{:S(2)}, u32[]{:S(2)}) collective-permute-start(bf16[896,128]{1,0:T(8,128)(2,1)S(1)} %fusion.2.rest_0_), channel_id=1, source_target_pairs={{0,4},{4,0},{8,12},{12,8},{1,5},{5,1},{9,13},{13,9},{2,6},{6,2},{1... | collective-permute-start | bytes 688136 | tf_op jit(solution)/shard_map/ppermute | solution.py:70
  34.9 10.4 %collective-permute-start.6 = (bf16[896,128]{1,0:T(8,128)(2,1)S(1)}, bf16[896,128]{1,0:T(8,128)(2,1)S(1)}, u32[]{:S(2)}, u32[]{:S(2)}) collective-permute-start(bf16[896,128]{1,0:T(8,128)(2,1)S(1)} %collective-permute-done.5.rest_2_), channel_id=1, source_target_pairs={{0,4},{4,0},{8,12},{12,8},{1,5},{5,1},{9,13},{13,9},{2,6},{6,2},{1... | collective-permute-start | bytes 688136 | tf_op jit(solution)/shard_map/ppermute | solution.py:72
  35.3 18.0 %collective-permute-start.9 = (bf16[128,768]{1,0:T(8,128)(2,1)S(1)}, bf16[128,768]{1,0:T(8,128)(2,1)S(1)}, u32[]{:S(2)}, u32[]{:S(2)}) collective-permute-start(bf16[128,768]{1,0:T(8,128)(2,1)S(1)} %collective-permute-done.8.rest_2_), channel_id=1, source_target_pairs={{0,4},{4,0},{8,12},{12,8},{1,5},{5,1},{9,13},{13,9},{2,6},{6,2},{1... | collective-permute-start | bytes 589832 | tf_op jit(solution)/shard_map/ppermute | solution.py:72
  36.9 16.3 %collective-permute-start.10 = (bf16[32,2688]{1,0:T(8,128)(2,1)S(1)}, bf16[32,2688]{1,0:T(8,128)(2,1)S(1)}, u32[]{:S(2)}, u32[]{:S(2)}) collective-permute-start(bf16[32,2688]{1,0:T(8,128)(2,1)S(1)} %fusion.4.rest_4_), channel_id=1, source_target_pairs={{0,4},{4,0},{8,12},{12,8},{1,5},{5,1},{9,13},{13,9},{2,6},{6,2},{1... | collective-permute-start | bytes 516104 | tf_op jit(solution)/shard_map/ppermute | solution.py:70
  38.5 17.5 %collective-permute-start.12 = (bf16[32,2688]{1,0:T(8,128)(2,1)S(1)}, bf16[32,2688]{1,0:T(8,128)(2,1)S(1)}, u32[]{:S(2)}, u32[]{:S(2)}) collective-permute-start(bf16[32,2688]{1,0:T(8,128)(2,1)S(1)} %collective-permute-done.11.rest_6_), channel_id=1, source_target_pairs={{0,4},{4,0},{8,12},{12,8},{1,5},{5,1},{9,13},{13,9},{2,6},{6,2},{1... | collective-permute-start | bytes 516104 | tf_op jit(solution)/shard_map/ppermute | solution.py:72

commit v4 on v3

--- a/solution.py
+++ b/solution.py
@@ -199,14 +199,14 @@
     near_down = lax.ppermute(give_down, "req", SIBLING)
     near_up = lax.ppermute(give_up, "req", SIBLING)
     far_down = lax.ppermute(keep_down[1] + near_down[1], "req", ACROSS)
-    pass_up, kv = lax.optimization_barrier((keep_up[1] + near_up[1], kv_base[0]))
+    pass_up = keep_up[1] + near_up[1]
     far_up = lax.ppermute(pass_up, "req", ACROSS)
-    kvs = spread(kv)
+    kvs = spread(kv_base[0])
     down = keep_down[0] + near_down[0] + far_down
     down, kvs[1] = lax.optimization_barrier((down, kvs[1]))
     downs = spread(down)
     up = keep_up[0] + near_up[0] + far_up
-    up, kvs[2] = lax.optimization_barrier((up, kvs[2]))
+    up, downs[1] = lax.optimization_barrier((up, downs[1]))
     ups = spread(up)
     low = low_rank(adapter_ids, rank_buckets, hidden_states[0], downs)
     return attend(lengths, queries_base[0], low, kvs, ups)[None]

time: 58.6 us -> 52.3 us (0.89)
  waiting for transfers between devices: 35.6 us -> 31.7 us
  starting transfers between devices: 15.4 us -> 13.2 us
    ppermute x3, waiting for transfers between devices: 12.9 us -> 5.96 us  [spread(): two = lax.ppermute(shard, 'ctx', [(i, i ^ 2) for i in range(4)])]
    ppermute x1, waiting for transfers between devices: 1.07 us -> 6.41 us  [body(): far_down = lax.ppermute(keep_down[1] + near_down[1], 'req', ACROSS)]
    ppermute x3, waiting for transfers between devices: 12.6 us -> 10.3 us  [spread(): near = lax.ppermute(shard, 'ctx', [(i, i ^ 1) for i in range(4)])]
    ppermute x1, starting transfers between devices: 2.84 us -> 0.51 us  [body(): far_down = lax.ppermute(keep_down[1] + near_down[1], 'req', ACROSS)]
    ppermute x1, waiting for transfers between devices: 1.36 us -> 0.01 us  [body(): near_down = lax.ppermute(give_down, 'req', SIBLING)]
    ppermute x3, starting transfers between devices: 5.8 us -> 4.55 us  [spread(): near = lax.ppermute(shard, 'ctx', [(i, i ^ 1) for i in range(4)])]
    ppermute x1, starting transfers between devices: 0.62 us -> 1.65 us  [body(): far_up = lax.ppermute(pass_up, 'req', ACROSS)]
    ppermute x1, waiting for transfers between devices: 0.01 us -> 0.85 us  [body(): far_up = lax.ppermute(pass_up, 'req', ACROSS)]
  transfers between devices with their start and end apart: 13 -> 13, of which waited for: 10 -> 9; matrix products, arithmetic and copies ran while one was open for 0% -> 0% of each run, Pallas kernels for 2% -> 2%
where the time goes in v4:
time: 52.3 us; the launch traced here: 52.2 us
  waiting for transfers between devices  31.7 us (61%)
  starting transfers between devices  13.2 us (25%)
  Pallas kernels  5.14 us (10%)
  local copies, waits for them, and re-layouts  1.41 us (3%)
  between operations  0.72 us (1%)
    ppermute x3, waiting for transfers between devices, spread(): near = lax.ppermute(shard, 'ctx', [(i, i ^ 1) for i in range(4)])  10.3 us
    ppermute x3, waiting for transfers between devices, spread(): cross = lax.ppermute(two, 'ctx', [(i, i ^ 1) for i in range(4)])  8.16 us
    ppermute x1, waiting for transfers between devices, body(): far_down = lax.ppermute(keep_down[1] + near_down[1], 'req', ACROSS)  6.41 us
    ppermute x3, waiting for transfers between devices, spread(): two = lax.ppermute(shard, 'ctx', [(i, i ^ 2) for i in range(4)])  5.96 us
    ppermute x3, starting transfers between devices, spread(): near = lax.ppermute(shard, 'ctx', [(i, i ^ 1) for i in range(4)])  4.55 us
    ppermute x3, starting transfers between devices, spread(): two = lax.ppermute(shard, 'ctx', [(i, i ^ 2) for i in range(4)])  3.88 us
    pallas_call x1, Pallas kernels, attend(): pl.pallas_call(attend_kernel, out_shape=jax.ShapeDtypeStruct(base.shape,...  2.33 us
    ppermute x3, starting transfers between devices, spread(): cross = lax.ppermute(two, 'ctx', [(i, i ^ 1) for i in range(4)])  2.03 us
  transfers between devices with their start and end apart: 13, of which 9 were waited for; matrix products, arithmetic and copies ran while one was open for 0% of the time, Pallas kernels for 2%

profile of v4, /device:TPU:0, one launch (start us, length us, event | category | flops | bytes accessed | tf_op | source)
XLA Modules:
  0.0 52.2 jit_solution(8998051055339789119)
XLA Ops:
  0.0 0.0 copy-start
  0.0 0.0 copy-start.1
  0.0 0.7 %copy-done.1 = s32[4]{0:T(128)S(1)} copy-done((s32[4]{0:T(128)S(1)}, s32[4]{0:T(128)}, u32[]{:S(2)}) %copy-start.1) | copy-done | bytes 40
  0.7 0.0 copy-start.3
  0.7 0.7 %copy-done.3 = s32[64]{0:T(128)S(1)} copy-done((s32[64]{0:T(128)S(1)}, s32[64]{0:T(128)}, u32[]{:S(2)}) %copy-start.3) | copy-done | bytes 280
  1.4 0.0 copy-start.5
  1.4 0.0 copy-start.2
  1.4 1.9 %shard_map.91 = (bf16[2,896,128]{2,1,0:T(8,128)(2,1)S(1)}, bf16[2,896,128]{2,1,0:T(8,128)(2,1)S(1)}, bf16[2,32,2688]{2,1,0:T(8,128)(2,1)S(1)}, bf16[2,32,2688]{2,1,0:T(8,128)(2,1)S(1)}) custom-call(s32[4]{0:T(128)S(1)} %copy-done.1, s32[64]{0:T(128)S(1)} %copy-done.3, bf16[16,896,128]{2,1,0:T(8,128)(2,1)} %rest_0_.1, bf16[16,32,2688]{2,1,0:T(8,128)(2,1)} %rest_1_.1), custom_call_target="tpu_custom_call" | custom-call | tf_op jit(solution)/shard_map/pallas_call | solution.py:57
  3.3 0.0 copy-start.4
  3.3 0.5 collective-permute-start
  3.8 0.1 collective-permute-start.3
  3.9 0.0 copy-done.5
  3.9 3.0 %collective-permute-start.2 = (bf16[128,768]{1,0:T(8,128)(2,1)S(1)}, bf16[128,768]{1,0:T(8,128)(2,1)S(1)}, u32[]{:S(2)}, u32[]{:S(2)}) collective-permute-start(bf16[128,768]{1,0:T(8,128)(2,1)S(1)} %bitcast.18), channel_id=1, source_target_pairs={{0,4},{4,0},{8,12},{12,8},{1,5},{5,1},{9,13},{13,9},{2,6},{6,2},{1... | collective-permute-start | bytes 589832 | tf_op jit(solution)/shard_map/ppermute | solution.py:70
  6.9 2.6 %collective-permute-start.8 = (bf16[128,768]{1,0:T(8,128)(2,1)S(1)}, bf16[128,768]{1,0:T(8,128)(2,1)S(1)}, u32[]{:S(2)}, u32[]{:S(2)}) collective-permute-start(bf16[128,768]{1,0:T(8,128)(2,1)S(1)} %bitcast.19), channel_id=1, source_target_pairs={{0,8},{4,12},{8,0},{12,4},{1,9},{5,13},{9,1},{13,5},{2,10},{6,14},... | collective-permute-start | bytes 589832 | tf_op jit(solution)/shard_map/ppermute | solution.py:71
  9.5 0.0 collective-permute-done
  9.5 0.5 collective-permute-start.1
  10.0 0.0 collective-permute-done.3
  10.0 1.6 %collective-permute-start.4 = (bf16[32,2688]{1,0:T(8,128)(2,1)S(1)}, bf16[32,2688]{1,0:T(8,128)(2,1)S(1)}, u32[]{:S(2)}, u32[]{:S(2)}) collective-permute-start(bf16[32,2688]{1,0:T(8,128)(2,1)S(1)} %fusion.3), channel_id=1, source_target_pairs={{0,2},{1,3},{2,0},{3,1},{4,6},{5,7},{6,4},{7,5},{8,10},{9,11},{10,... | collective-permute-start | bytes 516104 | tf_op jit(solution)/shard_map/ppermute | solution.py:203
  11.7 6.4 %collective-permute-done.1 = bf16[896,128]{1,0:T(8,128)(2,1)S(1)} collective-permute-done((bf16[896,128]{1,0:T(8,128)(2,1)S(1)}, bf16[896,128]{1,0:T(8,128)(2,1)S(1)}, u32[]{:S(2)}, u32[]{:S(2)}) %collective-permute-start.1) | collective-permute-done | bytes 229408 | tf_op jit(solution)/shard_map/ppermute | solution.py:201
  18.1 0.0 collective-permute-done.2.rest_1_
  18.2 0.5 collective-permute-start.5
  18.7 0.8 %collective-permute-start.6 = (bf16[896,128]{1,0:T(8,128)(2,1)S(1)}, bf16[896,128]{1,0:T(8,128)(2,1)S(1)}, u32[]{:S(2)}, u32[]{:S(2)}) collective-permute-start(bf16[896,128]{1,0:T(8,128)(2,1)S(1)} %fusion.2.rest_0_), channel_id=1, source_target_pairs={{0,8},{4,12},{8,0},{12,4},{1,9},{5,13},{9,1},{13,5},{2,10},{6,14},... | collective-permute-start | bytes 688136 | tf_op jit(solution)/shard_map/ppermute | solution.py:71
  19.4 0.9 %collective-permute-done.4 = bf16[32,2688]{1,0:T(8,128)(2,1)S(1)} collective-permute-done((bf16[32,2688]{1,0:T(8,128)(2,1)S(1)}, bf16[32,2688]{1,0:T(8,128)(2,1)S(1)}, u32[]{:S(2)}, u32[]{:S(2)}) %collective-permute-start.4) | collective-permute-done | bytes 172064 | tf_op jit(solution)/shard_map/ppermute | solution.py:203
  20.3 7.1 %collective-permute-done.5.rest_1_ = bf16[896,128]{1,0:T(8,128)(2,1)S(1)} collective-permute-done((bf16[896,128]{1,0:T(8,128)(2,1)S(1)}, bf16[896,128]{1,0:T(8,128)(2,1)S(1)}, u32[]{:S(2)}, u32[]{:S(2)}) %collective-permute-start.5) | collective-permute-done | bytes 229408 | tf_op jit(solution)/shard_map/ppermute | solution.py:70
  27.5 0.5 %collective-permute-start.11 = (bf16[32,2688]{1,0:T(8,128)(2,1)S(1)}, bf16[32,2688]{1,0:T(8,128)(2,1)S(1)}, u32[]{:S(2)}, u32[]{:S(2)}) collective-permute-start(bf16[32,2688]{1,0:T(8,128)(2,1)S(1)} %fusion.5.rest_4_), channel_id=1, source_target_pairs={{0,8},{4,12},{8,0},{12,4},{1,9},{5,13},{9,1},{13,5},{2,10},{6,14},... | collective-permute-start | bytes 516104 | tf_op jit(solution)/shard_map/ppermute | solution.py:71
  28.0 1.5 %collective-permute-done.6.rest_2_ = bf16[896,128]{1,0:T(8,128)(2,1)S(1)} collective-permute-done((bf16[896,128]{1,0:T(8,128)(2,1)S(1)}, bf16[896,128]{1,0:T(8,128)(2,1)S(1)}, u32[]{:S(2)}, u32[]{:S(2)}) %collective-permute-start.6) | collective-permute-done | bytes 229408 | tf_op jit(solution)/shard_map/ppermute | solution.py:71
  29.4 1.0 %collective-permute-start.7 = (bf16[896,128]{1,0:T(8,128)(2,1)S(1)}, bf16[896,128]{1,0:T(8,128)(2,1)S(1)}, u32[]{:S(2)}, u32[]{:S(2)}) collective-permute-start(bf16[896,128]{1,0:T(8,128)(2,1)S(1)} %collective-permute-done.6.rest_2_), channel_id=1, source_target_pairs={{0,4},{4,0},{8,12},{12,8},{1,5},{5,1},{9,13},{13,9},{2,6},{6,2},{1... | collective-permute-start | bytes 688136 | tf_op jit(solution)/shard_map/ppermute | solution.py:72
  30.5 0.0 collective-permute-done.8.rest_2_
  30.5 1.0 %collective-permute-start.9 = (bf16[128,768]{1,0:T(8,128)(2,1)S(1)}, bf16[128,768]{1,0:T(8,128)(2,1)S(1)}, u32[]{:S(2)}, u32[]{:S(2)}) collective-permute-start(bf16[128,768]{1,0:T(8,128)(2,1)S(1)} %collective-permute-done.8.rest_2_), channel_id=1, source_target_pairs={{0,4},{4,0},{8,12},{12,8},{1,5},{5,1},{9,13},{13,9},{2,6},{6,2},{1... | collective-permute-start | bytes 589832 | tf_op jit(solution)/shard_map/ppermute | solution.py:72
  31.5 1.0 %collective-permute-start.10 = (bf16[32,2688]{1,0:T(8,128)(2,1)S(1)}, bf16[32,2688]{1,0:T(8,128)(2,1)S(1)}, u32[]{:S(2)}, u32[]{:S(2)}) collective-permute-start(bf16[32,2688]{1,0:T(8,128)(2,1)S(1)} %fusion.5.rest_4_), channel_id=1, source_target_pairs={{0,4},{4,0},{8,12},{12,8},{1,5},{5,1},{9,13},{13,9},{2,6},{6,2},{1... | collective-permute-start | bytes 516104 | tf_op jit(solution)/shard_map/ppermute | solution.py:70
  32.5 4.5 %collective-permute-done.11.rest_6_ = bf16[32,2688]{1,0:T(8,128)(2,1)S(1)} collective-permute-done((bf16[32,2688]{1,0:T(8,128)(2,1)S(1)}, bf16[32,2688]{1,0:T(8,128)(2,1)S(1)}, u32[]{:S(2)}, u32[]{:S(2)}) %collective-permute-start.11) | collective-permute-done | bytes 172064 | tf_op jit(solution)/shard_map/ppermute | solution.py:71
  37.0 0.0 collective-permute-start.12
  37.7 3.1 %collective-permute-done.7.rest_3_ = bf16[896,128]{1,0:T(8,128)(2,1)S(1)} collective-permute-done((bf16[896,128]{1,0:T(8,128)(2,1)S(1)}, bf16[896,128]{1,0:T(8,128)(2,1)S(1)}, u32[]{:S(2)}, u32[]{:S(2)}) %collective-permute-start.7) | collective-permute-done | bytes 229408 | tf_op jit(solution)/shard_map/ppermute | solution.py:72
  40.7 0.0 copy-done
  40.7 0.0 copy-done.2
  40.7 0.9 %shard_map.92.low = bf16[128,128]{1,0:T(8,128)(2,1)S(1)} custom-call(s32[4]{0:T(128)S(1)} %copy-done.1, s32[64]{0:T(128)S(1)} %copy-done.2, bf16[128,3584]{1,0:T(8,128)(2,1)S(1)} %bitcast.16, bf16[896,128]{1,0:T(8,128)(2,1)S(1)} %fusion.2.rest_0_, bf16[896,128]{1,0:T(8,128)(2,1)S(1)} %collective-permute-done.5.rest_1_, ...), custom_call_target="tpu_custom_call" | custom-call | flops 134217728 | bytes 4194304 | tf_op jit(solution)/shard_map/pallas_call | solution.py:92
  41.7 3.3 %collective-permute-done.9.rest_3_ = bf16[128,768]{1,0:T(8,128)(2,1)S(1)} collective-permute-done((bf16[128,768]{1,0:T(8,128)(2,1)S(1)}, bf16[128,768]{1,0:T(8,128)(2,1)S(1)}, u32[]{:S(2)}, u32[]{:S(2)}) %collective-permute-start.9) | collective-permute-done | bytes 196640 | tf_op jit(solution)/shard_map/ppermute | solution.py:72
  44.9 3.1 %collective-permute-done.10.rest_5_ = bf16[32,2688]{1,0:T(8,128)(2,1)S(1)} collective-permute-done((bf16[32,2688]{1,0:T(8,128)(2,1)S(1)}, bf16[32,2688]{1,0:T(8,128)(2,1)S(1)}, u32[]{:S(2)}, u32[]{:S(2)}) %collective-permute-start.10) | collective-permute-done | bytes 172064 | tf_op jit(solution)/shard_map/ppermute | solution.py:70
  48.1 1.8 %collective-permute-done.12.rest_7_ = bf16[32,2688]{1,0:T(8,128)(2,1)S(1)} collective-permute-done((bf16[32,2688]{1,0:T(8,128)(2,1)S(1)}, bf16[32,2688]{1,0:T(8,128)(2,1)S(1)}, u32[]{:S(2)}, u32[]{:S(2)}) %collective-permute-start.12) | collective-permute-done | bytes 172064 | tf_op jit(solution)/shard_map/ppermute | solution.py:72
  49.9 0.0 copy-done.4
  49.9 2.3 %shard_map.93 = bf16[128,2688]{1,0:T(8,128)(2,1)} custom-call(s32[1]{0:T(128)S(6)} %copy.10.lengths, bf16[128,2688]{1,0:T(8,128)(2,1)S(1)} %bitcast.17, bf16[128,128]{1,0:T(8,128)(2,1)S(1)} %shard_map.92.low, bf16[128,768]{1,0:T(8,128)(2,1)S(1)} %bitcast.20, bf16[128,768]{1,0:T(8,128)(2,1)S(1)} %collective-permute-done.2.rest_1_, ...), custom_call_target="tpu_custom_call" | custom-call | flops 1073741824 | bytes 4194304 | tf_op jit(solution)/shard_map/pallas_call | solution.py:169
  (4 shorter events, 0.1 us)
Async XLA Ops:
  0.0 40.7 %copy-start = (bf16[1,128,3584]{2,1,0:T(8,128)(2,1)S(1)}, bf16[1,128,3584]{2,1,0:T(8,128)(2,1)}, u32[]{:S(2)}) copy-start(bf16[1,128,3584]{2,1,0:T(8,128)(2,1)} %param.9) | copy-start | bytes 2752516
  0.0 0.7 %copy-start.1 = (s32[4]{0:T(128)S(1)}, s32[4]{0:T(128)}, u32[]{:S(2)}) copy-start(s32[4]{0:T(128)} %ids.3) | copy-start | bytes 52
  0.7 0.7 %copy-start.3 = (s32[64]{0:T(128)S(1)}, s32[64]{0:T(128)}, u32[]{:S(2)}) copy-start(s32[64]{0:T(128)} %slots.1) | copy-start | bytes 772
  1.4 2.5 %copy-start.5 = (bf16[1,128,768]{2,1,0:T(8,128)(2,1)S(1)}, bf16[1,128,768]{2,1,0:T(8,128)(2,1)}, u32[]{:S(2)}) copy-start(bf16[1,128,768]{2,1,0:T(8,128)(2,1)} %param.11) | copy-start | bytes 589828
  1.4 39.3 %copy-start.2 = (s32[64]{0:T(128)S(1)}, s32[64]{0:T(128)}, u32[]{:S(2)}) copy-start(s32[64]{0:T(128)} %ranks.1) | copy-start | bytes 772
  3.3 46.6 %copy-start.4 = (bf16[1,128,2688]{2,1,0:T(8,128)(2,1)S(1)}, bf16[1,128,2688]{2,1,0:T(8,128)(2,1)}, u32[]{:S(2)}) copy-start(bf16[1,128,2688]{2,1,0:T(8,128)(2,1)} %param.10) | copy-start | bytes 2064388
  3.3 6.2 %collective-permute-start = (bf16[2,896,128]{2,1,0:T(8,128)(2,1)S(1)}, bf16[2,896,128]{2,1,0:T(8,128)(2,1)S(1)}, u32[]{:S(2)}, u32[]{:S(2)}) collective-permute-start(bf16[2,896,128]{2,1,0:T(8,128)(2,1)S(1)} %get-tuple-element.14), channel_id=1, source_target_pairs={{0,1},{1,0},{2,3},{3,2},{4,5},{5,4},{6,7},{7,6},{8,9},{9,8},{10,11... | collective-permute-start | bytes 1376264 | tf_op jit(solution)/shard_map/ppermute | solution.py:199
  3.8 6.2 %collective-permute-start.3 = (bf16[2,32,2688]{2,1,0:T(8,128)(2,1)S(1)}, bf16[2,32,2688]{2,1,0:T(8,128)(2,1)S(1)}, u32[]{:S(2)}, u32[]{:S(2)}) collective-permute-start(bf16[2,32,2688]{2,1,0:T(8,128)(2,1)S(1)} %get-tuple-element.17), channel_id=1, source_target_pairs={{0,1},{1,0},{2,3},{3,2},{4,5},{5,4},{6,7},{7,6},{8,9},{9,8},{10,11... | collective-permute-start | bytes 1032200 | tf_op jit(solution)/shard_map/ppermute | solution.py:200
  3.9 14.3 %collective-permute-start.2 = (bf16[128,768]{1,0:T(8,128)(2,1)S(1)}, bf16[128,768]{1,0:T(8,128)(2,1)S(1)}, u32[]{:S(2)}, u32[]{:S(2)}) collective-permute-start(bf16[128,768]{1,0:T(8,128)(2,1)S(1)} %bitcast.18), channel_id=1, source_target_pairs={{0,4},{4,0},{8,12},{12,8},{1,5},{5,1},{9,13},{13,9},{2,6},{6,2},{1... | collective-permute-start | bytes 589832 | tf_op jit(solution)/shard_map/ppermute | solution.py:70
  6.9 23.6 %collective-permute-start.8 = (bf16[128,768]{1,0:T(8,128)(2,1)S(1)}, bf16[128,768]{1,0:T(8,128)(2,1)S(1)}, u32[]{:S(2)}, u32[]{:S(2)}) collective-permute-start(bf16[128,768]{1,0:T(8,128)(2,1)S(1)} %bitcast.19), channel_id=1, source_target_pairs={{0,8},{4,12},{8,0},{12,4},{1,9},{5,13},{9,1},{13,5},{2,10},{6,14},... | collective-permute-start | bytes 589832 | tf_op jit(solution)/shard_map/ppermute | solution.py:71
  9.5 8.6 %collective-permute-start.1 = (bf16[896,128]{1,0:T(8,128)(2,1)S(1)}, bf16[896,128]{1,0:T(8,128)(2,1)S(1)}, u32[]{:S(2)}, u32[]{:S(2)}) collective-permute-start(bf16[896,128]{1,0:T(8,128)(2,1)S(1)} %fusion), channel_id=1, source_target_pairs={{0,2},{1,3},{2,0},{3,1},{4,6},{5,7},{6,4},{7,5},{8,10},{9,11},{10,... | collective-permute-start | bytes 688136 | tf_op jit(solution)/shard_map/ppermute | solution.py:201
  10.0 10.2 %collective-permute-start.4 = (bf16[32,2688]{1,0:T(8,128)(2,1)S(1)}, bf16[32,2688]{1,0:T(8,128)(2,1)S(1)}, u32[]{:S(2)}, u32[]{:S(2)}) collective-permute-start(bf16[32,2688]{1,0:T(8,128)(2,1)S(1)} %fusion.3), channel_id=1, source_target_pairs={{0,2},{1,3},{2,0},{3,1},{4,6},{5,7},{6,4},{7,5},{8,10},{9,11},{10,... | collective-permute-start | bytes 516104 | tf_op jit(solution)/shard_map/ppermute | solution.py:203
  18.2 9.3 %collective-permute-start.5 = (bf16[896,128]{1,0:T(8,128)(2,1)S(1)}, bf16[896,128]{1,0:T(8,128)(2,1)S(1)}, u32[]{:S(2)}, u32[]{:S(2)}) collective-permute-start(bf16[896,128]{1,0:T(8,128)(2,1)S(1)} %fusion.2.rest_0_), channel_id=1, source_target_pairs={{0,4},{4,0},{8,12},{12,8},{1,5},{5,1},{9,13},{13,9},{2,6},{6,2},{1... | collective-permute-start | bytes 688136 | tf_op jit(solution)/shard_map/ppermute | solution.py:70
  18.7 10.8 %collective-permute-start.6 = (bf16[896,128]{1,0:T(8,128)(2,1)S(1)}, bf16[896,128]{1,0:T(8,128)(2,1)S(1)}, u32[]{:S(2)}, u32[]{:S(2)}) collective-permute-start(bf16[896,128]{1,0:T(8,128)(2,1)S(1)} %fusion.2.rest_0_), channel_id=1, source_target_pairs={{0,8},{4,12},{8,0},{12,4},{1,9},{5,13},{9,1},{13,5},{2,10},{6,14},... | collective-permute-start | bytes 688136 | tf_op jit(solution)/shard_map/ppermute | solution.py:71
  27.5 9.5 %collective-permute-start.11 = (bf16[32,2688]{1,0:T(8,128)(2,1)S(1)}, bf16[32,2688]{1,0:T(8,128)(2,1)S(1)}, u32[]{:S(2)}, u32[]{:S(2)}) collective-permute-start(bf16[32,2688]{1,0:T(8,128)(2,1)S(1)} %fusion.5.rest_4_), channel_id=1, source_target_pairs={{0,8},{4,12},{8,0},{12,4},{1,9},{5,13},{9,1},{13,5},{2,10},{6,14},... | collective-permute-start | bytes 516104 | tf_op jit(solution)/shard_map/ppermute | solution.py:71
  29.4 11.3 %collective-permute-start.7 = (bf16[896,128]{1,0:T(8,128)(2,1)S(1)}, bf16[896,128]{1,0:T(8,128)(2,1)S(1)}, u32[]{:S(2)}, u32[]{:S(2)}) collective-permute-start(bf16[896,128]{1,0:T(8,128)(2,1)S(1)} %collective-permute-done.6.rest_2_), channel_id=1, source_target_pairs={{0,4},{4,0},{8,12},{12,8},{1,5},{5,1},{9,13},{13,9},{2,6},{6,2},{1... | collective-permute-start | bytes 688136 | tf_op jit(solution)/shard_map/ppermute | solution.py:72
  30.5 14.5 %collective-permute-start.9 = (bf16[128,768]{1,0:T(8,128)(2,1)S(1)}, bf16[128,768]{1,0:T(8,128)(2,1)S(1)}, u32[]{:S(2)}, u32[]{:S(2)}) collective-permute-start(bf16[128,768]{1,0:T(8,128)(2,1)S(1)} %collective-permute-done.8.rest_2_), channel_id=1, source_target_pairs={{0,4},{4,0},{8,12},{12,8},{1,5},{5,1},{9,13},{13,9},{2,6},{6,2},{1... | collective-permute-start | bytes 589832 | tf_op jit(solution)/shard_map/ppermute | solution.py:72
  31.5 16.6 %collective-permute-start.10 = (bf16[32,2688]{1,0:T(8,128)(2,1)S(1)}, bf16[32,2688]{1,0:T(8,128)(2,1)S(1)}, u32[]{:S(2)}, u32[]{:S(2)}) collective-permute-start(bf16[32,2688]{1,0:T(8,128)(2,1)S(1)} %fusion.5.rest_4_), channel_id=1, source_target_pairs={{0,4},{4,0},{8,12},{12,8},{1,5},{5,1},{9,13},{13,9},{2,6},{6,2},{1... | collective-permute-start | bytes 516104 | tf_op jit(solution)/shard_map/ppermute | solution.py:70
  37.0 12.9 %collective-permute-start.12 = (bf16[32,2688]{1,0:T(8,128)(2,1)S(1)}, bf16[32,2688]{1,0:T(8,128)(2,1)S(1)}, u32[]{:S(2)}, u32[]{:S(2)}) collective-permute-start(bf16[32,2688]{1,0:T(8,128)(2,1)S(1)} %collective-permute-done.11.rest_6_), channel_id=1, source_target_pairs={{0,4},{4,0},{8,12},{12,8},{1,5},{5,1},{9,13},{13,9},{2,6},{6,2},{1... | collective-permute-start | bytes 516104 | tf_op jit(solution)/shard_map/ppermute | solution.py:72

commit v5 on v4

--- a/solution.py
+++ b/solution.py
@@ -1,3 +1,4 @@
+import functools
 import math
 
 import jax
@@ -23,14 +24,14 @@
     return pl.BlockSpec(memory_space=space)
 
 
-def select_kernel(ids, slots, *rest):
+def select_kernel(table, *rest, requests):
     stores, outs, sems = rest[:2], rest[2:6], rest[6]
     per_shard = stores[0].shape[0]
     me = lax.axis_index("req")
     first = me * per_shard
     copies = []
     for i, flip in enumerate((0, 2, 1, 3)):
-        local = slots[ids[me ^ flip]] - first
+        local = table[requests + table[me ^ flip]] - first
         held = (local >= 0) & (local < per_shard)
         for f, store in enumerate(stores):
             out = outs[2 * f + i // 2]
@@ -55,22 +56,24 @@
 def select(ids, slots, down, up):
     shapes = [jax.ShapeDtypeStruct((2, *x.shape[1:]), x.dtype) for x in (down, down, up, up)]
     return pl.pallas_call(
-        select_kernel,
+        functools.partial(select_kernel, requests=ids.shape[0]),
         out_shape=shapes,
-        in_specs=[spec(SMEM), spec(SMEM), spec(HBM), spec(HBM)],
+        in_specs=[spec(SMEM), spec(HBM), spec(HBM)],
         out_specs=[spec(VMEM)] * 4,
         scratch_shapes=[pltpu.SemaphoreType.DMA((8,))],
         compiler_params=WHOLE,
-    )(ids, slots, down, up)
+    )(jnp.concatenate([ids, slots]), down, up)
 
 
 SIBLING = [(0, 1), (1, 0), (2, 3), (3, 2)]
 ACROSS = [(0, 2), (1, 3), (2, 0), (3, 1)]
+ONE = [(i, i ^ 1) for i in range(4)]
+TWO = [(i, i ^ 2) for i in range(4)]
+LAST = [(0, 0), (1, 1), (2, 3), (3, 2)]
+
+
 def spread(shard):
-    near = lax.ppermute(shard, "ctx", [(i, i ^ 1) for i in range(4)])
-    two = lax.ppermute(shard, "ctx", [(i, i ^ 2) for i in range(4)])
-    cross = lax.ppermute(two, "ctx", [(i, i ^ 1) for i in range(4)])
-    return [shard, near, two, cross]
+    return lax.ppermute(shard, "ctx", ONE), lax.ppermute(shard, "ctx", TWO)
 
 
 def low_rank_kernel(ids, ranks, hidden, *rest):
@@ -198,16 +201,24 @@
     )
     near_down = lax.ppermute(give_down, "req", SIBLING)
     near_up = lax.ppermute(give_up, "req", SIBLING)
-    far_down = lax.ppermute(keep_down[1] + near_down[1], "req", ACROSS)
-    pass_up = keep_up[1] + near_up[1]
+    pass_down, kv = lax.optimization_barrier((keep_down[1] + near_down[1], kv_base[0]))
+    far_down = lax.ppermute(pass_down, "req", ACROSS)
+    kv_one, kv_two = spread(kv)
+    pass_up, far_down = lax.optimization_barrier((keep_up[1] + near_up[1], far_down))
     far_up = lax.ppermute(pass_up, "req", ACROSS)
-    kvs = spread(kv_base[0])
     down = keep_down[0] + near_down[0] + far_down
-    down, kvs[1] = lax.optimization_barrier((down, kvs[1]))
-    downs = spread(down)
+    down, kv_one, kv_two = lax.optimization_barrier((down, kv_one, kv_two))
+    down_one, down_two = spread(down)
+    kv_three = lax.ppermute(kv_two, "ctx", LAST)
     up = keep_up[0] + near_up[0] + far_up
-    up, downs[1] = lax.optimization_barrier((up, downs[1]))
-    ups = spread(up)
+    up, down_one = lax.optimization_barrier((up, down_one))
+    up_one, up_two = spread(up)
+    down_two, up_one, kv_three = lax.optimization_barrier((down_two, up_one, kv_three))
+    down_three = lax.ppermute(down_two, "ctx", ONE)
+    up_three = lax.ppermute(up_two, "ctx", ONE)
+    kvs = [kv, kv_one, kv_two, kv_three]
+    downs = [down, down_one, down_two, down_three]
+    ups = [up, up_one, up_two, up_three]
     low = low_rank(adapter_ids, rank_buckets, hidden_states[0], downs)
     return attend(lengths, queries_base[0], low, kvs, ups)[None]
 

time: 52.3 us -> 53.6 us (1.025)
  the two profiles are of different devices: /device:TPU:0 before, /device:TPU:18 now
where the time goes in v5:
time: 53.6 us; the launch traced here: 53.4 us
  waiting for transfers between devices  31.3 us (58%)
  starting transfers between devices  14.8 us (28%)
  Pallas kernels  5.69 us (11%)
  other arithmetic  0.89 us (2%)
  between operations  0.74 us (1%)
    ppermute x6, waiting for transfers between devices, spread(): return (lax.ppermute(shard, 'ctx', ONE), lax.ppermute(shard, 'ctx', TWO))  12.4 us
    ppermute x6, starting transfers between devices, spread(): return (lax.ppermute(shard, 'ctx', ONE), lax.ppermute(shard, 'ctx', TWO))  7.5 us
    ppermute x1, waiting for transfers between devices, body(): down_three = lax.ppermute(down_two, 'ctx', ONE)  5.83 us
    ppermute x1, waiting for transfers between devices, body(): kv_three = lax.ppermute(kv_two, 'ctx', LAST)  5.41 us
    ppermute x1, waiting for transfers between devices, body(): far_down = lax.ppermute(pass_down, 'req', ACROSS)  5.24 us
    ppermute x1, starting transfers between devices, body(): kv_three = lax.ppermute(kv_two, 'ctx', LAST)  3.47 us
    pallas_call x1, Pallas kernels, attend(): pl.pallas_call(attend_kernel, out_shape=jax.ShapeDtypeStruct(base.shape,...  2.83 us
    ppermute x1, starting transfers between devices, body(): down_three = lax.ppermute(down_two, 'ctx', ONE)  2.48 us
  transfers between devices with their start and end apart: 13, of which 10 were waited for; matrix products, arithmetic and copies ran while one was open for 0% of the time, Pallas kernels for 2%

profile of v5, /device:TPU:18, one launch (start us, length us, event | category | flops | bytes accessed | tf_op | source)
XLA Modules:
  0.0 53.4 jit_solution(13008402633115710419)
XLA Ops:
  0.0 0.7 %pad_add_fusion.table = s32[68]{0:T(128)S(1)} fusion(s32[64]{0:T(128)} %param.15, s32[4]{0:T(128)} %ids.1), kind=kLoop, calls=%fused_computation.10 | loop fusion | flops 68 | bytes 544 | tf_op jit(solution)/shard_map/concatenate | solution.py:65
  0.7 0.0 copy-start.4
  0.7 0.0 copy-start
  0.8 0.0 copy-start.1
  0.8 0.0 copy-start.2
  0.8 1.9 %shard_map.91 = (bf16[2,896,128]{2,1,0:T(8,128)(2,1)S(1)}, bf16[2,896,128]{2,1,0:T(8,128)(2,1)S(1)}, bf16[2,32,2688]{2,1,0:T(8,128)(2,1)S(1)}, bf16[2,32,2688]{2,1,0:T(8,128)(2,1)S(1)}) custom-call(s32[68]{0:T(128)S(1)} %pad_add_fusion.table, bf16[16,896,128]{2,1,0:T(8,128)(2,1)} %rest_0_.1, bf16[16,32,2688]{2,1,0:T(8,128)(2,1)} %rest_1_.1), custom_call_target="tpu_custom_call" | custom-call | tf_op jit(solution)/shard_map/pallas_call | solution.py:58
  2.7 0.0 copy-start.3
  2.7 0.1 collective-permute-start
  2.8 0.5 collective-permute-start.1
  3.3 1.3 %collective-permute-done = bf16[2,896,128]{2,1,0:T(8,128)(2,1)S(1)} collective-permute-done((bf16[2,896,128]{2,1,0:T(8,128)(2,1)S(1)}, bf16[2,896,128]{2,1,0:T(8,128)(2,1)S(1)}, u32[]{:S(2)}, u32[]{:S(2)}) %collective-permute-start) | collective-permute-done | bytes 458784 | tf_op jit(solution)/shard_map/ppermute | solution.py:202
  4.6 0.4 collective-permute-start.2
  5.0 0.1 collective-permute-done.1
  5.1 0.0 copy-done.4
  5.1 1.6 %collective-permute-start.3 = (bf16[128,768]{1,0:T(8,128)(2,1)S(1)}, bf16[128,768]{1,0:T(8,128)(2,1)S(1)}, u32[]{:S(2)}, u32[]{:S(2)}) collective-permute-start(bf16[128,768]{1,0:T(8,128)(2,1)S(1)} %bitcast.18), channel_id=1, source_target_pairs={{0,4},{4,0},{8,12},{12,8},{1,5},{5,1},{9,13},{13,9},{2,6},{6,2},{1... | collective-permute-start | bytes 589832 | tf_op jit(solution)/shard_map/ppermute | solution.py:76
  6.7 0.3 collective-permute-start.4
  7.1 5.2 %collective-permute-done.2 = bf16[896,128]{1,0:T(8,128)(2,1)S(1)} collective-permute-done((bf16[896,128]{1,0:T(8,128)(2,1)S(1)}, bf16[896,128]{1,0:T(8,128)(2,1)S(1)}, u32[]{:S(2)}, u32[]{:S(2)}) %collective-permute-start.2) | collective-permute-done | bytes 229408 | tf_op jit(solution)/shard_map/ppermute | solution.py:205
  12.3 0.3 collective-permute-start.5
  12.7 1.5 %collective-permute-done.3.rest_1_ = bf16[128,768]{1,0:T(8,128)(2,1)S(1)} collective-permute-done((bf16[128,768]{1,0:T(8,128)(2,1)S(1)}, bf16[128,768]{1,0:T(8,128)(2,1)S(1)}, u32[]{:S(2)}, u32[]{:S(2)}) %collective-permute-start.3) | collective-permute-done | bytes 196640 | tf_op jit(solution)/shard_map/ppermute | solution.py:76
  14.2 2.1 %collective-permute-done.4.rest_2_ = bf16[128,768]{1,0:T(8,128)(2,1)S(1)} collective-permute-done((bf16[128,768]{1,0:T(8,128)(2,1)S(1)}, bf16[128,768]{1,0:T(8,128)(2,1)S(1)}, u32[]{:S(2)}, u32[]{:S(2)}) %collective-permute-start.4) | collective-permute-done | bytes 196640 | tf_op jit(solution)/shard_map/ppermute | solution.py:76
  16.3 2.7 %collective-permute-start.6 = (bf16[896,128]{1,0:T(8,128)(2,1)S(1)}, bf16[896,128]{1,0:T(8,128)(2,1)S(1)}, u32[]{:S(2)}, u32[]{:S(2)}) collective-permute-start(bf16[896,128]{1,0:T(8,128)(2,1)S(1)} %fusion.2.rest_0_), channel_id=1, source_target_pairs={{0,4},{4,0},{8,12},{12,8},{1,5},{5,1},{9,13},{13,9},{2,6},{6,2},{1... | collective-permute-start | bytes 688136 | tf_op jit(solution)/shard_map/ppermute | solution.py:76
  19.0 0.3 collective-permute-start.7
  19.4 3.5 %collective-permute-start.9 = (bf16[128,768]{1,0:T(8,128)(2,1)S(1)}, bf16[128,768]{1,0:T(8,128)(2,1)S(1)}, u32[]{:S(2)}, u32[]{:S(2)}) collective-permute-start(bf16[128,768]{1,0:T(8,128)(2,1)S(1)} %collective-permute-done.4.rest_2_), channel_id=1, source_target_pairs={{0,0},{4,4},{8,12},{12,8},{1,1},{5,5},{9,13},{13,9},{2,2},{6,6},{1... | collective-permute-start | bytes 589832 | tf_op jit(solution)/shard_map/ppermute | solution.py:212
  22.8 0.0 collective-permute-done.5
  22.9 6.2 %collective-permute-done.6.rest_1_ = bf16[896,128]{1,0:T(8,128)(2,1)S(1)} collective-permute-done((bf16[896,128]{1,0:T(8,128)(2,1)S(1)}, bf16[896,128]{1,0:T(8,128)(2,1)S(1)}, u32[]{:S(2)}, u32[]{:S(2)}) %collective-permute-start.6) | collective-permute-done | bytes 229408 | tf_op jit(solution)/shard_map/ppermute | solution.py:76
  29.1 2.5 %collective-permute-start.8 = (bf16[32,2688]{1,0:T(8,128)(2,1)S(1)}, bf16[32,2688]{1,0:T(8,128)(2,1)S(1)}, u32[]{:S(2)}, u32[]{:S(2)}) collective-permute-start(bf16[32,2688]{1,0:T(8,128)(2,1)S(1)} %fusion.4.rest_4_), channel_id=1, source_target_pairs={{0,4},{4,0},{8,12},{12,8},{1,5},{5,1},{9,13},{13,9},{2,6},{6,2},{1... | collective-permute-start | bytes 516104 | tf_op jit(solution)/shard_map/ppermute | solution.py:76
  31.5 0.0 collective-permute-start.11
  31.5 5.4 %collective-permute-done.9.rest_3_ = bf16[128,768]{1,0:T(8,128)(2,1)S(1)} collective-permute-done((bf16[128,768]{1,0:T(8,128)(2,1)S(1)}, bf16[128,768]{1,0:T(8,128)(2,1)S(1)}, u32[]{:S(2)}, u32[]{:S(2)}) %collective-permute-start.9) | collective-permute-done | bytes 196640 | tf_op jit(solution)/shard_map/ppermute | solution.py:212
  37.0 0.0 collective-permute-done.7.rest_2_
  37.0 2.6 %collective-permute-done.8.rest_5_ = bf16[32,2688]{1,0:T(8,128)(2,1)S(1)} collective-permute-done((bf16[32,2688]{1,0:T(8,128)(2,1)S(1)}, bf16[32,2688]{1,0:T(8,128)(2,1)S(1)}, u32[]{:S(2)}, u32[]{:S(2)}) %collective-permute-start.8) | collective-permute-done | bytes 172064 | tf_op jit(solution)/shard_map/ppermute | solution.py:76
  39.6 2.5 %collective-permute-start.10 = (bf16[896,128]{1,0:T(8,128)(2,1)S(1)}, bf16[896,128]{1,0:T(8,128)(2,1)S(1)}, u32[]{:S(2)}, u32[]{:S(2)}) collective-permute-start(bf16[896,128]{1,0:T(8,128)(2,1)S(1)} %collective-permute-done.7.rest_2_), channel_id=1, source_target_pairs={{0,4},{4,0},{8,12},{12,8},{1,5},{5,1},{9,13},{13,9},{2,6},{6,2},{1... | collective-permute-start | bytes 688136 | tf_op jit(solution)/shard_map/ppermute | solution.py:217
  42.1 0.0 collective-permute-done.11.rest_6_
  42.1 0.0 collective-permute-start.12
  42.7 5.8 %collective-permute-done.10.rest_3_ = bf16[896,128]{1,0:T(8,128)(2,1)S(1)} collective-permute-done((bf16[896,128]{1,0:T(8,128)(2,1)S(1)}, bf16[896,128]{1,0:T(8,128)(2,1)S(1)}, u32[]{:S(2)}, u32[]{:S(2)}) %collective-permute-start.10) | collective-permute-done | bytes 229408 | tf_op jit(solution)/shard_map/ppermute | solution.py:217
  48.6 0.0 copy-done
  48.6 0.0 copy-done.1
  48.6 0.0 copy-done.2
  48.6 0.9 %shard_map.92.low = bf16[128,128]{1,0:T(8,128)(2,1)S(1)} custom-call(s32[4]{0:T(128)S(1)} %copy-done.1, s32[64]{0:T(128)S(1)} %copy-done.2, bf16[128,3584]{1,0:T(8,128)(2,1)S(1)} %bitcast.16, bf16[896,128]{1,0:T(8,128)(2,1)S(1)} %fusion.2.rest_0_, bf16[896,128]{1,0:T(8,128)(2,1)S(1)} %collective-permute-done.6.rest_1_, ...), custom_call_target="tpu_custom_call" | custom-call | flops 134217728 | bytes 4194304 | tf_op jit(solution)/shard_map/pallas_call | solution.py:95
  49.5 1.0 %collective-permute-done.12.rest_7_ = bf16[32,2688]{1,0:T(8,128)(2,1)S(1)} collective-permute-done((bf16[32,2688]{1,0:T(8,128)(2,1)S(1)}, bf16[32,2688]{1,0:T(8,128)(2,1)S(1)}, u32[]{:S(2)}, u32[]{:S(2)}) %collective-permute-start.12) | collective-permute-done | bytes 172064 | tf_op jit(solution)/shard_map/ppermute | solution.py:218
  50.6 0.0 copy-done.3
  50.6 2.8 %shard_map.93 = bf16[128,2688]{1,0:T(8,128)(2,1)} custom-call(s32[1]{0:T(128)S(6)} %copy.10.lengths, bf16[128,2688]{1,0:T(8,128)(2,1)S(1)} %bitcast.17, bf16[128,128]{1,0:T(8,128)(2,1)S(1)} %shard_map.92.low, bf16[128,768]{1,0:T(8,128)(2,1)S(1)} %bitcast.20, bf16[128,768]{1,0:T(8,128)(2,1)S(1)} %collective-permute-done.3.rest_1_, ...), custom_call_target="tpu_custom_call" | custom-call | flops 1073741824 | bytes 4194304 | tf_op jit(solution)/shard_map/pallas_call | solution.py:172
  (4 shorter events, 0.1 us)
Async XLA Ops:
  0.7 4.3 %copy-start.4 = (bf16[1,128,768]{2,1,0:T(8,128)(2,1)S(1)}, bf16[1,128,768]{2,1,0:T(8,128)(2,1)}, u32[]{:S(2)}) copy-start(bf16[1,128,768]{2,1,0:T(8,128)(2,1)} %param.11) | copy-start | bytes 589828
  0.7 47.8 %copy-start = (bf16[1,128,3584]{2,1,0:T(8,128)(2,1)S(1)}, bf16[1,128,3584]{2,1,0:T(8,128)(2,1)}, u32[]{:S(2)}) copy-start(bf16[1,128,3584]{2,1,0:T(8,128)(2,1)} %param.9) | copy-start | bytes 2752516
  0.8 47.8 %copy-start.1 = (s32[4]{0:T(128)S(1)}, s32[4]{0:T(128)}, u32[]{:S(2)}) copy-start(s32[4]{0:T(128)} %ids.1) | copy-start | bytes 52
  0.8 47.8 %copy-start.2 = (s32[64]{0:T(128)S(1)}, s32[64]{0:T(128)}, u32[]{:S(2)}) copy-start(s32[64]{0:T(128)} %ranks.1) | copy-start | bytes 772
  2.7 47.9 %copy-start.3 = (bf16[1,128,2688]{2,1,0:T(8,128)(2,1)S(1)}, bf16[1,128,2688]{2,1,0:T(8,128)(2,1)}, u32[]{:S(2)}) copy-start(bf16[1,128,2688]{2,1,0:T(8,128)(2,1)} %param.10) | copy-start | bytes 2064388
  2.7 1.9 %collective-permute-start = (bf16[2,896,128]{2,1,0:T(8,128)(2,1)S(1)}, bf16[2,896,128]{2,1,0:T(8,128)(2,1)S(1)}, u32[]{:S(2)}, u32[]{:S(2)}) collective-permute-start(bf16[2,896,128]{2,1,0:T(8,128)(2,1)S(1)} %get-tuple-element.22), channel_id=1, source_target_pairs={{0,1},{1,0},{2,3},{3,2},{4,5},{5,4},{6,7},{7,6},{8,9},{9,8},{10,11... | collective-permute-start | bytes 1376264 | tf_op jit(solution)/shard_map/ppermute | solution.py:202
  2.8 2.3 %collective-permute-start.1 = (bf16[2,32,2688]{2,1,0:T(8,128)(2,1)S(1)}, bf16[2,32,2688]{2,1,0:T(8,128)(2,1)S(1)}, u32[]{:S(2)}, u32[]{:S(2)}) collective-permute-start(bf16[2,32,2688]{2,1,0:T(8,128)(2,1)S(1)} %get-tuple-element.24), channel_id=1, source_target_pairs={{0,1},{1,0},{2,3},{3,2},{4,5},{5,4},{6,7},{7,6},{8,9},{9,8},{10,11... | collective-permute-start | bytes 1032200 | tf_op jit(solution)/shard_map/ppermute | solution.py:203
  4.6 7.7 %collective-permute-start.2 = (bf16[896,128]{1,0:T(8,128)(2,1)S(1)}, bf16[896,128]{1,0:T(8,128)(2,1)S(1)}, u32[]{:S(2)}, u32[]{:S(2)}) collective-permute-start(bf16[896,128]{1,0:T(8,128)(2,1)S(1)} %fusion), channel_id=1, source_target_pairs={{0,2},{1,3},{2,0},{3,1},{4,6},{5,7},{6,4},{7,5},{8,10},{9,11},{10,... | collective-permute-start | bytes 688136 | tf_op jit(solution)/shard_map/ppermute | solution.py:205
  5.1 9.1 %collective-permute-start.3 = (bf16[128,768]{1,0:T(8,128)(2,1)S(1)}, bf16[128,768]{1,0:T(8,128)(2,1)S(1)}, u32[]{:S(2)}, u32[]{:S(2)}) collective-permute-start(bf16[128,768]{1,0:T(8,128)(2,1)S(1)} %bitcast.18), channel_id=1, source_target_pairs={{0,4},{4,0},{8,12},{12,8},{1,5},{5,1},{9,13},{13,9},{2,6},{6,2},{1... | collective-permute-start | bytes 589832 | tf_op jit(solution)/shard_map/ppermute | solution.py:76
  6.7 9.6 %collective-permute-start.4 = (bf16[128,768]{1,0:T(8,128)(2,1)S(1)}, bf16[128,768]{1,0:T(8,128)(2,1)S(1)}, u32[]{:S(2)}, u32[]{:S(2)}) collective-permute-start(bf16[128,768]{1,0:T(8,128)(2,1)S(1)} %bitcast.19), channel_id=1, source_target_pairs={{0,8},{4,12},{8,0},{12,4},{1,9},{5,13},{9,1},{13,5},{2,10},{6,14},... | collective-permute-start | bytes 589832 | tf_op jit(solution)/shard_map/ppermute | solution.py:76
  12.3 10.5 %collective-permute-start.5 = (bf16[32,2688]{1,0:T(8,128)(2,1)S(1)}, bf16[32,2688]{1,0:T(8,128)(2,1)S(1)}, u32[]{:S(2)}, u32[]{:S(2)}) collective-permute-start(bf16[32,2688]{1,0:T(8,128)(2,1)S(1)} %fusion.5), channel_id=1, source_target_pairs={{0,2},{1,3},{2,0},{3,1},{4,6},{5,7},{6,4},{7,5},{8,10},{9,11},{10,... | collective-permute-start | bytes 516104 | tf_op jit(solution)/shard_map/ppermute | solution.py:208
  16.3 12.7 %collective-permute-start.6 = (bf16[896,128]{1,0:T(8,128)(2,1)S(1)}, bf16[896,128]{1,0:T(8,128)(2,1)S(1)}, u32[]{:S(2)}, u32[]{:S(2)}) collective-permute-start(bf16[896,128]{1,0:T(8,128)(2,1)S(1)} %fusion.2.rest_0_), channel_id=1, source_target_pairs={{0,4},{4,0},{8,12},{12,8},{1,5},{5,1},{9,13},{13,9},{2,6},{6,2},{1... | collective-permute-start | bytes 688136 | tf_op jit(solution)/shard_map/ppermute | solution.py:76
  19.0 17.9 %collective-permute-start.7 = (bf16[896,128]{1,0:T(8,128)(2,1)S(1)}, bf16[896,128]{1,0:T(8,128)(2,1)S(1)}, u32[]{:S(2)}, u32[]{:S(2)}) collective-permute-start(bf16[896,128]{1,0:T(8,128)(2,1)S(1)} %fusion.2.rest_0_), channel_id=1, source_target_pairs={{0,8},{4,12},{8,0},{12,4},{1,9},{5,13},{9,1},{13,5},{2,10},{6,14},... | collective-permute-start | bytes 688136 | tf_op jit(solution)/shard_map/ppermute | solution.py:76
  19.4 17.6 %collective-permute-start.9 = (bf16[128,768]{1,0:T(8,128)(2,1)S(1)}, bf16[128,768]{1,0:T(8,128)(2,1)S(1)}, u32[]{:S(2)}, u32[]{:S(2)}) collective-permute-start(bf16[128,768]{1,0:T(8,128)(2,1)S(1)} %collective-permute-done.4.rest_2_), channel_id=1, source_target_pairs={{0,0},{4,4},{8,12},{12,8},{1,1},{5,5},{9,13},{13,9},{2,2},{6,6},{1... | collective-permute-start | bytes 589832 | tf_op jit(solution)/shard_map/ppermute | solution.py:212
  29.1 10.5 %collective-permute-start.8 = (bf16[32,2688]{1,0:T(8,128)(2,1)S(1)}, bf16[32,2688]{1,0:T(8,128)(2,1)S(1)}, u32[]{:S(2)}, u32[]{:S(2)}) collective-permute-start(bf16[32,2688]{1,0:T(8,128)(2,1)S(1)} %fusion.4.rest_4_), channel_id=1, source_target_pairs={{0,4},{4,0},{8,12},{12,8},{1,5},{5,1},{9,13},{13,9},{2,6},{6,2},{1... | collective-permute-start | bytes 516104 | tf_op jit(solution)/shard_map/ppermute | solution.py:76
  31.5 10.5 %collective-permute-start.11 = (bf16[32,2688]{1,0:T(8,128)(2,1)S(1)}, bf16[32,2688]{1,0:T(8,128)(2,1)S(1)}, u32[]{:S(2)}, u32[]{:S(2)}) collective-permute-start(bf16[32,2688]{1,0:T(8,128)(2,1)S(1)} %fusion.4.rest_4_), channel_id=1, source_target_pairs={{0,8},{4,12},{8,0},{12,4},{1,9},{5,13},{9,1},{13,5},{2,10},{6,14},... | collective-permute-start | bytes 516104 | tf_op jit(solution)/shard_map/ppermute | solution.py:76
  39.6 9.0 %collective-permute-start.10 = (bf16[896,128]{1,0:T(8,128)(2,1)S(1)}, bf16[896,128]{1,0:T(8,128)(2,1)S(1)}, u32[]{:S(2)}, u32[]{:S(2)}) collective-permute-start(bf16[896,128]{1,0:T(8,128)(2,1)S(1)} %collective-permute-done.7.rest_2_), channel_id=1, source_target_pairs={{0,4},{4,0},{8,12},{12,8},{1,5},{5,1},{9,13},{13,9},{2,6},{6,2},{1... | collective-permute-start | bytes 688136 | tf_op jit(solution)/shard_map/ppermute | solution.py:217
  42.1 8.5 %collective-permute-start.12 = (bf16[32,2688]{1,0:T(8,128)(2,1)S(1)}, bf16[32,2688]{1,0:T(8,128)(2,1)S(1)}, u32[]{:S(2)}, u32[]{:S(2)}) collective-permute-start(bf16[32,2688]{1,0:T(8,128)(2,1)S(1)} %collective-permute-done.11.rest_6_), channel_id=1, source_target_pairs={{0,4},{4,0},{8,12},{12,8},{1,5},{5,1},{9,13},{13,9},{2,6},{6,2},{1... | collective-permute-start | bytes 516104 | tf_op jit(solution)/shard_map/ppermute | solution.py:218

commit v6 on v5

--- a/solution.py
+++ b/solution.py
@@ -69,7 +69,7 @@
 ACROSS = [(0, 2), (1, 3), (2, 0), (3, 1)]
 ONE = [(i, i ^ 1) for i in range(4)]
 TWO = [(i, i ^ 2) for i in range(4)]
-LAST = [(0, 0), (1, 1), (2, 3), (3, 2)]
+THREE = [(i, i ^ 3) for i in range(4)]
 
 
 def spread(shard):
@@ -199,19 +199,18 @@
     keep_down, give_down, keep_up, give_up = select(
         adapter_ids, adapter_slots, adapter_down, adapter_up
     )
+    kv = kv_base[0]
+    kv_one, kv_two = spread(kv)
     near_down = lax.ppermute(give_down, "req", SIBLING)
     near_up = lax.ppermute(give_up, "req", SIBLING)
-    pass_down, kv = lax.optimization_barrier((keep_down[1] + near_down[1], kv_base[0]))
+    pass_down, kv = lax.optimization_barrier((keep_down[1] + near_down[1], kv))
     far_down = lax.ppermute(pass_down, "req", ACROSS)
-    kv_one, kv_two = spread(kv)
-    pass_up, far_down = lax.optimization_barrier((keep_up[1] + near_up[1], far_down))
-    far_up = lax.ppermute(pass_up, "req", ACROSS)
+    kv_three = lax.ppermute(kv, "ctx", THREE)
+    far_up = lax.ppermute(keep_up[1] + near_up[1], "req", ACROSS)
     down = keep_down[0] + near_down[0] + far_down
     down, kv_one, kv_two = lax.optimization_barrier((down, kv_one, kv_two))
     down_one, down_two = spread(down)
-    kv_three = lax.ppermute(kv_two, "ctx", LAST)
     up = keep_up[0] + near_up[0] + far_up
-    up, down_one = lax.optimization_barrier((up, down_one))
     up_one, up_two = spread(up)
     down_two, up_one, kv_three = lax.optimization_barrier((down_two, up_one, kv_three))
     down_three = lax.ppermute(down_two, "ctx", ONE)

time: 53.6 us -> 54.8 us (1.022)
  the two profiles are of different devices: /device:TPU:18 before, /device:TPU:0 now
where the time goes in v6:
time: 54.8 us
  waiting for transfers between devices  33.4 us (61%)
  starting transfers between devices  15.7 us (29%)
  Pallas kernels  4.09 us (7%)
  other arithmetic  0.93 us (2%)
  between operations  0.71 us (1%)
    ppermute x6, waiting for transfers between devices, spread(): return (lax.ppermute(shard, 'ctx', ONE), lax.ppermute(shard, 'ctx', TWO))  21.5 us
    ppermute x6, starting transfers between devices, spread(): return (lax.ppermute(shard, 'ctx', ONE), lax.ppermute(shard, 'ctx', TWO))  10.7 us
    ppermute x1, waiting for transfers between devices, body(): far_down = lax.ppermute(pass_down, 'req', ACROSS)  5.55 us
    ppermute x1, waiting for transfers between devices, body(): down_three = lax.ppermute(down_two, 'ctx', ONE)  4.92 us
    pallas_call x1, Pallas kernels, attend(): pl.pallas_call(attend_kernel, out_shape=jax.ShapeDtypeStruct(base.shape,...  2.33 us
    ppermute x1, starting transfers between devices, body(): near_down = lax.ppermute(give_down, 'req', SIBLING)  1.69 us
    ppermute x1, waiting for transfers between devices, body(): up_three = lax.ppermute(up_two, 'ctx', ONE)  1.44 us
    ppermute x1, starting transfers between devices, body(): far_down = lax.ppermute(pass_down, 'req', ACROSS)  1.32 us
  transfers between devices with their start and end apart: 13, of which 8 were waited for; matrix products, arithmetic and copies ran while one was open for 0% of the time, Pallas kernels for 2%

profile of v6, /device:TPU:0, one launch (start us, length us, event | category | flops | bytes accessed | tf_op | source)
XLA Modules:
  0.0 54.8 jit_solution(2243539479731607469)
XLA Ops:
  0.0 0.0 copy-start.4
  0.0 0.8 %pad_add_fusion.table = s32[68]{0:T(128)S(1)} fusion(s32[64]{0:T(128)} %param.15, s32[4]{0:T(128)} %ids.1), kind=kLoop, calls=%fused_computation.10 | loop fusion | flops 68 | bytes 544 | tf_op jit(solution)/shard_map/concatenate | solution.py:65
  0.8 0.0 copy-start
  0.8 0.0 copy-start.1
  0.8 0.0 copy-start.2
  0.8 0.8 %shard_map.91 = (bf16[2,896,128]{2,1,0:T(8,128)(2,1)S(1)}, bf16[2,896,128]{2,1,0:T(8,128)(2,1)S(1)}, bf16[2,32,2688]{2,1,0:T(8,128)(2,1)S(1)}, bf16[2,32,2688]{2,1,0:T(8,128)(2,1)S(1)}) custom-call(s32[68]{0:T(128)S(1)} %pad_add_fusion.table, bf16[16,896,128]{2,1,0:T(8,128)(2,1)} %rest_0_.1, bf16[16,32,2688]{2,1,0:T(8,128)(2,1)} %rest_1_.1), custom_call_target="tpu_custom_call" | custom-call | tf_op jit(solution)/shard_map/pallas_call | solution.py:58
  1.6 0.0 copy-start.3
  1.6 1.7 %collective-permute-start = (bf16[2,896,128]{2,1,0:T(8,128)(2,1)S(1)}, bf16[2,896,128]{2,1,0:T(8,128)(2,1)S(1)}, u32[]{:S(2)}, u32[]{:S(2)}) collective-permute-start(bf16[2,896,128]{2,1,0:T(8,128)(2,1)S(1)} %get-tuple-element.18), channel_id=1, source_target_pairs={{0,1},{1,0},{2,3},{3,2},{4,5},{5,4},{6,7},{7,6},{8,9},{9,8},{10,11... | collective-permute-start | bytes 1376264 | tf_op jit(solution)/shard_map/ppermute | solution.py:204
  3.3 0.1 collective-permute-start.6
  3.4 0.0 copy-done.4
  3.4 2.4 %collective-permute-start.2 = (bf16[128,768]{1,0:T(8,128)(2,1)S(1)}, bf16[128,768]{1,0:T(8,128)(2,1)S(1)}, u32[]{:S(2)}, u32[]{:S(2)}) collective-permute-start(bf16[128,768]{1,0:T(8,128)(2,1)S(1)} %bitcast.18), channel_id=1, source_target_pairs={{0,4},{4,0},{8,12},{12,8},{1,5},{5,1},{9,13},{13,9},{2,6},{6,2},{1... | collective-permute-start | bytes 589832 | tf_op jit(solution)/shard_map/ppermute | solution.py:76
  5.8 2.6 %collective-permute-start.3 = (bf16[128,768]{1,0:T(8,128)(2,1)S(1)}, bf16[128,768]{1,0:T(8,128)(2,1)S(1)}, u32[]{:S(2)}, u32[]{:S(2)}) collective-permute-start(bf16[128,768]{1,0:T(8,128)(2,1)S(1)} %bitcast.19), channel_id=1, source_target_pairs={{0,8},{4,12},{8,0},{12,4},{1,9},{5,13},{9,1},{13,5},{2,10},{6,14},... | collective-permute-start | bytes 589832 | tf_op jit(solution)/shard_map/ppermute | solution.py:76
  8.4 0.0 collective-permute-done
  8.4 1.3 %collective-permute-start.1 = (bf16[896,128]{1,0:T(8,128)(2,1)S(1)}, bf16[896,128]{1,0:T(8,128)(2,1)S(1)}, u32[]{:S(2)}, u32[]{:S(2)}) collective-permute-start(bf16[896,128]{1,0:T(8,128)(2,1)S(1)} %fusion), channel_id=1, source_target_pairs={{0,2},{1,3},{2,0},{3,1},{4,6},{5,7},{6,4},{7,5},{8,10},{9,11},{10,... | collective-permute-start | bytes 688136 | tf_op jit(solution)/shard_map/ppermute | solution.py:207
  9.8 0.0 collective-permute-done.6
  9.8 0.8 %collective-permute-start.7 = (bf16[32,2688]{1,0:T(8,128)(2,1)S(1)}, bf16[32,2688]{1,0:T(8,128)(2,1)S(1)}, u32[]{:S(2)}, u32[]{:S(2)}) collective-permute-start(bf16[32,2688]{1,0:T(8,128)(2,1)S(1)} %fusion.3), channel_id=1, source_target_pairs={{0,2},{1,3},{2,0},{3,1},{4,6},{5,7},{6,4},{7,5},{8,10},{9,11},{10,... | collective-permute-start | bytes 516104 | tf_op jit(solution)/shard_map/ppermute | solution.py:209
  10.6 0.8 %collective-permute-start.9 = (bf16[128,768]{1,0:T(8,128)(2,1)S(1)}, bf16[128,768]{1,0:T(8,128)(2,1)S(1)}, u32[]{:S(2)}, u32[]{:S(2)}) collective-permute-start(bf16[128,768]{1,0:T(8,128)(2,1)S(1)} %bitcast.20), channel_id=1, source_target_pairs={{0,12},{4,8},{8,4},{12,0},{1,13},{5,9},{9,5},{13,1},{2,14},{6,10},... | collective-permute-start | bytes 589832 | tf_op jit(solution)/shard_map/ppermute | solution.py:208
  11.4 5.6 %collective-permute-done.1 = bf16[896,128]{1,0:T(8,128)(2,1)S(1)} collective-permute-done((bf16[896,128]{1,0:T(8,128)(2,1)S(1)}, bf16[896,128]{1,0:T(8,128)(2,1)S(1)}, u32[]{:S(2)}, u32[]{:S(2)}) %collective-permute-start.1) | collective-permute-done | bytes 229408 | tf_op jit(solution)/shard_map/ppermute | solution.py:207
  17.0 0.0 collective-permute-done.2.rest_1_
  17.0 5.9 %collective-permute-done.3.rest_2_ = bf16[128,768]{1,0:T(8,128)(2,1)S(1)} collective-permute-done((bf16[128,768]{1,0:T(8,128)(2,1)S(1)}, bf16[128,768]{1,0:T(8,128)(2,1)S(1)}, u32[]{:S(2)}, u32[]{:S(2)}) %collective-permute-start.3) | collective-permute-done | bytes 196640 | tf_op jit(solution)/shard_map/ppermute | solution.py:76
  22.9 0.0 collective-permute-start.5
  22.9 0.0 collective-permute-done.7
  23.0 5.6 %collective-permute-start.8 = (bf16[32,2688]{1,0:T(8,128)(2,1)S(1)}, bf16[32,2688]{1,0:T(8,128)(2,1)S(1)}, u32[]{:S(2)}, u32[]{:S(2)}) collective-permute-start(bf16[32,2688]{1,0:T(8,128)(2,1)S(1)} %fusion.5.rest_4_), channel_id=1, source_target_pairs={{0,4},{4,0},{8,12},{12,8},{1,5},{5,1},{9,13},{13,9},{2,6},{6,2},{1... | collective-permute-start | bytes 516104 | tf_op jit(solution)/shard_map/ppermute | solution.py:76
  28.5 0.0 collective-permute-start.11
  28.5 0.2 collective-permute-start.4
  28.7 0.0 collective-permute-done.9.rest_3_
  28.7 8.1 %collective-permute-done.8.rest_5_ = bf16[32,2688]{1,0:T(8,128)(2,1)S(1)} collective-permute-done((bf16[32,2688]{1,0:T(8,128)(2,1)S(1)}, bf16[32,2688]{1,0:T(8,128)(2,1)S(1)}, u32[]{:S(2)}, u32[]{:S(2)}) %collective-permute-start.8) | collective-permute-done | bytes 172064 | tf_op jit(solution)/shard_map/ppermute | solution.py:76
  36.8 3.3 %collective-permute-done.5.rest_2_ = bf16[896,128]{1,0:T(8,128)(2,1)S(1)} collective-permute-done((bf16[896,128]{1,0:T(8,128)(2,1)S(1)}, bf16[896,128]{1,0:T(8,128)(2,1)S(1)}, u32[]{:S(2)}, u32[]{:S(2)}) %collective-permute-start.5) | collective-permute-done | bytes 229408 | tf_op jit(solution)/shard_map/ppermute | solution.py:76
  40.1 0.2 collective-permute-start.10
  40.4 3.3 %collective-permute-done.11.rest_6_ = bf16[32,2688]{1,0:T(8,128)(2,1)S(1)} collective-permute-done((bf16[32,2688]{1,0:T(8,128)(2,1)S(1)}, bf16[32,2688]{1,0:T(8,128)(2,1)S(1)}, u32[]{:S(2)}, u32[]{:S(2)}) %collective-permute-start.11) | collective-permute-done | bytes 172064 | tf_op jit(solution)/shard_map/ppermute | solution.py:76
  43.6 0.0 collective-permute-start.12
  44.3 0.9 %collective-permute-done.4.rest_1_ = bf16[896,128]{1,0:T(8,128)(2,1)S(1)} collective-permute-done((bf16[896,128]{1,0:T(8,128)(2,1)S(1)}, bf16[896,128]{1,0:T(8,128)(2,1)S(1)}, u32[]{:S(2)}, u32[]{:S(2)}) %collective-permute-start.4) | collective-permute-done | bytes 229408 | tf_op jit(solution)/shard_map/ppermute | solution.py:76
  45.2 4.9 %collective-permute-done.10.rest_3_ = bf16[896,128]{1,0:T(8,128)(2,1)S(1)} collective-permute-done((bf16[896,128]{1,0:T(8,128)(2,1)S(1)}, bf16[896,128]{1,0:T(8,128)(2,1)S(1)}, u32[]{:S(2)}, u32[]{:S(2)}) %collective-permute-start.10) | collective-permute-done | bytes 229408 | tf_op jit(solution)/shard_map/ppermute | solution.py:216
  50.1 0.0 copy-done
  50.1 0.0 copy-done.1
  50.1 0.0 copy-done.2
  50.1 0.9 %shard_map.92.low = bf16[128,128]{1,0:T(8,128)(2,1)S(1)} custom-call(s32[4]{0:T(128)S(1)} %copy-done.1, s32[64]{0:T(128)S(1)} %copy-done.2, bf16[128,3584]{1,0:T(8,128)(2,1)S(1)} %bitcast.16, bf16[896,128]{1,0:T(8,128)(2,1)S(1)} %fusion.2.rest_0_, bf16[896,128]{1,0:T(8,128)(2,1)S(1)} %collective-permute-done.4.rest_1_, ...), custom_call_target="tpu_custom_call" | custom-call | flops 134217728 | bytes 4194304 | tf_op jit(solution)/shard_map/pallas_call | solution.py:95
  51.0 1.4 %collective-permute-done.12.rest_7_ = bf16[32,2688]{1,0:T(8,128)(2,1)S(1)} collective-permute-done((bf16[32,2688]{1,0:T(8,128)(2,1)S(1)}, bf16[32,2688]{1,0:T(8,128)(2,1)S(1)}, u32[]{:S(2)}, u32[]{:S(2)}) %collective-permute-start.12) | collective-permute-done | bytes 172064 | tf_op jit(solution)/shard_map/ppermute | solution.py:217
  52.5 0.0 copy-done.3
  52.5 2.3 %shard_map.93 = bf16[128,2688]{1,0:T(8,128)(2,1)} custom-call(s32[1]{0:T(128)S(6)} %copy.10.lengths, bf16[128,2688]{1,0:T(8,128)(2,1)S(1)} %bitcast.17, bf16[128,128]{1,0:T(8,128)(2,1)S(1)} %shard_map.92.low, bf16[128,768]{1,0:T(8,128)(2,1)S(1)} %bitcast.21, bf16[128,768]{1,0:T(8,128)(2,1)S(1)} %collective-permute-done.2.rest_1_, ...), custom_call_target="tpu_custom_call" | custom-call | flops 1073741824 | bytes 4194304 | tf_op jit(solution)/shard_map/pallas_call | solution.py:172
  (4 shorter events, 0.1 us)
Async XLA Ops:
  0.0 3.4 %copy-start.4 = (bf16[1,128,768]{2,1,0:T(8,128)(2,1)S(1)}, bf16[1,128,768]{2,1,0:T(8,128)(2,1)}, u32[]{:S(2)}) copy-start(bf16[1,128,768]{2,1,0:T(8,128)(2,1)} %param.11) | copy-start | bytes 589828
  0.8 49.3 %copy-start = (bf16[1,128,3584]{2,1,0:T(8,128)(2,1)S(1)}, bf16[1,128,3584]{2,1,0:T(8,128)(2,1)}, u32[]{:S(2)}) copy-start(bf16[1,128,3584]{2,1,0:T(8,128)(2,1)} %param.9) | copy-start | bytes 2752516
  0.8 49.3 %copy-start.1 = (s32[4]{0:T(128)S(1)}, s32[4]{0:T(128)}, u32[]{:S(2)}) copy-start(s32[4]{0:T(128)} %ids.1) | copy-start | bytes 52
  0.8 49.3 %copy-start.2 = (s32[64]{0:T(128)S(1)}, s32[64]{0:T(128)}, u32[]{:S(2)}) copy-start(s32[64]{0:T(128)} %ranks.1) | copy-start | bytes 772
  1.6 50.9 %copy-start.3 = (bf16[1,128,2688]{2,1,0:T(8,128)(2,1)S(1)}, bf16[1,128,2688]{2,1,0:T(8,128)(2,1)}, u32[]{:S(2)}) copy-start(bf16[1,128,2688]{2,1,0:T(8,128)(2,1)} %param.10) | copy-start | bytes 2064388
  1.6 6.8 %collective-permute-start = (bf16[2,896,128]{2,1,0:T(8,128)(2,1)S(1)}, bf16[2,896,128]{2,1,0:T(8,128)(2,1)S(1)}, u32[]{:S(2)}, u32[]{:S(2)}) collective-permute-start(bf16[2,896,128]{2,1,0:T(8,128)(2,1)S(1)} %get-tuple-element.18), channel_id=1, source_target_pairs={{0,1},{1,0},{2,3},{3,2},{4,5},{5,4},{6,7},{7,6},{8,9},{9,8},{10,11... | collective-permute-start | bytes 1376264 | tf_op jit(solution)/shard_map/ppermute | solution.py:204
  3.3 6.4 %collective-permute-start.6 = (bf16[2,32,2688]{2,1,0:T(8,128)(2,1)S(1)}, bf16[2,32,2688]{2,1,0:T(8,128)(2,1)S(1)}, u32[]{:S(2)}, u32[]{:S(2)}) collective-permute-start(bf16[2,32,2688]{2,1,0:T(8,128)(2,1)S(1)} %get-tuple-element.22), channel_id=1, source_target_pairs={{0,1},{1,0},{2,3},{3,2},{4,5},{5,4},{6,7},{7,6},{8,9},{9,8},{10,11... | collective-permute-start | bytes 1032200 | tf_op jit(solution)/shard_map/ppermute | solution.py:205
  3.4 13.6 %collective-permute-start.2 = (bf16[128,768]{1,0:T(8,128)(2,1)S(1)}, bf16[128,768]{1,0:T(8,128)(2,1)S(1)}, u32[]{:S(2)}, u32[]{:S(2)}) collective-permute-start(bf16[128,768]{1,0:T(8,128)(2,1)S(1)} %bitcast.18), channel_id=1, source_target_pairs={{0,4},{4,0},{8,12},{12,8},{1,5},{5,1},{9,13},{13,9},{2,6},{6,2},{1... | collective-permute-start | bytes 589832 | tf_op jit(solution)/shard_map/ppermute | solution.py:76
  5.8 17.1 %collective-permute-start.3 = (bf16[128,768]{1,0:T(8,128)(2,1)S(1)}, bf16[128,768]{1,0:T(8,128)(2,1)S(1)}, u32[]{:S(2)}, u32[]{:S(2)}) collective-permute-start(bf16[128,768]{1,0:T(8,128)(2,1)S(1)} %bitcast.19), channel_id=1, source_target_pairs={{0,8},{4,12},{8,0},{12,4},{1,9},{5,13},{9,1},{13,5},{2,10},{6,14},... | collective-permute-start | bytes 589832 | tf_op jit(solution)/shard_map/ppermute | solution.py:76
  8.4 8.6 %collective-permute-start.1 = (bf16[896,128]{1,0:T(8,128)(2,1)S(1)}, bf16[896,128]{1,0:T(8,128)(2,1)S(1)}, u32[]{:S(2)}, u32[]{:S(2)}) collective-permute-start(bf16[896,128]{1,0:T(8,128)(2,1)S(1)} %fusion), channel_id=1, source_target_pairs={{0,2},{1,3},{2,0},{3,1},{4,6},{5,7},{6,4},{7,5},{8,10},{9,11},{10,... | collective-permute-start | bytes 688136 | tf_op jit(solution)/shard_map/ppermute | solution.py:207
  9.8 13.1 %collective-permute-start.7 = (bf16[32,2688]{1,0:T(8,128)(2,1)S(1)}, bf16[32,2688]{1,0:T(8,128)(2,1)S(1)}, u32[]{:S(2)}, u32[]{:S(2)}) collective-permute-start(bf16[32,2688]{1,0:T(8,128)(2,1)S(1)} %fusion.3), channel_id=1, source_target_pairs={{0,2},{1,3},{2,0},{3,1},{4,6},{5,7},{6,4},{7,5},{8,10},{9,11},{10,... | collective-permute-start | bytes 516104 | tf_op jit(solution)/shard_map/ppermute | solution.py:209
  10.6 18.1 %collective-permute-start.9 = (bf16[128,768]{1,0:T(8,128)(2,1)S(1)}, bf16[128,768]{1,0:T(8,128)(2,1)S(1)}, u32[]{:S(2)}, u32[]{:S(2)}) collective-permute-start(bf16[128,768]{1,0:T(8,128)(2,1)S(1)} %bitcast.20), channel_id=1, source_target_pairs={{0,12},{4,8},{8,4},{12,0},{1,13},{5,9},{9,5},{13,1},{2,14},{6,10},... | collective-permute-start | bytes 589832 | tf_op jit(solution)/shard_map/ppermute | solution.py:208
  22.9 17.2 %collective-permute-start.5 = (bf16[896,128]{1,0:T(8,128)(2,1)S(1)}, bf16[896,128]{1,0:T(8,128)(2,1)S(1)}, u32[]{:S(2)}, u32[]{:S(2)}) collective-permute-start(bf16[896,128]{1,0:T(8,128)(2,1)S(1)} %fusion.2.rest_0_), channel_id=1, source_target_pairs={{0,8},{4,12},{8,0},{12,4},{1,9},{5,13},{9,1},{13,5},{2,10},{6,14},... | collective-permute-start | bytes 688136 | tf_op jit(solution)/shard_map/ppermute | solution.py:76
  23.0 13.8 %collective-permute-start.8 = (bf16[32,2688]{1,0:T(8,128)(2,1)S(1)}, bf16[32,2688]{1,0:T(8,128)(2,1)S(1)}, u32[]{:S(2)}, u32[]{:S(2)}) collective-permute-start(bf16[32,2688]{1,0:T(8,128)(2,1)S(1)} %fusion.5.rest_4_), channel_id=1, source_target_pairs={{0,4},{4,0},{8,12},{12,8},{1,5},{5,1},{9,13},{13,9},{2,6},{6,2},{1... | collective-permute-start | bytes 516104 | tf_op jit(solution)/shard_map/ppermute | solution.py:76
  28.5 15.1 %collective-permute-start.11 = (bf16[32,2688]{1,0:T(8,128)(2,1)S(1)}, bf16[32,2688]{1,0:T(8,128)(2,1)S(1)}, u32[]{:S(2)}, u32[]{:S(2)}) collective-permute-start(bf16[32,2688]{1,0:T(8,128)(2,1)S(1)} %fusion.5.rest_4_), channel_id=1, source_target_pairs={{0,8},{4,12},{8,0},{12,4},{1,9},{5,13},{9,1},{13,5},{2,10},{6,14},... | collective-permute-start | bytes 516104 | tf_op jit(solution)/shard_map/ppermute | solution.py:76
  28.5 16.6 %collective-permute-start.4 = (bf16[896,128]{1,0:T(8,128)(2,1)S(1)}, bf16[896,128]{1,0:T(8,128)(2,1)S(1)}, u32[]{:S(2)}, u32[]{:S(2)}) collective-permute-start(bf16[896,128]{1,0:T(8,128)(2,1)S(1)} %fusion.2.rest_0_), channel_id=1, source_target_pairs={{0,4},{4,0},{8,12},{12,8},{1,5},{5,1},{9,13},{13,9},{2,6},{6,2},{1... | collective-permute-start | bytes 688136 | tf_op jit(solution)/shard_map/ppermute | solution.py:76
  40.1 9.9 %collective-permute-start.10 = (bf16[896,128]{1,0:T(8,128)(2,1)S(1)}, bf16[896,128]{1,0:T(8,128)(2,1)S(1)}, u32[]{:S(2)}, u32[]{:S(2)}) collective-permute-start(bf16[896,128]{1,0:T(8,128)(2,1)S(1)} %collective-permute-done.5.rest_2_), channel_id=1, source_target_pairs={{0,4},{4,0},{8,12},{12,8},{1,5},{5,1},{9,13},{13,9},{2,6},{6,2},{1... | collective-permute-start | bytes 688136 | tf_op jit(solution)/shard_map/ppermute | solution.py:216
  43.6 8.8 %collective-permute-start.12 = (bf16[32,2688]{1,0:T(8,128)(2,1)S(1)}, bf16[32,2688]{1,0:T(8,128)(2,1)S(1)}, u32[]{:S(2)}, u32[]{:S(2)}) collective-permute-start(bf16[32,2688]{1,0:T(8,128)(2,1)S(1)} %collective-permute-done.11.rest_6_), channel_id=1, source_target_pairs={{0,4},{4,0},{8,12},{12,8},{1,5},{5,1},{9,13},{13,9},{2,6},{6,2},{1... | collective-permute-start | bytes 516104 | tf_op jit(solution)/shard_map/ppermute | solution.py:217

commit v7 on v6

--- a/solution.py
+++ b/solution.py
@@ -69,7 +69,7 @@
 ACROSS = [(0, 2), (1, 3), (2, 0), (3, 1)]
 ONE = [(i, i ^ 1) for i in range(4)]
 TWO = [(i, i ^ 2) for i in range(4)]
-THREE = [(i, i ^ 3) for i in range(4)]
+LAST = [(0, 0), (1, 1), (2, 3), (3, 2)]
 
 
 def spread(shard):
@@ -201,19 +201,19 @@
     )
     kv = kv_base[0]
     kv_one, kv_two = spread(kv)
+    kv_three = lax.ppermute(kv_two, "ctx", LAST)
     near_down = lax.ppermute(give_down, "req", SIBLING)
     near_up = lax.ppermute(give_up, "req", SIBLING)
-    pass_down, kv = lax.optimization_barrier((keep_down[1] + near_down[1], kv))
-    far_down = lax.ppermute(pass_down, "req", ACROSS)
-    kv_three = lax.ppermute(kv, "ctx", THREE)
+    far_down = lax.ppermute(keep_down[1] + near_down[1], "req", ACROSS)
     far_up = lax.ppermute(keep_up[1] + near_up[1], "req", ACROSS)
     down = keep_down[0] + near_down[0] + far_down
-    down, kv_one, kv_two = lax.optimization_barrier((down, kv_one, kv_two))
+    down, kv_one = lax.optimization_barrier((down, kv_one))
     down_one, down_two = spread(down)
     up = keep_up[0] + near_up[0] + far_up
     up_one, up_two = spread(up)
-    down_two, up_one, kv_three = lax.optimization_barrier((down_two, up_one, kv_three))
+    down_two, up_one = lax.optimization_barrier((down_two, up_one))
     down_three = lax.ppermute(down_two, "ctx", ONE)
+    up_two, kv_three = lax.optimization_barrier((up_two, kv_three))
     up_three = lax.ppermute(up_two, "ctx", ONE)
     kvs = [kv, kv_one, kv_two, kv_three]
     downs = [down, down_one, down_two, down_three]

time: 54.8 us -> 51.5 us (0.940)
  the two profiles are of different devices: /device:TPU:0 before, /device:TPU:24 now
where the time goes in v7:
time: 51.5 us; the launch traced here: 51.3 us
  waiting for transfers between devices  32.9 us (64%)
  starting transfers between devices  10.5 us (20%)
  Pallas kernels  6.18 us (12%)
  other arithmetic  0.93 us (2%)
  between operations  0.73 us (1%)
    ppermute x6, waiting for transfers between devices, spread(): return (lax.ppermute(shard, 'ctx', ONE), lax.ppermute(shard, 'ctx', TWO))  11.8 us
    ppermute x1, waiting for transfers between devices, body(): kv_three = lax.ppermute(kv_two, 'ctx', LAST)  6.5 us
    ppermute x1, waiting for transfers between devices, body(): far_down = lax.ppermute(keep_down[1] + near_down[1], 'req', ACROSS)  6.32 us
    ppermute x6, starting transfers between devices, spread(): return (lax.ppermute(shard, 'ctx', ONE), lax.ppermute(shard, 'ctx', TWO))  5.88 us
    ppermute x1, waiting for transfers between devices, body(): down_three = lax.ppermute(down_two, 'ctx', ONE)  4.91 us
    pallas_call x1, Pallas kernels, attend(): pl.pallas_call(attend_kernel, out_shape=jax.ShapeDtypeStruct(base.shape,...  3.37 us
    ppermute x1, waiting for transfers between devices, body(): up_three = lax.ppermute(up_two, 'ctx', ONE)  1.98 us
    ppermute x1, starting transfers between devices, body(): kv_three = lax.ppermute(kv_two, 'ctx', LAST)  1.91 us
  transfers between devices with their start and end apart: 13, of which 10 were waited for; matrix products, arithmetic and copies ran while one was open for 0% of the time, Pallas kernels for 2%

profile of v7, /device:TPU:24, one launch (start us, length us, event | category | flops | bytes accessed | tf_op | source)
XLA Modules:
  0.0 51.3 jit_solution(7293810852810165464)
XLA Ops:
  0.0 0.0 copy-start.4
  0.0 0.8 %pad_add_fusion.table = s32[68]{0:T(128)S(1)} fusion(s32[64]{0:T(128)} %param.15, s32[4]{0:T(128)} %ids.1), kind=kLoop, calls=%fused_computation.10 | loop fusion | flops 68 | bytes 544 | tf_op jit(solution)/shard_map/concatenate | solution.py:65
  0.8 0.0 copy-start
  0.8 0.0 copy-start.1
  0.8 0.0 copy-start.2
  0.8 1.9 %shard_map.91 = (bf16[2,896,128]{2,1,0:T(8,128)(2,1)S(1)}, bf16[2,896,128]{2,1,0:T(8,128)(2,1)S(1)}, bf16[2,32,2688]{2,1,0:T(8,128)(2,1)S(1)}, bf16[2,32,2688]{2,1,0:T(8,128)(2,1)S(1)}) custom-call(s32[68]{0:T(128)S(1)} %pad_add_fusion.table, bf16[16,896,128]{2,1,0:T(8,128)(2,1)} %rest_0_.1, bf16[16,32,2688]{2,1,0:T(8,128)(2,1)} %rest_1_.1), custom_call_target="tpu_custom_call" | custom-call | tf_op jit(solution)/shard_map/pallas_call | solution.py:58
  2.7 0.0 copy-start.3
  2.7 0.1 collective-permute-start
  2.8 0.5 collective-permute-start.5
  3.3 0.0 copy-done.4
  3.3 0.4 collective-permute-start.2
  3.7 0.0 collective-permute-start.9
  3.7 0.8 %collective-permute-done = bf16[2,896,128]{2,1,0:T(8,128)(2,1)S(1)} collective-permute-done((bf16[2,896,128]{2,1,0:T(8,128)(2,1)S(1)}, bf16[2,896,128]{2,1,0:T(8,128)(2,1)S(1)}, u32[]{:S(2)}, u32[]{:S(2)}) %collective-permute-start) | collective-permute-done | bytes 458784 | tf_op jit(solution)/shard_map/ppermute | solution.py:205
  4.6 1.5 %collective-permute-start.1 = (bf16[896,128]{1,0:T(8,128)(2,1)S(1)}, bf16[896,128]{1,0:T(8,128)(2,1)S(1)}, u32[]{:S(2)}, u32[]{:S(2)}) collective-permute-start(bf16[896,128]{1,0:T(8,128)(2,1)S(1)} %fusion), channel_id=1, source_target_pairs={{0,2},{1,3},{2,0},{3,1},{4,6},{5,7},{6,4},{7,5},{8,10},{9,11},{10,... | collective-permute-start | bytes 688136 | tf_op jit(solution)/shard_map/ppermute | solution.py:207
  6.1 0.0 collective-permute-done.5
  6.1 0.7 %collective-permute-start.6 = (bf16[32,2688]{1,0:T(8,128)(2,1)S(1)}, bf16[32,2688]{1,0:T(8,128)(2,1)S(1)}, u32[]{:S(2)}, u32[]{:S(2)}) collective-permute-start(bf16[32,2688]{1,0:T(8,128)(2,1)S(1)} %fusion.3), channel_id=1, source_target_pairs={{0,2},{1,3},{2,0},{3,1},{4,6},{5,7},{6,4},{7,5},{8,10},{9,11},{10,... | collective-permute-start | bytes 516104 | tf_op jit(solution)/shard_map/ppermute | solution.py:208
  6.8 6.3 %collective-permute-done.1 = bf16[896,128]{1,0:T(8,128)(2,1)S(1)} collective-permute-done((bf16[896,128]{1,0:T(8,128)(2,1)S(1)}, bf16[896,128]{1,0:T(8,128)(2,1)S(1)}, u32[]{:S(2)}, u32[]{:S(2)}) %collective-permute-start.1) | collective-permute-done | bytes 229408 | tf_op jit(solution)/shard_map/ppermute | solution.py:207
  13.2 0.0 collective-permute-done.2.rest_1_
  13.2 2.2 %collective-permute-start.4 = (bf16[896,128]{1,0:T(8,128)(2,1)S(1)}, bf16[896,128]{1,0:T(8,128)(2,1)S(1)}, u32[]{:S(2)}, u32[]{:S(2)}) collective-permute-start(bf16[896,128]{1,0:T(8,128)(2,1)S(1)} %fusion.2.rest_0_), channel_id=1, source_target_pairs={{0,8},{4,12},{8,0},{12,4},{1,9},{5,13},{9,1},{13,5},{2,10},{6,14},... | collective-permute-start | bytes 688136 | tf_op jit(solution)/shard_map/ppermute | solution.py:76
  15.4 0.6 %collective-permute-done.6 = bf16[32,2688]{1,0:T(8,128)(2,1)S(1)} collective-permute-done((bf16[32,2688]{1,0:T(8,128)(2,1)S(1)}, bf16[32,2688]{1,0:T(8,128)(2,1)S(1)}, u32[]{:S(2)}, u32[]{:S(2)}) %collective-permute-start.6) | collective-permute-done | bytes 172064 | tf_op jit(solution)/shard_map/ppermute | solution.py:208
  16.0 1.0 %collective-permute-start.7 = (bf16[32,2688]{1,0:T(8,128)(2,1)S(1)}, bf16[32,2688]{1,0:T(8,128)(2,1)S(1)}, u32[]{:S(2)}, u32[]{:S(2)}) collective-permute-start(bf16[32,2688]{1,0:T(8,128)(2,1)S(1)} %fusion.5.rest_4_), channel_id=1, source_target_pairs={{0,4},{4,0},{8,12},{12,8},{1,5},{5,1},{9,13},{13,9},{2,6},{6,2},{1... | collective-permute-start | bytes 516104 | tf_op jit(solution)/shard_map/ppermute | solution.py:76
  17.1 1.4 %collective-permute-done.9.rest_2_ = bf16[128,768]{1,0:T(8,128)(2,1)S(1)} collective-permute-done((bf16[128,768]{1,0:T(8,128)(2,1)S(1)}, bf16[128,768]{1,0:T(8,128)(2,1)S(1)}, u32[]{:S(2)}, u32[]{:S(2)}) %collective-permute-start.9) | collective-permute-done | bytes 196640 | tf_op jit(solution)/shard_map/ppermute | solution.py:76
  18.5 1.9 %collective-permute-start.11 = (bf16[128,768]{1,0:T(8,128)(2,1)S(1)}, bf16[128,768]{1,0:T(8,128)(2,1)S(1)}, u32[]{:S(2)}, u32[]{:S(2)}) collective-permute-start(bf16[128,768]{1,0:T(8,128)(2,1)S(1)} %collective-permute-done.9.rest_2_), channel_id=1, source_target_pairs={{0,0},{4,4},{8,12},{12,8},{1,1},{5,5},{9,13},{13,9},{2,2},{6,6},{1... | collective-permute-start | bytes 589832 | tf_op jit(solution)/shard_map/ppermute | solution.py:204
  20.4 0.1 collective-permute-start.10
  20.5 2.1 %collective-permute-start.3 = (bf16[896,128]{1,0:T(8,128)(2,1)S(1)}, bf16[896,128]{1,0:T(8,128)(2,1)S(1)}, u32[]{:S(2)}, u32[]{:S(2)}) collective-permute-start(bf16[896,128]{1,0:T(8,128)(2,1)S(1)} %fusion.2.rest_0_), channel_id=1, source_target_pairs={{0,4},{4,0},{8,12},{12,8},{1,5},{5,1},{9,13},{13,9},{2,6},{6,2},{1... | collective-permute-start | bytes 688136 | tf_op jit(solution)/shard_map/ppermute | solution.py:76
  22.6 4.2 %collective-permute-done.7.rest_5_ = bf16[32,2688]{1,0:T(8,128)(2,1)S(1)} collective-permute-done((bf16[32,2688]{1,0:T(8,128)(2,1)S(1)}, bf16[32,2688]{1,0:T(8,128)(2,1)S(1)}, u32[]{:S(2)}, u32[]{:S(2)}) %collective-permute-start.7) | collective-permute-done | bytes 172064 | tf_op jit(solution)/shard_map/ppermute | solution.py:76
  26.8 1.8 %collective-permute-done.4.rest_2_ = bf16[896,128]{1,0:T(8,128)(2,1)S(1)} collective-permute-done((bf16[896,128]{1,0:T(8,128)(2,1)S(1)}, bf16[896,128]{1,0:T(8,128)(2,1)S(1)}, u32[]{:S(2)}, u32[]{:S(2)}) %collective-permute-start.4) | collective-permute-done | bytes 229408 | tf_op jit(solution)/shard_map/ppermute | solution.py:76
  28.7 0.0 collective-permute-start.8
  28.7 6.5 %collective-permute-done.11.rest_3_ = bf16[128,768]{1,0:T(8,128)(2,1)S(1)} collective-permute-done((bf16[128,768]{1,0:T(8,128)(2,1)S(1)}, bf16[128,768]{1,0:T(8,128)(2,1)S(1)}, u32[]{:S(2)}, u32[]{:S(2)}) %collective-permute-start.11) | collective-permute-done | bytes 196640 | tf_op jit(solution)/shard_map/ppermute | solution.py:204
  35.2 0.0 collective-permute-done.10.rest_6_
  35.2 0.0 collective-permute-start.12
  35.8 4.3 %collective-permute-done.3.rest_1_ = bf16[896,128]{1,0:T(8,128)(2,1)S(1)} collective-permute-done((bf16[896,128]{1,0:T(8,128)(2,1)S(1)}, bf16[896,128]{1,0:T(8,128)(2,1)S(1)}, u32[]{:S(2)}, u32[]{:S(2)}) %collective-permute-start.3) | collective-permute-done | bytes 229408 | tf_op jit(solution)/shard_map/ppermute | solution.py:76
  40.1 4.9 %collective-permute-done.8.rest_3_ = bf16[896,128]{1,0:T(8,128)(2,1)S(1)} collective-permute-done((bf16[896,128]{1,0:T(8,128)(2,1)S(1)}, bf16[896,128]{1,0:T(8,128)(2,1)S(1)}, u32[]{:S(2)}, u32[]{:S(2)}) %collective-permute-start.8) | collective-permute-done | bytes 229408 | tf_op jit(solution)/shard_map/ppermute | solution.py:215
  45.0 0.0 copy-done
  45.0 0.0 copy-done.1
  45.0 0.0 copy-done.2
  45.0 0.9 %shard_map.92.low = bf16[128,128]{1,0:T(8,128)(2,1)S(1)} custom-call(s32[4]{0:T(128)S(1)} %copy-done.1, s32[64]{0:T(128)S(1)} %copy-done.2, bf16[128,3584]{1,0:T(8,128)(2,1)S(1)} %bitcast.16, bf16[896,128]{1,0:T(8,128)(2,1)S(1)} %fusion.2.rest_0_, bf16[896,128]{1,0:T(8,128)(2,1)S(1)} %collective-permute-done.3.rest_1_, ...), custom_call_target="tpu_custom_call" | custom-call | flops 134217728 | bytes 4194304 | tf_op jit(solution)/shard_map/pallas_call | solution.py:95
  46.0 2.0 %collective-permute-done.12.rest_7_ = bf16[32,2688]{1,0:T(8,128)(2,1)S(1)} collective-permute-done((bf16[32,2688]{1,0:T(8,128)(2,1)S(1)}, bf16[32,2688]{1,0:T(8,128)(2,1)S(1)}, u32[]{:S(2)}, u32[]{:S(2)}) %collective-permute-start.12) | collective-permute-done | bytes 172064 | tf_op jit(solution)/shard_map/ppermute | solution.py:217
  47.9 0.0 copy-done.3
  47.9 3.4 %shard_map.93 = bf16[128,2688]{1,0:T(8,128)(2,1)} custom-call(s32[1]{0:T(128)S(6)} %copy.10.lengths, bf16[128,2688]{1,0:T(8,128)(2,1)S(1)} %bitcast.17, bf16[128,128]{1,0:T(8,128)(2,1)S(1)} %shard_map.92.low, bf16[128,768]{1,0:T(8,128)(2,1)S(1)} %bitcast.20, bf16[128,768]{1,0:T(8,128)(2,1)S(1)} %collective-permute-done.2.rest_1_, ...), custom_call_target="tpu_custom_call" | custom-call | flops 1073741824 | bytes 4194304 | tf_op jit(solution)/shard_map/pallas_call | solution.py:172
  (4 shorter events, 0.1 us)
Async XLA Ops:
  0.0 3.3 %copy-start.4 = (bf16[1,128,768]{2,1,0:T(8,128)(2,1)S(1)}, bf16[1,128,768]{2,1,0:T(8,128)(2,1)}, u32[]{:S(2)}) copy-start(bf16[1,128,768]{2,1,0:T(8,128)(2,1)} %param.11) | copy-start | bytes 589828
  0.8 44.2 %copy-start = (bf16[1,128,3584]{2,1,0:T(8,128)(2,1)S(1)}, bf16[1,128,3584]{2,1,0:T(8,128)(2,1)}, u32[]{:S(2)}) copy-start(bf16[1,128,3584]{2,1,0:T(8,128)(2,1)} %param.9) | copy-start | bytes 2752516
  0.8 44.2 %copy-start.1 = (s32[4]{0:T(128)S(1)}, s32[4]{0:T(128)}, u32[]{:S(2)}) copy-start(s32[4]{0:T(128)} %ids.1) | copy-start | bytes 52
  0.8 44.2 %copy-start.2 = (s32[64]{0:T(128)S(1)}, s32[64]{0:T(128)}, u32[]{:S(2)}) copy-start(s32[64]{0:T(128)} %ranks.1) | copy-start | bytes 772
  2.7 45.3 %copy-start.3 = (bf16[1,128,2688]{2,1,0:T(8,128)(2,1)S(1)}, bf16[1,128,2688]{2,1,0:T(8,128)(2,1)}, u32[]{:S(2)}) copy-start(bf16[1,128,2688]{2,1,0:T(8,128)(2,1)} %param.10) | copy-start | bytes 2064388
  2.7 1.9 %collective-permute-start = (bf16[2,896,128]{2,1,0:T(8,128)(2,1)S(1)}, bf16[2,896,128]{2,1,0:T(8,128)(2,1)S(1)}, u32[]{:S(2)}, u32[]{:S(2)}) collective-permute-start(bf16[2,896,128]{2,1,0:T(8,128)(2,1)S(1)} %get-tuple-element.16), channel_id=1, source_target_pairs={{0,1},{1,0},{2,3},{3,2},{4,5},{5,4},{6,7},{7,6},{8,9},{9,8},{10,11... | collective-permute-start | bytes 1376264 | tf_op jit(solution)/shard_map/ppermute | solution.py:205
  2.8 3.3 %collective-permute-start.5 = (bf16[2,32,2688]{2,1,0:T(8,128)(2,1)S(1)}, bf16[2,32,2688]{2,1,0:T(8,128)(2,1)S(1)}, u32[]{:S(2)}, u32[]{:S(2)}) collective-permute-start(bf16[2,32,2688]{2,1,0:T(8,128)(2,1)S(1)} %get-tuple-element.19), channel_id=1, source_target_pairs={{0,1},{1,0},{2,3},{3,2},{4,5},{5,4},{6,7},{7,6},{8,9},{9,8},{10,11... | collective-permute-start | bytes 1032200 | tf_op jit(solution)/shard_map/ppermute | solution.py:206
  3.3 9.9 %collective-permute-start.2 = (bf16[128,768]{1,0:T(8,128)(2,1)S(1)}, bf16[128,768]{1,0:T(8,128)(2,1)S(1)}, u32[]{:S(2)}, u32[]{:S(2)}) collective-permute-start(bf16[128,768]{1,0:T(8,128)(2,1)S(1)} %bitcast.18), channel_id=1, source_target_pairs={{0,4},{4,0},{8,12},{12,8},{1,5},{5,1},{9,13},{13,9},{2,6},{6,2},{1... | collective-permute-start | bytes 589832 | tf_op jit(solution)/shard_map/ppermute | solution.py:76
  3.7 14.8 %collective-permute-start.9 = (bf16[128,768]{1,0:T(8,128)(2,1)S(1)}, bf16[128,768]{1,0:T(8,128)(2,1)S(1)}, u32[]{:S(2)}, u32[]{:S(2)}) collective-permute-start(bf16[128,768]{1,0:T(8,128)(2,1)S(1)} %bitcast.19), channel_id=1, source_target_pairs={{0,8},{4,12},{8,0},{12,4},{1,9},{5,13},{9,1},{13,5},{2,10},{6,14},... | collective-permute-start | bytes 589832 | tf_op jit(solution)/shard_map/ppermute | solution.py:76
  4.6 8.5 %collective-permute-start.1 = (bf16[896,128]{1,0:T(8,128)(2,1)S(1)}, bf16[896,128]{1,0:T(8,128)(2,1)S(1)}, u32[]{:S(2)}, u32[]{:S(2)}) collective-permute-start(bf16[896,128]{1,0:T(8,128)(2,1)S(1)} %fusion), channel_id=1, source_target_pairs={{0,2},{1,3},{2,0},{3,1},{4,6},{5,7},{6,4},{7,5},{8,10},{9,11},{10,... | collective-permute-start | bytes 688136 | tf_op jit(solution)/shard_map/ppermute | solution.py:207
  6.1 9.9 %collective-permute-start.6 = (bf16[32,2688]{1,0:T(8,128)(2,1)S(1)}, bf16[32,2688]{1,0:T(8,128)(2,1)S(1)}, u32[]{:S(2)}, u32[]{:S(2)}) collective-permute-start(bf16[32,2688]{1,0:T(8,128)(2,1)S(1)} %fusion.3), channel_id=1, source_target_pairs={{0,2},{1,3},{2,0},{3,1},{4,6},{5,7},{6,4},{7,5},{8,10},{9,11},{10,... | collective-permute-start | bytes 516104 | tf_op jit(solution)/shard_map/ppermute | solution.py:208
  13.2 15.5 %collective-permute-start.4 = (bf16[896,128]{1,0:T(8,128)(2,1)S(1)}, bf16[896,128]{1,0:T(8,128)(2,1)S(1)}, u32[]{:S(2)}, u32[]{:S(2)}) collective-permute-start(bf16[896,128]{1,0:T(8,128)(2,1)S(1)} %fusion.2.rest_0_), channel_id=1, source_target_pairs={{0,8},{4,12},{8,0},{12,4},{1,9},{5,13},{9,1},{13,5},{2,10},{6,14},... | collective-permute-start | bytes 688136 | tf_op jit(solution)/shard_map/ppermute | solution.py:76
  16.0 10.8 %collective-permute-start.7 = (bf16[32,2688]{1,0:T(8,128)(2,1)S(1)}, bf16[32,2688]{1,0:T(8,128)(2,1)S(1)}, u32[]{:S(2)}, u32[]{:S(2)}) collective-permute-start(bf16[32,2688]{1,0:T(8,128)(2,1)S(1)} %fusion.5.rest_4_), channel_id=1, source_target_pairs={{0,4},{4,0},{8,12},{12,8},{1,5},{5,1},{9,13},{13,9},{2,6},{6,2},{1... | collective-permute-start | bytes 516104 | tf_op jit(solution)/shard_map/ppermute | solution.py:76
  18.5 16.7 %collective-permute-start.11 = (bf16[128,768]{1,0:T(8,128)(2,1)S(1)}, bf16[128,768]{1,0:T(8,128)(2,1)S(1)}, u32[]{:S(2)}, u32[]{:S(2)}) collective-permute-start(bf16[128,768]{1,0:T(8,128)(2,1)S(1)} %collective-permute-done.9.rest_2_), channel_id=1, source_target_pairs={{0,0},{4,4},{8,12},{12,8},{1,1},{5,5},{9,13},{13,9},{2,2},{6,6},{1... | collective-permute-start | bytes 589832 | tf_op jit(solution)/shard_map/ppermute | solution.py:204
  20.4 14.8 %collective-permute-start.10 = (bf16[32,2688]{1,0:T(8,128)(2,1)S(1)}, bf16[32,2688]{1,0:T(8,128)(2,1)S(1)}, u32[]{:S(2)}, u32[]{:S(2)}) collective-permute-start(bf16[32,2688]{1,0:T(8,128)(2,1)S(1)} %fusion.5.rest_4_), channel_id=1, source_target_pairs={{0,8},{4,12},{8,0},{12,4},{1,9},{5,13},{9,1},{13,5},{2,10},{6,14},... | collective-permute-start | bytes 516104 | tf_op jit(solution)/shard_map/ppermute | solution.py:76
  20.5 19.6 %collective-permute-start.3 = (bf16[896,128]{1,0:T(8,128)(2,1)S(1)}, bf16[896,128]{1,0:T(8,128)(2,1)S(1)}, u32[]{:S(2)}, u32[]{:S(2)}) collective-permute-start(bf16[896,128]{1,0:T(8,128)(2,1)S(1)} %fusion.2.rest_0_), channel_id=1, source_target_pairs={{0,4},{4,0},{8,12},{12,8},{1,5},{5,1},{9,13},{13,9},{2,6},{6,2},{1... | collective-permute-start | bytes 688136 | tf_op jit(solution)/shard_map/ppermute | solution.py:76
  28.7 16.3 %collective-permute-start.8 = (bf16[896,128]{1,0:T(8,128)(2,1)S(1)}, bf16[896,128]{1,0:T(8,128)(2,1)S(1)}, u32[]{:S(2)}, u32[]{:S(2)}) collective-permute-start(bf16[896,128]{1,0:T(8,128)(2,1)S(1)} %collective-permute-done.4.rest_2_), channel_id=1, source_target_pairs={{0,4},{4,0},{8,12},{12,8},{1,5},{5,1},{9,13},{13,9},{2,6},{6,2},{1... | collective-permute-start | bytes 688136 | tf_op jit(solution)/shard_map/ppermute | solution.py:215
  35.2 12.8 %collective-permute-start.12 = (bf16[32,2688]{1,0:T(8,128)(2,1)S(1)}, bf16[32,2688]{1,0:T(8,128)(2,1)S(1)}, u32[]{:S(2)}, u32[]{:S(2)}) collective-permute-start(bf16[32,2688]{1,0:T(8,128)(2,1)S(1)} %collective-permute-done.10.rest_6_), channel_id=1, source_target_pairs={{0,4},{4,0},{8,12},{12,8},{1,5},{5,1},{9,13},{13,9},{2,6},{6,2},{1... | collective-permute-start | bytes 516104 | tf_op jit(solution)/shard_map/ppermute | solution.py:217

commit v8 on v7

--- a/solution.py
+++ b/solution.py
@@ -211,9 +211,9 @@
     down_one, down_two = spread(down)
     up = keep_up[0] + near_up[0] + far_up
     up_one, up_two = spread(up)
-    down_two, up_one = lax.optimization_barrier((down_two, up_one))
+    down_two, down_one = lax.optimization_barrier((down_two, down_one))
     down_three = lax.ppermute(down_two, "ctx", ONE)
-    up_two, kv_three = lax.optimization_barrier((up_two, kv_three))
+    up_two, up_one = lax.optimization_barrier((up_two, up_one))
     up_three = lax.ppermute(up_two, "ctx", ONE)
     kvs = [kv, kv_one, kv_two, kv_three]
     downs = [down, down_one, down_two, down_three]

time: 51.5 us -> 49.1 us (0.953)
  waiting for transfers between devices: 32.9 us -> 26.7 us
  starting transfers between devices: 10.5 us -> 14.4 us
    ppermute x1, waiting for transfers between devices: 6.5 us -> 3.25 us  [body(): kv_three = lax.ppermute(kv_two, 'ctx', LAST)]
    ppermute x1, waiting for transfers between devices: 4.91 us -> 2.96 us  [body(): down_three = lax.ppermute(down_two, 'ctx', ONE)]
    ppermute x1, starting transfers between devices: 0.01 us -> 1.3 us  [body(): up_three = lax.ppermute(up_two, 'ctx', ONE)]
    ppermute x1, starting transfers between devices: 0.01 us -> 1.08 us  [body(): down_three = lax.ppermute(down_two, 'ctx', ONE)]
    ppermute x1, starting transfers between devices: 1.91 us -> 2.88 us  [body(): kv_three = lax.ppermute(kv_two, 'ctx', LAST)]
    ppermute x6, waiting for transfers between devices: 11.8 us -> 10.8 us  [spread(): return (lax.ppermute(shard, 'ctx', ONE), lax.ppermute(shard, 'ctx', TWO))]
    ppermute x1, waiting for transfers between devices: 0.6 us -> 0.01 us  [body(): far_up = lax.ppermute(keep_up[1] + near_up[1], 'req', ACROSS)]
  transfers between devices with their start and end apart: 13 -> 13, of which waited for: 10 -> 8; matrix products, arithmetic and copies ran while one was open for 0% -> 0% of each run, Pallas kernels for 2% -> 2%
where the time goes in v8:
time: 49.1 us; the launch traced here: 48.8 us
  waiting for transfers between devices  26.7 us (54%)
  starting transfers between devices  14.4 us (29%)
  Pallas kernels  6.1 us (12%)
  other arithmetic  0.93 us (2%)
  between operations  0.72 us (1%)
    ppermute x6, waiting for transfers between devices, spread(): return (lax.ppermute(shard, 'ctx', ONE), lax.ppermute(shard, 'ctx', TWO))  10.8 us
    ppermute x6, starting transfers between devices, spread(): return (lax.ppermute(shard, 'ctx', ONE), lax.ppermute(shard, 'ctx', TWO))  6.37 us
    ppermute x1, waiting for transfers between devices, body(): far_down = lax.ppermute(keep_down[1] + near_down[1], 'req', ACROSS)  6.32 us
    pallas_call x1, Pallas kernels, attend(): pl.pallas_call(attend_kernel, out_shape=jax.ShapeDtypeStruct(base.shape,...  3.37 us
    ppermute x1, waiting for transfers between devices, body(): kv_three = lax.ppermute(kv_two, 'ctx', LAST)  3.25 us
    ppermute x1, waiting for transfers between devices, body(): down_three = lax.ppermute(down_two, 'ctx', ONE)  2.96 us
    ppermute x1, starting transfers between devices, body(): kv_three = lax.ppermute(kv_two, 'ctx', LAST)  2.88 us
    ppermute x1, waiting for transfers between devices, body(): up_three = lax.ppermute(up_two, 'ctx', ONE)  2.5 us
  transfers between devices with their start and end apart: 13, of which 8 were waited for; matrix products, arithmetic and copies ran while one was open for 0% of the time, Pallas kernels for 2%

profile of v8, /device:TPU:24, one launch (start us, length us, event | category | flops | bytes accessed | tf_op | source)
XLA Modules:
  0.0 48.8 jit_solution(15715338102982908948)
XLA Ops:
  0.0 0.0 copy-start.4
  0.0 0.8 %pad_add_fusion.table = s32[68]{0:T(128)S(1)} fusion(s32[64]{0:T(128)} %param.15, s32[4]{0:T(128)} %ids.1), kind=kLoop, calls=%fused_computation.10 | loop fusion | flops 68 | bytes 544 | tf_op jit(solution)/shard_map/concatenate | solution.py:65
  0.8 0.0 copy-start
  0.8 0.0 copy-start.1
  0.8 0.0 copy-start.2
  0.8 1.8 %shard_map.91 = (bf16[2,896,128]{2,1,0:T(8,128)(2,1)S(1)}, bf16[2,896,128]{2,1,0:T(8,128)(2,1)S(1)}, bf16[2,32,2688]{2,1,0:T(8,128)(2,1)S(1)}, bf16[2,32,2688]{2,1,0:T(8,128)(2,1)S(1)}) custom-call(s32[68]{0:T(128)S(1)} %pad_add_fusion.table, bf16[16,896,128]{2,1,0:T(8,128)(2,1)} %rest_0_.1, bf16[16,32,2688]{2,1,0:T(8,128)(2,1)} %rest_1_.1), custom_call_target="tpu_custom_call" | custom-call | tf_op jit(solution)/shard_map/pallas_call | solution.py:58
  2.6 0.0 copy-start.3
  2.6 0.1 collective-permute-start
  2.7 0.5 %collective-permute-start.8 = (bf16[2,32,2688]{2,1,0:T(8,128)(2,1)S(1)}, bf16[2,32,2688]{2,1,0:T(8,128)(2,1)S(1)}, u32[]{:S(2)}, u32[]{:S(2)}) collective-permute-start(bf16[2,32,2688]{2,1,0:T(8,128)(2,1)S(1)} %get-tuple-element.22), channel_id=1, source_target_pairs={{0,1},{1,0},{2,3},{3,2},{4,5},{5,4},{6,7},{7,6},{8,9},{9,8},{10,11... | collective-permute-start | bytes 1032200 | tf_op jit(solution)/shard_map/ppermute | solution.py:206
  3.2 0.0 copy-done.4
  3.2 0.4 collective-permute-start.2
  3.6 0.0 collective-permute-start.6
  3.6 0.8 %collective-permute-done = bf16[2,896,128]{2,1,0:T(8,128)(2,1)S(1)} collective-permute-done((bf16[2,896,128]{2,1,0:T(8,128)(2,1)S(1)}, bf16[2,896,128]{2,1,0:T(8,128)(2,1)S(1)}, u32[]{:S(2)}, u32[]{:S(2)}) %collective-permute-start) | collective-permute-done | bytes 458784 | tf_op jit(solution)/shard_map/ppermute | solution.py:205
  4.5 1.5 %collective-permute-start.1 = (bf16[896,128]{1,0:T(8,128)(2,1)S(1)}, bf16[896,128]{1,0:T(8,128)(2,1)S(1)}, u32[]{:S(2)}, u32[]{:S(2)}) collective-permute-start(bf16[896,128]{1,0:T(8,128)(2,1)S(1)} %fusion), channel_id=1, source_target_pairs={{0,2},{1,3},{2,0},{3,1},{4,6},{5,7},{6,4},{7,5},{8,10},{9,11},{10,... | collective-permute-start | bytes 688136 | tf_op jit(solution)/shard_map/ppermute | solution.py:207
  6.0 0.0 collective-permute-done.8
  6.0 0.7 %collective-permute-start.9 = (bf16[32,2688]{1,0:T(8,128)(2,1)S(1)}, bf16[32,2688]{1,0:T(8,128)(2,1)S(1)}, u32[]{:S(2)}, u32[]{:S(2)}) collective-permute-start(bf16[32,2688]{1,0:T(8,128)(2,1)S(1)} %fusion.3), channel_id=1, source_target_pairs={{0,2},{1,3},{2,0},{3,1},{4,6},{5,7},{6,4},{7,5},{8,10},{9,11},{10,... | collective-permute-start | bytes 516104 | tf_op jit(solution)/shard_map/ppermute | solution.py:208
  6.7 6.3 %collective-permute-done.1 = bf16[896,128]{1,0:T(8,128)(2,1)S(1)} collective-permute-done((bf16[896,128]{1,0:T(8,128)(2,1)S(1)}, bf16[896,128]{1,0:T(8,128)(2,1)S(1)}, u32[]{:S(2)}, u32[]{:S(2)}) %collective-permute-start.1) | collective-permute-done | bytes 229408 | tf_op jit(solution)/shard_map/ppermute | solution.py:207
  13.1 0.0 collective-permute-done.2.rest_1_
  13.1 2.2 %collective-permute-start.3 = (bf16[896,128]{1,0:T(8,128)(2,1)S(1)}, bf16[896,128]{1,0:T(8,128)(2,1)S(1)}, u32[]{:S(2)}, u32[]{:S(2)}) collective-permute-start(bf16[896,128]{1,0:T(8,128)(2,1)S(1)} %fusion.2.rest_0_), channel_id=1, source_target_pairs={{0,8},{4,12},{8,0},{12,4},{1,9},{5,13},{9,1},{13,5},{2,10},{6,14},... | collective-permute-start | bytes 688136 | tf_op jit(solution)/shard_map/ppermute | solution.py:76
  15.3 1.6 %collective-permute-start.4 = (bf16[896,128]{1,0:T(8,128)(2,1)S(1)}, bf16[896,128]{1,0:T(8,128)(2,1)S(1)}, u32[]{:S(2)}, u32[]{:S(2)}) collective-permute-start(bf16[896,128]{1,0:T(8,128)(2,1)S(1)} %fusion.2.rest_0_), channel_id=1, source_target_pairs={{0,4},{4,0},{8,12},{12,8},{1,5},{5,1},{9,13},{13,9},{2,6},{6,2},{1... | collective-permute-start | bytes 688136 | tf_op jit(solution)/shard_map/ppermute | solution.py:76
  16.9 0.0 collective-permute-done.9
  16.9 0.5 %collective-permute-start.10 = (bf16[32,2688]{1,0:T(8,128)(2,1)S(1)}, bf16[32,2688]{1,0:T(8,128)(2,1)S(1)}, u32[]{:S(2)}, u32[]{:S(2)}) collective-permute-start(bf16[32,2688]{1,0:T(8,128)(2,1)S(1)} %fusion.5.rest_4_), channel_id=1, source_target_pairs={{0,8},{4,12},{8,0},{12,4},{1,9},{5,13},{9,1},{13,5},{2,10},{6,14},... | collective-permute-start | bytes 516104 | tf_op jit(solution)/shard_map/ppermute | solution.py:76
  17.5 1.6 %collective-permute-start.11 = (bf16[32,2688]{1,0:T(8,128)(2,1)S(1)}, bf16[32,2688]{1,0:T(8,128)(2,1)S(1)}, u32[]{:S(2)}, u32[]{:S(2)}) collective-permute-start(bf16[32,2688]{1,0:T(8,128)(2,1)S(1)} %fusion.5.rest_4_), channel_id=1, source_target_pairs={{0,4},{4,0},{8,12},{12,8},{1,5},{5,1},{9,13},{13,9},{2,6},{6,2},{1... | collective-permute-start | bytes 516104 | tf_op jit(solution)/shard_map/ppermute | solution.py:76
  19.1 8.6 %collective-permute-done.3.rest_2_ = bf16[896,128]{1,0:T(8,128)(2,1)S(1)} collective-permute-done((bf16[896,128]{1,0:T(8,128)(2,1)S(1)}, bf16[896,128]{1,0:T(8,128)(2,1)S(1)}, u32[]{:S(2)}, u32[]{:S(2)}) %collective-permute-start.3) | collective-permute-done | bytes 229408 | tf_op jit(solution)/shard_map/ppermute | solution.py:76
  27.6 0.0 collective-permute-done.4.rest_1_
  27.6 1.1 %collective-permute-start.5 = (bf16[896,128]{1,0:T(8,128)(2,1)S(1)}, bf16[896,128]{1,0:T(8,128)(2,1)S(1)}, u32[]{:S(2)}, u32[]{:S(2)}) collective-permute-start(bf16[896,128]{1,0:T(8,128)(2,1)S(1)} %collective-permute-done.3.rest_2_), channel_id=1, source_target_pairs={{0,4},{4,0},{8,12},{12,8},{1,5},{5,1},{9,13},{13,9},{2,6},{6,2},{1... | collective-permute-start | bytes 688136 | tf_op jit(solution)/shard_map/ppermute | solution.py:215
  28.7 0.0 collective-permute-done.6.rest_2_
  28.7 2.9 %collective-permute-start.7 = (bf16[128,768]{1,0:T(8,128)(2,1)S(1)}, bf16[128,768]{1,0:T(8,128)(2,1)S(1)}, u32[]{:S(2)}, u32[]{:S(2)}) collective-permute-start(bf16[128,768]{1,0:T(8,128)(2,1)S(1)} %collective-permute-done.6.rest_2_), channel_id=1, source_target_pairs={{0,0},{4,4},{8,12},{12,8},{1,1},{5,5},{9,13},{13,9},{2,2},{6,6},{1... | collective-permute-start | bytes 589832 | tf_op jit(solution)/shard_map/ppermute | solution.py:204
  31.6 1.1 %collective-permute-done.10.rest_6_ = bf16[32,2688]{1,0:T(8,128)(2,1)S(1)} collective-permute-done((bf16[32,2688]{1,0:T(8,128)(2,1)S(1)}, bf16[32,2688]{1,0:T(8,128)(2,1)S(1)}, u32[]{:S(2)}, u32[]{:S(2)}) %collective-permute-start.10) | collective-permute-done | bytes 172064 | tf_op jit(solution)/shard_map/ppermute | solution.py:76
  32.7 1.2 %collective-permute-done.11.rest_5_ = bf16[32,2688]{1,0:T(8,128)(2,1)S(1)} collective-permute-done((bf16[32,2688]{1,0:T(8,128)(2,1)S(1)}, bf16[32,2688]{1,0:T(8,128)(2,1)S(1)}, u32[]{:S(2)}, u32[]{:S(2)}) %collective-permute-start.11) | collective-permute-done | bytes 172064 | tf_op jit(solution)/shard_map/ppermute | solution.py:76
  33.9 1.3 %collective-permute-start.12 = (bf16[32,2688]{1,0:T(8,128)(2,1)S(1)}, bf16[32,2688]{1,0:T(8,128)(2,1)S(1)}, u32[]{:S(2)}, u32[]{:S(2)}) collective-permute-start(bf16[32,2688]{1,0:T(8,128)(2,1)S(1)} %collective-permute-done.10.rest_6_), channel_id=1, source_target_pairs={{0,4},{4,0},{8,12},{12,8},{1,5},{5,1},{9,13},{13,9},{2,6},{6,2},{1... | collective-permute-start | bytes 516104 | tf_op jit(solution)/shard_map/ppermute | solution.py:217
  35.8 3.0 %collective-permute-done.5.rest_3_ = bf16[896,128]{1,0:T(8,128)(2,1)S(1)} collective-permute-done((bf16[896,128]{1,0:T(8,128)(2,1)S(1)}, bf16[896,128]{1,0:T(8,128)(2,1)S(1)}, u32[]{:S(2)}, u32[]{:S(2)}) %collective-permute-start.5) | collective-permute-done | bytes 229408 | tf_op jit(solution)/shard_map/ppermute | solution.py:215
  38.8 0.0 copy-done
  38.8 0.0 copy-done.1
  38.8 0.0 copy-done.2
  38.8 0.9 %shard_map.92.low = bf16[128,128]{1,0:T(8,128)(2,1)S(1)} custom-call(s32[4]{0:T(128)S(1)} %copy-done.1, s32[64]{0:T(128)S(1)} %copy-done.2, bf16[128,3584]{1,0:T(8,128)(2,1)S(1)} %bitcast.16, bf16[896,128]{1,0:T(8,128)(2,1)S(1)} %fusion.2.rest_0_, bf16[896,128]{1,0:T(8,128)(2,1)S(1)} %collective-permute-done.4.rest_1_, ...), custom_call_target="tpu_custom_call" | custom-call | flops 134217728 | bytes 4194304 | tf_op jit(solution)/shard_map/pallas_call | solution.py:95
  39.7 3.3 %collective-permute-done.7.rest_3_ = bf16[128,768]{1,0:T(8,128)(2,1)S(1)} collective-permute-done((bf16[128,768]{1,0:T(8,128)(2,1)S(1)}, bf16[128,768]{1,0:T(8,128)(2,1)S(1)}, u32[]{:S(2)}, u32[]{:S(2)}) %collective-permute-start.7) | collective-permute-done | bytes 196640 | tf_op jit(solution)/shard_map/ppermute | solution.py:204
  43.0 2.5 %collective-permute-done.12.rest_7_ = bf16[32,2688]{1,0:T(8,128)(2,1)S(1)} collective-permute-done((bf16[32,2688]{1,0:T(8,128)(2,1)S(1)}, bf16[32,2688]{1,0:T(8,128)(2,1)S(1)}, u32[]{:S(2)}, u32[]{:S(2)}) %collective-permute-start.12) | collective-permute-done | bytes 172064 | tf_op jit(solution)/shard_map/ppermute | solution.py:217
  45.5 0.0 copy-done.3
  45.5 3.4 %shard_map.93 = bf16[128,2688]{1,0:T(8,128)(2,1)} custom-call(s32[1]{0:T(128)S(6)} %copy.10.lengths, bf16[128,2688]{1,0:T(8,128)(2,1)S(1)} %bitcast.17, bf16[128,128]{1,0:T(8,128)(2,1)S(1)} %shard_map.92.low, bf16[128,768]{1,0:T(8,128)(2,1)S(1)} %bitcast.20, bf16[128,768]{1,0:T(8,128)(2,1)S(1)} %collective-permute-done.2.rest_1_, ...), custom_call_target="tpu_custom_call" | custom-call | flops 1073741824 | bytes 4194304 | tf_op jit(solution)/shard_map/pallas_call | solution.py:172
  (4 shorter events, 0.1 us)
Async XLA Ops:
  0.0 3.2 %copy-start.4 = (bf16[1,128,768]{2,1,0:T(8,128)(2,1)S(1)}, bf16[1,128,768]{2,1,0:T(8,128)(2,1)}, u32[]{:S(2)}) copy-start(bf16[1,128,768]{2,1,0:T(8,128)(2,1)} %param.11) | copy-start | bytes 589828
  0.8 38.0 %copy-start = (bf16[1,128,3584]{2,1,0:T(8,128)(2,1)S(1)}, bf16[1,128,3584]{2,1,0:T(8,128)(2,1)}, u32[]{:S(2)}) copy-start(bf16[1,128,3584]{2,1,0:T(8,128)(2,1)} %param.9) | copy-start | bytes 2752516
  0.8 38.0 %copy-start.1 = (s32[4]{0:T(128)S(1)}, s32[4]{0:T(128)}, u32[]{:S(2)}) copy-start(s32[4]{0:T(128)} %ids.1) | copy-start | bytes 52
  0.8 38.0 %copy-start.2 = (s32[64]{0:T(128)S(1)}, s32[64]{0:T(128)}, u32[]{:S(2)}) copy-start(s32[64]{0:T(128)} %ranks.1) | copy-start | bytes 772
  2.6 42.9 %copy-start.3 = (bf16[1,128,2688]{2,1,0:T(8,128)(2,1)S(1)}, bf16[1,128,2688]{2,1,0:T(8,128)(2,1)}, u32[]{:S(2)}) copy-start(bf16[1,128,2688]{2,1,0:T(8,128)(2,1)} %param.10) | copy-start | bytes 2064388
  2.6 1.9 %collective-permute-start = (bf16[2,896,128]{2,1,0:T(8,128)(2,1)S(1)}, bf16[2,896,128]{2,1,0:T(8,128)(2,1)S(1)}, u32[]{:S(2)}, u32[]{:S(2)}) collective-permute-start(bf16[2,896,128]{2,1,0:T(8,128)(2,1)S(1)} %get-tuple-element.16), channel_id=1, source_target_pairs={{0,1},{1,0},{2,3},{3,2},{4,5},{5,4},{6,7},{7,6},{8,9},{9,8},{10,11... | collective-permute-start | bytes 1376264 | tf_op jit(solution)/shard_map/ppermute | solution.py:205
  2.7 3.3 %collective-permute-start.8 = (bf16[2,32,2688]{2,1,0:T(8,128)(2,1)S(1)}, bf16[2,32,2688]{2,1,0:T(8,128)(2,1)S(1)}, u32[]{:S(2)}, u32[]{:S(2)}) collective-permute-start(bf16[2,32,2688]{2,1,0:T(8,128)(2,1)S(1)} %get-tuple-element.22), channel_id=1, source_target_pairs={{0,1},{1,0},{2,3},{3,2},{4,5},{5,4},{6,7},{7,6},{8,9},{9,8},{10,11... | collective-permute-start | bytes 1032200 | tf_op jit(solution)/shard_map/ppermute | solution.py:206
  3.2 9.9 %collective-permute-start.2 = (bf16[128,768]{1,0:T(8,128)(2,1)S(1)}, bf16[128,768]{1,0:T(8,128)(2,1)S(1)}, u32[]{:S(2)}, u32[]{:S(2)}) collective-permute-start(bf16[128,768]{1,0:T(8,128)(2,1)S(1)} %bitcast.18), channel_id=1, source_target_pairs={{0,4},{4,0},{8,12},{12,8},{1,5},{5,1},{9,13},{13,9},{2,6},{6,2},{1... | collective-permute-start | bytes 589832 | tf_op jit(solution)/shard_map/ppermute | solution.py:76
  3.6 25.1 %collective-permute-start.6 = (bf16[128,768]{1,0:T(8,128)(2,1)S(1)}, bf16[128,768]{1,0:T(8,128)(2,1)S(1)}, u32[]{:S(2)}, u32[]{:S(2)}) collective-permute-start(bf16[128,768]{1,0:T(8,128)(2,1)S(1)} %bitcast.19), channel_id=1, source_target_pairs={{0,8},{4,12},{8,0},{12,4},{1,9},{5,13},{9,1},{13,5},{2,10},{6,14},... | collective-permute-start | bytes 589832 | tf_op jit(solution)/shard_map/ppermute | solution.py:76
  4.5 8.5 %collective-permute-start.1 = (bf16[896,128]{1,0:T(8,128)(2,1)S(1)}, bf16[896,128]{1,0:T(8,128)(2,1)S(1)}, u32[]{:S(2)}, u32[]{:S(2)}) collective-permute-start(bf16[896,128]{1,0:T(8,128)(2,1)S(1)} %fusion), channel_id=1, source_target_pairs={{0,2},{1,3},{2,0},{3,1},{4,6},{5,7},{6,4},{7,5},{8,10},{9,11},{10,... | collective-permute-start | bytes 688136 | tf_op jit(solution)/shard_map/ppermute | solution.py:207
  6.0 10.9 %collective-permute-start.9 = (bf16[32,2688]{1,0:T(8,128)(2,1)S(1)}, bf16[32,2688]{1,0:T(8,128)(2,1)S(1)}, u32[]{:S(2)}, u32[]{:S(2)}) collective-permute-start(bf16[32,2688]{1,0:T(8,128)(2,1)S(1)} %fusion.3), channel_id=1, source_target_pairs={{0,2},{1,3},{2,0},{3,1},{4,6},{5,7},{6,4},{7,5},{8,10},{9,11},{10,... | collective-permute-start | bytes 516104 | tf_op jit(solution)/shard_map/ppermute | solution.py:208
  13.1 14.6 %collective-permute-start.3 = (bf16[896,128]{1,0:T(8,128)(2,1)S(1)}, bf16[896,128]{1,0:T(8,128)(2,1)S(1)}, u32[]{:S(2)}, u32[]{:S(2)}) collective-permute-start(bf16[896,128]{1,0:T(8,128)(2,1)S(1)} %fusion.2.rest_0_), channel_id=1, source_target_pairs={{0,8},{4,12},{8,0},{12,4},{1,9},{5,13},{9,1},{13,5},{2,10},{6,14},... | collective-permute-start | bytes 688136 | tf_op jit(solution)/shard_map/ppermute | solution.py:76
  15.3 12.3 %collective-permute-start.4 = (bf16[896,128]{1,0:T(8,128)(2,1)S(1)}, bf16[896,128]{1,0:T(8,128)(2,1)S(1)}, u32[]{:S(2)}, u32[]{:S(2)}) collective-permute-start(bf16[896,128]{1,0:T(8,128)(2,1)S(1)} %fusion.2.rest_0_), channel_id=1, source_target_pairs={{0,4},{4,0},{8,12},{12,8},{1,5},{5,1},{9,13},{13,9},{2,6},{6,2},{1... | collective-permute-start | bytes 688136 | tf_op jit(solution)/shard_map/ppermute | solution.py:76
  16.9 15.8 %collective-permute-start.10 = (bf16[32,2688]{1,0:T(8,128)(2,1)S(1)}, bf16[32,2688]{1,0:T(8,128)(2,1)S(1)}, u32[]{:S(2)}, u32[]{:S(2)}) collective-permute-start(bf16[32,2688]{1,0:T(8,128)(2,1)S(1)} %fusion.5.rest_4_), channel_id=1, source_target_pairs={{0,8},{4,12},{8,0},{12,4},{1,9},{5,13},{9,1},{13,5},{2,10},{6,14},... | collective-permute-start | bytes 516104 | tf_op jit(solution)/shard_map/ppermute | solution.py:76
  17.5 16.4 %collective-permute-start.11 = (bf16[32,2688]{1,0:T(8,128)(2,1)S(1)}, bf16[32,2688]{1,0:T(8,128)(2,1)S(1)}, u32[]{:S(2)}, u32[]{:S(2)}) collective-permute-start(bf16[32,2688]{1,0:T(8,128)(2,1)S(1)} %fusion.5.rest_4_), channel_id=1, source_target_pairs={{0,4},{4,0},{8,12},{12,8},{1,5},{5,1},{9,13},{13,9},{2,6},{6,2},{1... | collective-permute-start | bytes 516104 | tf_op jit(solution)/shard_map/ppermute | solution.py:76
  27.6 11.1 %collective-permute-start.5 = (bf16[896,128]{1,0:T(8,128)(2,1)S(1)}, bf16[896,128]{1,0:T(8,128)(2,1)S(1)}, u32[]{:S(2)}, u32[]{:S(2)}) collective-permute-start(bf16[896,128]{1,0:T(8,128)(2,1)S(1)} %collective-permute-done.3.rest_2_), channel_id=1, source_target_pairs={{0,4},{4,0},{8,12},{12,8},{1,5},{5,1},{9,13},{13,9},{2,6},{6,2},{1... | collective-permute-start | bytes 688136 | tf_op jit(solution)/shard_map/ppermute | solution.py:215
  28.7 14.3 %collective-permute-start.7 = (bf16[128,768]{1,0:T(8,128)(2,1)S(1)}, bf16[128,768]{1,0:T(8,128)(2,1)S(1)}, u32[]{:S(2)}, u32[]{:S(2)}) collective-permute-start(bf16[128,768]{1,0:T(8,128)(2,1)S(1)} %collective-permute-done.6.rest_2_), channel_id=1, source_target_pairs={{0,0},{4,4},{8,12},{12,8},{1,1},{5,5},{9,13},{13,9},{2,2},{6,6},{1... | collective-permute-start | bytes 589832 | tf_op jit(solution)/shard_map/ppermute | solution.py:204
  33.9 11.6 %collective-permute-start.12 = (bf16[32,2688]{1,0:T(8,128)(2,1)S(1)}, bf16[32,2688]{1,0:T(8,128)(2,1)S(1)}, u32[]{:S(2)}, u32[]{:S(2)}) collective-permute-start(bf16[32,2688]{1,0:T(8,128)(2,1)S(1)} %collective-permute-done.10.rest_6_), channel_id=1, source_target_pairs={{0,4},{4,0},{8,12},{12,8},{1,5},{5,1},{9,13},{13,9},{2,6},{6,2},{1... | collective-permute-start | bytes 516104 | tf_op jit(solution)/shard_map/ppermute | solution.py:217

commit v9 on v8

--- a/solution.py
+++ b/solution.py
@@ -70,37 +70,51 @@
 ONE = [(i, i ^ 1) for i in range(4)]
 TWO = [(i, i ^ 2) for i in range(4)]
 LAST = [(0, 0), (1, 1), (2, 3), (3, 2)]
+INWARD = [(0, 1), (3, 2)]
+OUTWARD = [(1, 0), (2, 3)]
 
 
 def spread(shard):
     return lax.ppermute(shard, "ctx", ONE), lax.ppermute(shard, "ctx", TWO)
 
 
-def low_rank_kernel(ids, ranks, hidden, *rest):
-    pieces, out, accum = rest[:-2], rest[-2], rest[-1]
+def product_kernel(features, piece, out):
+    out[...] = jnp.dot(features[...], piece[...], preferred_element_type=jnp.float32)
+
+
+def product(features, piece):
+    return pl.pallas_call(
+        product_kernel,
+        out_shape=jax.ShapeDtypeStruct((features.shape[0], piece.shape[1]), jnp.float32),
+        in_specs=[spec(VMEM)] * 2,
+        out_specs=spec(VMEM),
+        compiler_params=PARAMS,
+        cost_estimate=pl.CostEstimate(flops=1 << 25, bytes_accessed=1 << 19, transcendentals=0),
+    )(features, piece)
+
+
+def low_rank_kernel(ids, ranks, hidden, partial, *rest):
+    pieces, out = rest[:-1], rest[-1]
     rows = pieces[0].shape[0]
     rank = ranks[ids[lax.axis_index("req")]]
-    accum[...] = jnp.zeros_like(accum)
+    total = partial[...]
     for flip, piece in enumerate(pieces):
         place = lax.axis_index("ctx") ^ flip
         columns = pl.ds(pl.multiple_of(place * rows, HD), rows)
-        accum[...] += jnp.dot(hidden[:, columns], piece[...], preferred_element_type=jnp.float32)
-
-    column = lax.broadcasted_iota(jnp.int32, accum.shape, 1)
-    out[...] = jnp.where(column < rank, accum[...], 0.0).astype(jnp.bfloat16)
-
-
-def low_rank(ids, ranks, hidden, pieces):
-    shape = (hidden.shape[0], pieces[0].shape[1])
+        total += jnp.dot(hidden[:, columns], piece[...], preferred_element_type=jnp.float32)
+    column = lax.broadcasted_iota(jnp.int32, total.shape, 1)
+    out[...] = jnp.where(column < rank, total, 0.0).astype(jnp.bfloat16)
+
+
+def low_rank(ids, ranks, hidden, partial, pieces):
     return pl.pallas_call(
         low_rank_kernel,
-        out_shape=jax.ShapeDtypeStruct(shape, jnp.bfloat16),
-        in_specs=[spec(SMEM)] * 2 + [spec(VMEM)] * (1 + len(pieces)),
+        out_shape=jax.ShapeDtypeStruct(partial.shape, jnp.bfloat16),
+        in_specs=[spec(SMEM)] * 2 + [spec(VMEM)] * (2 + len(pieces)),
         out_specs=spec(VMEM),
-        scratch_shapes=[VMEM(shape, jnp.float32)],
         compiler_params=PARAMS,
         cost_estimate=pl.CostEstimate(flops=1 << 27, bytes_accessed=1 << 22, transcendentals=0),
-    )(ids, ranks, hidden, *pieces)
+    )(ids, ranks, hidden, partial, *pieces)
 
 
 def attend_kernel(lengths, base, low, *rest):
@@ -202,23 +216,31 @@
     kv = kv_base[0]
     kv_one, kv_two = spread(kv)
     kv_three = lax.ppermute(kv_two, "ctx", LAST)
+    hidden = hidden_states[0]
+    rows = adapter_down.shape[1]
+    start = (lax.axis_index("ctx") ^ 1) * rows
     near_down = lax.ppermute(give_down, "req", SIBLING)
     near_up = lax.ppermute(give_up, "req", SIBLING)
     far_down = lax.ppermute(keep_down[1] + near_down[1], "req", ACROSS)
-    far_up = lax.ppermute(keep_up[1] + near_up[1], "req", ACROSS)
+    pass_up, early = lax.optimization_barrier((keep_up[1] + near_up[1], hidden))
+    far_up = lax.ppermute(pass_up, "req", ACROSS)
+    features = lax.ppermute(lax.dynamic_slice_in_dim(early, start, rows, 1), "ctx", INWARD)
     down = keep_down[0] + near_down[0] + far_down
     down, kv_one = lax.optimization_barrier((down, kv_one))
-    down_one, down_two = spread(down)
+    down_one = lax.ppermute(down, "ctx", INWARD)
+    down_two = lax.ppermute(down, "ctx", TWO)
     up = keep_up[0] + near_up[0] + far_up
+    up, features = lax.optimization_barrier((up, features))
     up_one, up_two = spread(up)
+    partial = lax.ppermute(product(features, down), "ctx", OUTWARD)
     down_two, down_one = lax.optimization_barrier((down_two, down_one))
     down_three = lax.ppermute(down_two, "ctx", ONE)
-    up_two, up_one = lax.optimization_barrier((up_two, up_one))
+    up_two, up_one, partial = lax.optimization_barrier((up_two, up_one, partial))
     up_three = lax.ppermute(up_two, "ctx", ONE)
     kvs = [kv, kv_one, kv_two, kv_three]
     downs = [down, down_one, down_two, down_three]
     ups = [up, up_one, up_two, up_three]
-    low = low_rank(adapter_ids, rank_buckets, hidden_states[0], downs)
+    low = low_rank(adapter_ids, rank_buckets, hidden, partial, downs)
     return attend(lengths, queries_base[0], low, kvs, ups)[None]
 
 

time: 49.1 us -> 53.9 us (1.098)
  the two profiles are of different devices: /device:TPU:24 before, /device:TPU:18 now
where the time goes in v9:
time: 53.9 us; the launch traced here: 53.1 us
  starting transfers between devices  21.9 us (41%)
  waiting for transfers between devices  20 us (37%)
  Pallas kernels  5.82 us (11%)
  other arithmetic  4.63 us (9%)
  between operations  0.8 us (1%)
    ppermute x1, waiting for transfers between devices, body(): down_two = lax.ppermute(down, 'ctx', TWO)  7.86 us
    ppermute x1, waiting for transfers between devices, body(): far_down = lax.ppermute(keep_down[1] + near_down[1], 'req', ACROSS)  4.11 us
    ppermute x4, starting transfers between devices, spread(): return (lax.ppermute(shard, 'ctx', ONE), lax.ppermute(shard, 'ctx', TWO))  3.88 us
    pallas_call x1, Pallas kernels, attend(): pl.pallas_call(attend_kernel, out_shape=jax.ShapeDtypeStruct(base.shape,...  3.85 us
    ppermute x1, starting transfers between devices, body(): down_two = lax.ppermute(down, 'ctx', TWO)  3.74 us
    ppermute x1, starting transfers between devices, body(): up_three = lax.ppermute(up_two, 'ctx', ONE)  2.48 us
    ppermute x1, waiting for transfers between devices, body(): down_one = lax.ppermute(down, 'ctx', INWARD)  2.45 us
    ppermute x1, starting transfers between devices, body(): partial = lax.ppermute(product(features, down), 'ctx', OUTWARD)  2.22 us
  transfers between devices with their start and end apart: 15, of which 6 were waited for; matrix products, arithmetic and copies ran while one was open for 7% of the time, Pallas kernels for 2%

profile of v9, /device:TPU:18, one launch (start us, length us, event | category | flops | bytes accessed | tf_op | source)
XLA Modules:
  0.0 53.1 jit_solution(14966501203544736614)
XLA Ops:
  0.0 0.0 copy-start.4
  0.0 0.8 %pad_add_fusion.table = s32[68]{0:T(128)S(1)} fusion(s32[64]{0:T(128)} %param.15, s32[4]{0:T(128)} %ids.1), kind=kLoop, calls=%fused_computation.10 | loop fusion | flops 68 | bytes 544 | tf_op jit(solution)/shard_map/concatenate | solution.py:65
  0.8 0.0 copy-start
  0.8 0.0 copy-start.1
  0.8 0.0 copy-start.2
  0.8 0.8 %shard_map.91 = (bf16[2,896,128]{2,1,0:T(8,128)(2,1)S(1)}, bf16[2,896,128]{2,1,0:T(8,128)(2,1)S(1)}, bf16[2,32,2688]{2,1,0:T(8,128)(2,1)S(1)}, bf16[2,32,2688]{2,1,0:T(8,128)(2,1)S(1)}) custom-call(s32[68]{0:T(128)S(1)} %pad_add_fusion.table, bf16[16,896,128]{2,1,0:T(8,128)(2,1)} %rest_0_.1, bf16[16,32,2688]{2,1,0:T(8,128)(2,1)} %rest_1_.1), custom_call_target="tpu_custom_call" | custom-call | tf_op jit(solution)/shard_map/pallas_call | solution.py:58
  1.6 0.0 copy-start.3
  1.6 1.1 %collective-permute-start.5 = (bf16[2,896,128]{2,1,0:T(8,128)(2,1)S(1)}, bf16[2,896,128]{2,1,0:T(8,128)(2,1)}, u32[]{:S(2)}, u32[]{:S(2)}) collective-permute-start(bf16[2,896,128]{2,1,0:T(8,128)(2,1)S(1)} %get-tuple-element.27), channel_id=1, source_target_pairs={{0,1},{1,0},{2,3},{3,2},{4,5},{5,4},{6,7},{7,6},{8,9},{9,8},{10,11... | collective-permute-start | bytes 1376264 | tf_op jit(solution)/shard_map/ppermute | solution.py:222
  2.7 0.1 collective-permute-start
  2.8 0.0 copy-done.4
  2.8 1.6 %collective-permute-start.7 = (bf16[128,768]{1,0:T(8,128)(2,1)S(1)}, bf16[128,768]{1,0:T(8,128)(2,1)}, u32[]{:S(2)}, u32[]{:S(2)}) collective-permute-start(bf16[128,768]{1,0:T(8,128)(2,1)S(1)} %bitcast.19), channel_id=1, source_target_pairs={{0,4},{4,0},{8,12},{12,8},{1,5},{5,1},{9,13},{13,9},{2,6},{6,2},{1... | collective-permute-start | bytes 589832 | tf_op jit(solution)/shard_map/ppermute | solution.py:78
  4.4 0.3 collective-permute-start.12
  4.7 0.0 collective-permute-done.5
  4.7 1.0 %fusion = bf16[896,128]{1,0:T(8,128)(2,1)S(1)} fusion(bf16[2,896,128]{2,1,0:T(8,128)(2,1)} %collective-permute-done.5, bf16[2,896,128]{2,1,0:T(8,128)(2,1)S(1)} %get-tuple-element.26), kind=kLoop, calls=%fused_computation.1 | loop fusion | flops 114688 | bytes 688128 | tf_op jit(solution)/shard_map/add | solution.py:224
  5.7 0.4 collective-permute-start.6
  6.1 0.0 collective-permute-done
  6.1 0.9 %fusion.3 = bf16[32,2688]{1,0:T(8,128)(2,1)S(1)} fusion(bf16[2,32,2688]{2,1,0:T(8,128)(2,1)} %collective-permute-done, bf16[2,32,2688]{2,1,0:T(8,128)(2,1)S(1)} %get-tuple-element.20), kind=kLoop, calls=%fused_computation.6 | loop fusion | flops 86016 | bytes 516096 | tf_op jit(solution)/shard_map/add | solution.py:225
  7.0 1.8 %collective-permute-start.1 = (bf16[32,2688]{1,0:T(8,128)(2,1)S(1)}, bf16[32,2688]{1,0:T(8,128)(2,1)S(1)}, u32[]{:S(2)}, u32[]{:S(2)}) collective-permute-start(bf16[32,2688]{1,0:T(8,128)(2,1)S(1)} %fusion.3), channel_id=1, source_target_pairs={{0,2},{1,3},{2,0},{3,1},{4,6},{5,7},{6,4},{7,5},{8,10},{9,11},{10,... | collective-permute-start | bytes 516104 | tf_op jit(solution)/shard_map/ppermute | solution.py:226
  8.8 0.0 copy-done
  8.8 1.3 %collective-permute-start.2 = (bf16[128,896]{1,0:T(8,128)(2,1)S(1)}, bf16[128,896]{1,0:T(8,128)(2,1)S(1)}, u32[]{:S(2)}, u32[]{:S(2)}) collective-permute-start(bf16[128,896]{1,0:T(8,128)(2,1)S(1)} %constant_dynamic-slice_fusion), channel_id=1, source_target_pairs={{0,4},{12,8},{1,5},{13,9},{2,6},{14,10},{3,7},{15,11},{16,20},{28,... | collective-permute-start | bytes 688136 | tf_op jit(solution)/shard_map/ppermute | solution.py:227
  10.1 4.1 %collective-permute-done.6 = bf16[896,128]{1,0:T(8,128)(2,1)S(1)} collective-permute-done((bf16[896,128]{1,0:T(8,128)(2,1)S(1)}, bf16[896,128]{1,0:T(8,128)(2,1)S(1)}, u32[]{:S(2)}, u32[]{:S(2)}) %collective-permute-start.6) | collective-permute-done | bytes 229408 | tf_op jit(solution)/shard_map/ppermute | solution.py:224
  14.2 1.0 %fusion.2.piece.rest_0_ = bf16[896,128]{1,0:T(8,128)(2,1)S(1)} fusion(bf16[896,128]{1,0:T(8,128)(2,1)S(1)} %collective-permute-done.6, bf16[2,896,128]{2,1,0:T(8,128)(2,1)} %collective-permute-done.5, bf16[2,896,128]{2,1,0:T(8,128)(2,1)S(1)} %get-tuple-element.26), kind=kLoop, calls=%fused_computation.4 | loop fusion | flops 229376 | bytes 917504 | tf_op jit(solution)/shard_map/add | solution.py:228
  15.2 0.0 collective-permute-done.7.rest_1_
  15.2 1.3 %collective-permute-start.10 = (bf16[896,128]{1,0:T(8,128)(2,1)S(1)}, bf16[896,128]{1,0:T(8,128)(2,1)S(1)}, u32[]{:S(2)}, u32[]{:S(2)}) collective-permute-start(bf16[896,128]{1,0:T(8,128)(2,1)S(1)} %fusion.2.piece.rest_0_), channel_id=1, source_target_pairs={{0,4},{12,8},{1,5},{13,9},{2,6},{14,10},{3,7},{15,11},{16,20},{28,... | collective-permute-start | bytes 688136 | tf_op jit(solution)/shard_map/ppermute | solution.py:230
  16.5 3.7 %collective-permute-start.9 = (bf16[896,128]{1,0:T(8,128)(2,1)S(1)}, bf16[896,128]{1,0:T(8,128)(2,1)S(1)}, u32[]{:S(2)}, u32[]{:S(2)}) collective-permute-start(bf16[896,128]{1,0:T(8,128)(2,1)S(1)} %fusion.2.piece.rest_0_), channel_id=1, source_target_pairs={{0,8},{4,12},{8,0},{12,4},{1,9},{5,13},{9,1},{13,5},{2,10},{6,14},... | collective-permute-start | bytes 688136 | tf_op jit(solution)/shard_map/ppermute | solution.py:231
  20.2 0.0 collective-permute-done.1
  20.3 1.0 %fusion.5.rest_4_ = bf16[32,2688]{1,0:T(8,128)(2,1)S(1)} fusion(bf16[32,2688]{1,0:T(8,128)(2,1)S(1)} %collective-permute-done.1, bf16[2,32,2688]{2,1,0:T(8,128)(2,1)} %collective-permute-done, bf16[2,32,2688]{2,1,0:T(8,128)(2,1)S(1)} %get-tuple-element.20), kind=kLoop, calls=%fused_computation.9 | loop fusion | flops 172032 | bytes 688128 | tf_op jit(solution)/shard_map/add | solution.py:232
  21.2 0.0 collective-permute-done.2.features
  21.2 0.1 collective-permute-start.3
  21.3 1.9 %collective-permute-start.4 = (bf16[32,2688]{1,0:T(8,128)(2,1)S(1)}, bf16[32,2688]{1,0:T(8,128)(2,1)S(1)}, u32[]{:S(2)}, u32[]{:S(2)}) collective-permute-start(bf16[32,2688]{1,0:T(8,128)(2,1)S(1)} %fusion.5.rest_4_), channel_id=1, source_target_pairs={{0,4},{4,0},{8,12},{12,8},{1,5},{5,1},{9,13},{13,9},{2,6},{6,2},{1... | collective-permute-start | bytes 516104 | tf_op jit(solution)/shard_map/ppermute | solution.py:78
  23.2 2.5 %collective-permute-done.10.rest_1_ = bf16[896,128]{1,0:T(8,128)(2,1)S(1)} collective-permute-done((bf16[896,128]{1,0:T(8,128)(2,1)S(1)}, bf16[896,128]{1,0:T(8,128)(2,1)S(1)}, u32[]{:S(2)}, u32[]{:S(2)}) %collective-permute-start.10) | collective-permute-done | bytes 229408 | tf_op jit(solution)/shard_map/ppermute | solution.py:230
  25.6 7.9 %collective-permute-done.9.rest_2_ = bf16[896,128]{1,0:T(8,128)(2,1)S(1)} collective-permute-done((bf16[896,128]{1,0:T(8,128)(2,1)S(1)}, bf16[896,128]{1,0:T(8,128)(2,1)S(1)}, u32[]{:S(2)}, u32[]{:S(2)}) %collective-permute-start.9) | collective-permute-done | bytes 229408 | tf_op jit(solution)/shard_map/ppermute | solution.py:231
  33.5 1.7 %collective-permute-start.11 = (bf16[896,128]{1,0:T(8,128)(2,1)S(1)}, bf16[896,128]{1,0:T(8,128)(2,1)S(1)}, u32[]{:S(2)}, u32[]{:S(2)}) collective-permute-start(bf16[896,128]{1,0:T(8,128)(2,1)S(1)} %collective-permute-done.9.rest_2_), channel_id=1, source_target_pairs={{0,4},{4,0},{8,12},{12,8},{1,5},{5,1},{9,13},{13,9},{2,6},{6,2},{1... | collective-permute-start | bytes 688136 | tf_op jit(solution)/shard_map/ppermute | solution.py:237
  35.2 0.2 shard_map.92
  35.4 2.2 %collective-permute-start.8 = (f32[128,128]{1,0:T(8,128)S(1)}, f32[128,128]{1,0:T(8,128)S(1)}, u32[]{:S(2)}, u32[]{:S(2)}) collective-permute-start(f32[128,128]{1,0:T(8,128)S(1)} %shard_map.92), channel_id=1, source_target_pairs={{4,0},{8,12},{5,1},{9,13},{6,2},{10,14},{7,3},{11,15},{20,16},{24,... | collective-permute-start | bytes 196616 | tf_op jit(solution)/shard_map/ppermute | solution.py:235
  37.7 0.0 collective-permute-done.12.rest_2_
  37.7 1.9 %collective-permute-start.13 = (bf16[128,768]{1,0:T(8,128)(2,1)}, bf16[128,768]{1,0:T(8,128)(2,1)S(1)}, u32[]{:S(2)}, u32[]{:S(2)}) collective-permute-start(bf16[128,768]{1,0:T(8,128)(2,1)} %collective-permute-done.12.rest_2_), channel_id=1, source_target_pairs={{0,0},{4,4},{8,12},{12,8},{1,1},{5,5},{9,13},{13,9},{2,2},{6,6},{1... | collective-permute-start | bytes 589832 | tf_op jit(solution)/shard_map/ppermute | solution.py:218
  39.6 0.0 collective-permute-done.3.rest_6_
  39.6 0.0 collective-permute-done.4.rest_5_
  39.6 1.8 %collective-permute-done.8.partial = f32[128,128]{1,0:T(8,128)S(1)} collective-permute-done((f32[128,128]{1,0:T(8,128)S(1)}, f32[128,128]{1,0:T(8,128)S(1)}, u32[]{:S(2)}, u32[]{:S(2)}) %collective-permute-start.8) | collective-permute-done | bytes 65568 | tf_op jit(solution)/shard_map/ppermute | solution.py:235
  41.4 2.5 %collective-permute-start.14 = (bf16[32,2688]{1,0:T(8,128)(2,1)S(1)}, bf16[32,2688]{1,0:T(8,128)(2,1)S(1)}, u32[]{:S(2)}, u32[]{:S(2)}) collective-permute-start(bf16[32,2688]{1,0:T(8,128)(2,1)S(1)} %collective-permute-done.3.rest_6_), channel_id=1, source_target_pairs={{0,4},{4,0},{8,12},{12,8},{1,5},{5,1},{9,13},{13,9},{2,6},{6,2},{1... | collective-permute-start | bytes 516104 | tf_op jit(solution)/shard_map/ppermute | solution.py:239
  44.6 0.0 collective-permute-done.11.rest_3_
  44.6 0.0 copy-done.1
  44.6 0.0 copy-done.2
  44.6 0.9 %shard_map.93.low = bf16[128,128]{1,0:T(8,128)(2,1)S(1)} custom-call(s32[4]{0:T(128)S(1)} %copy-done.1, s32[64]{0:T(128)S(1)} %copy-done.2, bf16[128,3584]{1,0:T(8,128)(2,1)S(1)} %bitcast.17, f32[128,128]{1,0:T(8,128)S(1)} %collective-permute-done.8.partial, bf16[896,128]{1,0:T(8,128)(2,1)S(1)} %fusion.2.piece.rest_0_, ...), custom_call_target="tpu_custom_call" | custom-call | flops 134217728 | bytes 4194304 | tf_op jit(solution)/shard_map/pallas_call | solution.py:110
  45.5 1.9 %collective-permute-done.13.rest_3_ = bf16[128,768]{1,0:T(8,128)(2,1)S(1)} collective-permute-done((bf16[128,768]{1,0:T(8,128)(2,1)}, bf16[128,768]{1,0:T(8,128)(2,1)S(1)}, u32[]{:S(2)}, u32[]{:S(2)}) %collective-permute-start.13) | collective-permute-done | bytes 196640 | tf_op jit(solution)/shard_map/ppermute | solution.py:218
  47.4 1.8 %collective-permute-done.14.rest_7_ = bf16[32,2688]{1,0:T(8,128)(2,1)S(1)} collective-permute-done((bf16[32,2688]{1,0:T(8,128)(2,1)S(1)}, bf16[32,2688]{1,0:T(8,128)(2,1)S(1)}, u32[]{:S(2)}, u32[]{:S(2)}) %collective-permute-start.14) | collective-permute-done | bytes 172064 | tf_op jit(solution)/shard_map/ppermute | solution.py:239
  49.3 0.0 copy-done.3
  49.3 3.9 %shard_map.94 = bf16[128,2688]{1,0:T(8,128)(2,1)} custom-call(s32[1]{0:T(128)S(6)} %copy.10.lengths, bf16[128,2688]{1,0:T(8,128)(2,1)S(1)} %bitcast.18, bf16[128,128]{1,0:T(8,128)(2,1)S(1)} %shard_map.93.low, bf16[128,768]{1,0:T(8,128)(2,1)S(1)} %bitcast.21, bf16[128,768]{1,0:T(8,128)(2,1)} %collective-permute-done.7.rest_1_, ...), custom_call_target="tpu_custom_call" | custom-call | flops 1073741824 | bytes 4194304 | tf_op jit(solution)/shard_map/pallas_call | solution.py:186
  (1 shorter events, 0.0 us)
Async XLA Ops:
  0.0 2.8 %copy-start.4 = (bf16[1,128,768]{2,1,0:T(8,128)(2,1)S(1)}, bf16[1,128,768]{2,1,0:T(8,128)(2,1)}, u32[]{:S(2)}) copy-start(bf16[1,128,768]{2,1,0:T(8,128)(2,1)} %param.11) | copy-start | bytes 589828
  0.8 8.0 %copy-start = (bf16[1,128,3584]{2,1,0:T(8,128)(2,1)S(1)}, bf16[1,128,3584]{2,1,0:T(8,128)(2,1)}, u32[]{:S(2)}) copy-start(bf16[1,128,3584]{2,1,0:T(8,128)(2,1)} %param.9) | copy-start | bytes 2752516
  0.8 43.8 %copy-start.1 = (s32[4]{0:T(128)S(1)}, s32[4]{0:T(128)}, u32[]{:S(2)}) copy-start(s32[4]{0:T(128)} %ids.1) | copy-start | bytes 52
  0.8 43.8 %copy-start.2 = (s32[64]{0:T(128)S(1)}, s32[64]{0:T(128)}, u32[]{:S(2)}) copy-start(s32[64]{0:T(128)} %ranks.1) | copy-start | bytes 772
  1.6 47.7 %copy-start.3 = (bf16[1,128,2688]{2,1,0:T(8,128)(2,1)S(1)}, bf16[1,128,2688]{2,1,0:T(8,128)(2,1)}, u32[]{:S(2)}) copy-start(bf16[1,128,2688]{2,1,0:T(8,128)(2,1)} %param.10) | copy-start | bytes 2064388
  1.6 3.1 %collective-permute-start.5 = (bf16[2,896,128]{2,1,0:T(8,128)(2,1)S(1)}, bf16[2,896,128]{2,1,0:T(8,128)(2,1)}, u32[]{:S(2)}, u32[]{:S(2)}) collective-permute-start(bf16[2,896,128]{2,1,0:T(8,128)(2,1)S(1)} %get-tuple-element.27), channel_id=1, source_target_pairs={{0,1},{1,0},{2,3},{3,2},{4,5},{5,4},{6,7},{7,6},{8,9},{9,8},{10,11... | collective-permute-start | bytes 1376264 | tf_op jit(solution)/shard_map/ppermute | solution.py:222
  2.7 3.4 %collective-permute-start = (bf16[2,32,2688]{2,1,0:T(8,128)(2,1)S(1)}, bf16[2,32,2688]{2,1,0:T(8,128)(2,1)}, u32[]{:S(2)}, u32[]{:S(2)}) collective-permute-start(bf16[2,32,2688]{2,1,0:T(8,128)(2,1)S(1)} %get-tuple-element.21), channel_id=1, source_target_pairs={{0,1},{1,0},{2,3},{3,2},{4,5},{5,4},{6,7},{7,6},{8,9},{9,8},{10,11... | collective-permute-start | bytes 1032200 | tf_op jit(solution)/shard_map/ppermute | solution.py:223
  2.8 12.4 %collective-permute-start.7 = (bf16[128,768]{1,0:T(8,128)(2,1)S(1)}, bf16[128,768]{1,0:T(8,128)(2,1)}, u32[]{:S(2)}, u32[]{:S(2)}) collective-permute-start(bf16[128,768]{1,0:T(8,128)(2,1)S(1)} %bitcast.19), channel_id=1, source_target_pairs={{0,4},{4,0},{8,12},{12,8},{1,5},{5,1},{9,13},{13,9},{2,6},{6,2},{1... | collective-permute-start | bytes 589832 | tf_op jit(solution)/shard_map/ppermute | solution.py:78
  4.4 33.3 %collective-permute-start.12 = (bf16[128,768]{1,0:T(8,128)(2,1)S(1)}, bf16[128,768]{1,0:T(8,128)(2,1)}, u32[]{:S(2)}, u32[]{:S(2)}) collective-permute-start(bf16[128,768]{1,0:T(8,128)(2,1)S(1)} %bitcast.20), channel_id=1, source_target_pairs={{0,8},{4,12},{8,0},{12,4},{1,9},{5,13},{9,1},{13,5},{2,10},{6,14},... | collective-permute-start | bytes 589832 | tf_op jit(solution)/shard_map/ppermute | solution.py:78
  5.7 8.5 %collective-permute-start.6 = (bf16[896,128]{1,0:T(8,128)(2,1)S(1)}, bf16[896,128]{1,0:T(8,128)(2,1)S(1)}, u32[]{:S(2)}, u32[]{:S(2)}) collective-permute-start(bf16[896,128]{1,0:T(8,128)(2,1)S(1)} %fusion), channel_id=1, source_target_pairs={{0,2},{1,3},{2,0},{3,1},{4,6},{5,7},{6,4},{7,5},{8,10},{9,11},{10,... | collective-permute-start | bytes 688136 | tf_op jit(solution)/shard_map/ppermute | solution.py:224
  7.0 13.2 %collective-permute-start.1 = (bf16[32,2688]{1,0:T(8,128)(2,1)S(1)}, bf16[32,2688]{1,0:T(8,128)(2,1)S(1)}, u32[]{:S(2)}, u32[]{:S(2)}) collective-permute-start(bf16[32,2688]{1,0:T(8,128)(2,1)S(1)} %fusion.3), channel_id=1, source_target_pairs={{0,2},{1,3},{2,0},{3,1},{4,6},{5,7},{6,4},{7,5},{8,10},{9,11},{10,... | collective-permute-start | bytes 516104 | tf_op jit(solution)/shard_map/ppermute | solution.py:226
  8.8 12.4 %collective-permute-start.2 = (bf16[128,896]{1,0:T(8,128)(2,1)S(1)}, bf16[128,896]{1,0:T(8,128)(2,1)S(1)}, u32[]{:S(2)}, u32[]{:S(2)}) collective-permute-start(bf16[128,896]{1,0:T(8,128)(2,1)S(1)} %constant_dynamic-slice_fusion), channel_id=1, source_target_pairs={{0,4},{12,8},{1,5},{13,9},{2,6},{14,10},{3,7},{15,11},{16,20},{28,... | collective-permute-start | bytes 688136 | tf_op jit(solution)/shard_map/ppermute | solution.py:227
  15.2 10.4 %collective-permute-start.10 = (bf16[896,128]{1,0:T(8,128)(2,1)S(1)}, bf16[896,128]{1,0:T(8,128)(2,1)S(1)}, u32[]{:S(2)}, u32[]{:S(2)}) collective-permute-start(bf16[896,128]{1,0:T(8,128)(2,1)S(1)} %fusion.2.piece.rest_0_), channel_id=1, source_target_pairs={{0,4},{12,8},{1,5},{13,9},{2,6},{14,10},{3,7},{15,11},{16,20},{28,... | collective-permute-start | bytes 688136 | tf_op jit(solution)/shard_map/ppermute | solution.py:230
  16.5 17.0 %collective-permute-start.9 = (bf16[896,128]{1,0:T(8,128)(2,1)S(1)}, bf16[896,128]{1,0:T(8,128)(2,1)S(1)}, u32[]{:S(2)}, u32[]{:S(2)}) collective-permute-start(bf16[896,128]{1,0:T(8,128)(2,1)S(1)} %fusion.2.piece.rest_0_), channel_id=1, source_target_pairs={{0,8},{4,12},{8,0},{12,4},{1,9},{5,13},{9,1},{13,5},{2,10},{6,14},... | collective-permute-start | bytes 688136 | tf_op jit(solution)/shard_map/ppermute | solution.py:231
  21.2 18.4 %collective-permute-start.3 = (bf16[32,2688]{1,0:T(8,128)(2,1)S(1)}, bf16[32,2688]{1,0:T(8,128)(2,1)S(1)}, u32[]{:S(2)}, u32[]{:S(2)}) collective-permute-start(bf16[32,2688]{1,0:T(8,128)(2,1)S(1)} %fusion.5.rest_4_), channel_id=1, source_target_pairs={{0,8},{4,12},{8,0},{12,4},{1,9},{5,13},{9,1},{13,5},{2,10},{6,14},... | collective-permute-start | bytes 516104 | tf_op jit(solution)/shard_map/ppermute | solution.py:78
  21.3 18.3 %collective-permute-start.4 = (bf16[32,2688]{1,0:T(8,128)(2,1)S(1)}, bf16[32,2688]{1,0:T(8,128)(2,1)S(1)}, u32[]{:S(2)}, u32[]{:S(2)}) collective-permute-start(bf16[32,2688]{1,0:T(8,128)(2,1)S(1)} %fusion.5.rest_4_), channel_id=1, source_target_pairs={{0,4},{4,0},{8,12},{12,8},{1,5},{5,1},{9,13},{13,9},{2,6},{6,2},{1... | collective-permute-start | bytes 516104 | tf_op jit(solution)/shard_map/ppermute | solution.py:78
  33.5 11.1 %collective-permute-start.11 = (bf16[896,128]{1,0:T(8,128)(2,1)S(1)}, bf16[896,128]{1,0:T(8,128)(2,1)S(1)}, u32[]{:S(2)}, u32[]{:S(2)}) collective-permute-start(bf16[896,128]{1,0:T(8,128)(2,1)S(1)} %collective-permute-done.9.rest_2_), channel_id=1, source_target_pairs={{0,4},{4,0},{8,12},{12,8},{1,5},{5,1},{9,13},{13,9},{2,6},{6,2},{1... | collective-permute-start | bytes 688136 | tf_op jit(solution)/shard_map/ppermute | solution.py:237
  35.4 6.0 %collective-permute-start.8 = (f32[128,128]{1,0:T(8,128)S(1)}, f32[128,128]{1,0:T(8,128)S(1)}, u32[]{:S(2)}, u32[]{:S(2)}) collective-permute-start(f32[128,128]{1,0:T(8,128)S(1)} %shard_map.92), channel_id=1, source_target_pairs={{4,0},{8,12},{5,1},{9,13},{6,2},{10,14},{7,3},{11,15},{20,16},{24,... | collective-permute-start | bytes 196616 | tf_op jit(solution)/shard_map/ppermute | solution.py:235
  37.7 9.8 %collective-permute-start.13 = (bf16[128,768]{1,0:T(8,128)(2,1)}, bf16[128,768]{1,0:T(8,128)(2,1)S(1)}, u32[]{:S(2)}, u32[]{:S(2)}) collective-permute-start(bf16[128,768]{1,0:T(8,128)(2,1)} %collective-permute-done.12.rest_2_), channel_id=1, source_target_pairs={{0,0},{4,4},{8,12},{12,8},{1,1},{5,5},{9,13},{13,9},{2,2},{6,6},{1... | collective-permute-start | bytes 589832 | tf_op jit(solution)/shard_map/ppermute | solution.py:218
  41.4 7.9 %collective-permute-start.14 = (bf16[32,2688]{1,0:T(8,128)(2,1)S(1)}, bf16[32,2688]{1,0:T(8,128)(2,1)S(1)}, u32[]{:S(2)}, u32[]{:S(2)}) collective-permute-start(bf16[32,2688]{1,0:T(8,128)(2,1)S(1)} %collective-permute-done.3.rest_6_), channel_id=1, source_target_pairs={{0,4},{4,0},{8,12},{12,8},{1,5},{5,1},{9,13},{13,9},{2,6},{6,2},{1... | collective-permute-start | bytes 516104 | tf_op jit(solution)/shard_map/ppermute | solution.py:239
